TPU v7x, 32 devices: a whole 2x2x4 slice. The times are simulated.
32 devices in a mesh: dp: 8 (over z, y), sp: 4 (over x, core).
Axes of the slice: x: 2, y: 2, z: 4, core: 2. Of those that a mesh axis runs over, the one named last changes fastest.
Arguments:
- tokens: bfloat16 [16, 1536, 2048], P('dp', 'sp'), may hold values from -6 to 6
- cotangent: bfloat16 [16, 1536, 2048], P('dp', 'sp'), may hold values from -6 to 6
- lengths: int32 [16], P('dp'), may hold values from 256 to 1536, as said below
- query_weight: bfloat16 [2048, 2048], P(('dp', 'sp')), may hold values from -0.125 to 0.125
- key_weight: bfloat16 [2048, 256], P(('dp', 'sp')), may hold values from -0.125 to 0.125
- value_weight: bfloat16 [2048, 256], P(('dp', 'sp')), may hold values from -0.125 to 0.125
- output_weight: bfloat16 [2048, 2048], P(('dp', 'sp')), may hold values from -1 to 1
- gate_weight: bfloat16 [2048, 5632], P('dp', 'sp'), may hold values from -0.125 to 0.125
- up_weight: bfloat16 [2048, 5632], P('dp', 'sp'), may hold values from -0.125 to 0.125
- down_weight: bfloat16 [5632, 2048], P('sp', 'dp'), may hold values from -0.078125 to 0.078125
- attention_gain: bfloat16 [2048], P(('dp', 'sp')), may hold values from 0.5 to 1.5
- feed_gain: bfloat16 [2048], P(('dp', 'sp')), may hold values from 0.5 to 1.5
Outputs:
- block_out: bfloat16 [16, 1536, 2048], P('dp', 'sp')
- input_grad: bfloat16 [16, 1536, 2048], P('dp', 'sp')
- query_grad: float32 [2048, 2048], P(('dp', 'sp'))
- key_grad: float32 [2048, 256], P(('dp', 'sp'))
- value_grad: float32 [2048, 256], P(('dp', 'sp'))
- output_grad: float32 [2048, 2048], P(('dp', 'sp'))
- gate_grad: float32 [2048, 5632], P('dp', 'sp')
- up_grad: float32 [2048, 5632], P('dp', 'sp')
- down_grad: float32 [5632, 2048], P('sp', 'dp')
- attention_gain_grad: float32 [2048], P(('dp', 'sp'))
- feed_gain_grad: float32 [2048], P(('dp', 'sp'))
- branch_norms: float32 [3, 16], P(None, 'dp')
Inputs may be any that keep to these rules, and one draw needn't show every extreme that they name: `lengths`: among the 2 sequences of each index of dp, one drawn at random is exactly 1536 long.
All inputs are finite; a program needn't handle non-finite values.
Results may differ from a plain program's by a relative error of at most 0.017.
Values may be sent and summed in bfloat16 or wider, within the bound.
No kernel may reach another device: no remote copies, remote signals or barrier semaphores. Data moves between devices by JAX's collectives and lax.ppermute only.
A program may use at most 320 MiB of HBM per device.

v0:
```python
import jax
import jax.numpy as jnp
from jax import lax
from jax.sharding import PartitionSpec as P

HEADS = 32
KV = 4
HD = 64


epsilon = 1e-05


def rms_norm(values, gain):
    return values * lax.rsqrt(jnp.mean(values * values, axis=-1, keepdims=True) + epsilon) * gain


def rope_tables(positions, width):
    half_width = width // 2
    frequency = jnp.power(10000.0, -2.0 * jnp.arange(half_width).astype(jnp.float32) / width)
    angles = positions.astype(jnp.float32)[:, None] * frequency[None, :]
    return (
        jnp.concatenate([jnp.cos(angles), jnp.cos(angles)], -1),
        jnp.concatenate([jnp.sin(angles), jnp.sin(angles)], -1),
    )


def rotate(values, cos_table, sin_table):
    half_width = values.shape[-1] // 2
    turned = jnp.concatenate([-values[..., half_width:], values[..., :half_width]], -1)
    return values * cos_table[:, None, :] + turned * sin_table[:, None, :]


def rope_back(grad, cos_table, sin_table):
    unused, pull = jax.vjp(
        lambda values: rotate(values, cos_table, sin_table), jnp.zeros_like(grad)
    )
    return pull(grad)[0]


def to_low(values):
    return values.astype(jnp.bfloat16)


def project(left, right):
    return jnp.einsum("...d,df->...f", left, right, preferred_element_type=jnp.float32)


def score_block(query_block, start, keys, length):
    row_pos = start + jnp.arange(query_block.shape[0])
    col_pos = jnp.arange(keys.shape[0])
    allowed = (col_pos[None, :] <= row_pos[:, None]) & (col_pos[None, :] < length)
    raw = jnp.einsum(
        "qhd,khd->hqk", query_block, keys, preferred_element_type=jnp.float32
    ) * HD ** (-0.5)
    return jnp.where(allowed[None], raw, -1e30)


def attend_forward(queries, keys, values, length, block):
    block_count = queries.shape[0] // block
    starts = jnp.arange(block_count) * block

    def one_block(packed):
        query_block, start = packed
        scores = score_block(query_block, start, keys, length)
        row_max = jnp.max(scores, axis=-1, keepdims=True)
        exp_scores = jnp.exp(scores - row_max)
        row_total = jnp.sum(exp_scores, axis=-1, keepdims=True)
        soft_probs = to_low(exp_scores / row_total)
        result = jnp.einsum("hqk,khd->qhd", soft_probs, values, preferred_element_type=jnp.float32)
        return (to_low(result), row_max + jnp.log(row_total))

    shaped = queries.reshape((block_count, block) + queries.shape[1:])
    results, log_sums = lax.map(one_block, (shaped, starts))
    return (results.reshape(queries.shape), log_sums)


def attend_backward(queries, keys, values, out_grad, log_sums, length, block):
    block_count = queries.shape[0] // block
    starts = jnp.arange(block_count) * block
    score_scale = HD ** (-0.5)

    def one_block(carry, packed):
        query_block, grad_block, lse_block, start = packed
        scores = score_block(query_block, start, keys, length)
        soft_probs = jnp.exp(scores - lse_block)
        prob_grad = jnp.einsum(
            "qhd,khd->hqk", grad_block, values, preferred_element_type=jnp.float32
        )
        row_delta = jnp.sum(soft_probs * prob_grad, axis=-1, keepdims=True)
        score_grad = to_low(soft_probs * (prob_grad - row_delta))
        query_grad = (
            jnp.einsum("hqk,khd->qhd", score_grad, keys, preferred_element_type=jnp.float32)
            * score_scale
        )
        key_grad = (
            carry[0]
            + jnp.einsum(
                "hqk,qhd->khd", score_grad, query_block, preferred_element_type=jnp.float32
            )
            * score_scale
        )
        value_grad = carry[1] + jnp.einsum(
            "hqk,qhd->khd", to_low(soft_probs), grad_block, preferred_element_type=jnp.float32
        )
        return ((key_grad, value_grad), query_grad)

    def shape_blocks(array):
        return array.reshape((block_count, block) + array.shape[1:])

    zeros = jnp.zeros(keys.shape, jnp.float32)
    (key_grad, value_grad), query_grad = lax.scan(
        one_block, (zeros, zeros), (shape_blocks(queries), shape_blocks(out_grad), log_sums, starts)
    )
    return (query_grad.reshape(queries.shape), key_grad, value_grad)


def body(
    tokens,
    cotangent,
    lengths,
    query_weight,
    key_weight,
    value_weight,
    output_weight,
    gate_weight,
    up_weight,
    down_weight,
    attention_gain,
    feed_gain,
):
    seq_dev, local_len, width = tokens.shape
    sp_count = lax.axis_size("sp")
    full_len = local_len * sp_count
    group = HEADS // KV
    attn_block = min(512, full_len)
    positions = lax.axis_index("sp") * local_len + jnp.arange(local_len)
    cos_table, sin_table = rope_tables(positions, HD)
    valid_rows = positions[None, :] < lengths[:, None]
    gathered = (
        lax.all_gather(query_weight, ("dp", "sp"), axis=0, tiled=True),
        lax.all_gather(key_weight, ("dp", "sp"), axis=0, tiled=True),
        lax.all_gather(value_weight, ("dp", "sp"), axis=0, tiled=True),
        lax.all_gather(output_weight, ("dp", "sp"), axis=0, tiled=True),
        lax.all_gather(attention_gain, ("dp", "sp"), axis=0, tiled=True),
        lax.all_gather(feed_gain, ("dp", "sp"), axis=0, tiled=True),
    )
    query_full, key_full, value_full, output_full = (
        gathered[0],
        gathered[1],
        gathered[2],
        gathered[3],
    )
    gain_one = gathered[4].astype(jnp.float32)
    gain_two = gathered[5].astype(jnp.float32)
    gate_part, up_part, down_part = (
        lax.all_gather(gate_weight, "dp", axis=0, tiled=True),
        lax.all_gather(up_weight, "dp", axis=0, tiled=True),
        lax.all_gather(down_weight, "dp", axis=1, tiled=True),
    )
    resid = tokens.astype(jnp.float32)
    normed_one = to_low(rms_norm(resid, gain_one))
    query_rot = to_low(
        rotate(
            project(normed_one, query_full).reshape(seq_dev, local_len, HEADS, HD),
            cos_table,
            sin_table,
        )
    )
    key_rot = rotate(
        project(normed_one, key_full).reshape(seq_dev, local_len, KV, HD), cos_table, sin_table
    )
    value_raw = project(normed_one, value_full).reshape(seq_dev, local_len, KV, HD)
    key_rep = to_low(jnp.repeat(key_rot, group, axis=2))
    value_rep = to_low(jnp.repeat(value_raw, group, axis=2))
    head_query, head_key, head_value = (
        lax.all_to_all(query_rot, "sp", split_axis=2, concat_axis=1, tiled=True),
        lax.all_to_all(key_rep, "sp", split_axis=2, concat_axis=1, tiled=True),
        lax.all_to_all(value_rep, "sp", split_axis=2, concat_axis=1, tiled=True),
    )
    head_outs = []
    log_sums = []
    for sequence in range(seq_dev):
        result, row_lse = attend_forward(
            head_query[sequence],
            head_key[sequence],
            head_value[sequence],
            lengths[sequence],
            attn_block,
        )
        head_outs.append(result)
        log_sums.append(row_lse)
    attended = lax.all_to_all(
        jnp.stack(head_outs), "sp", split_axis=1, concat_axis=2, tiled=True
    ).reshape(seq_dev, local_len, HEADS * HD)
    branch = project(attended, output_full)
    middle = resid + branch
    normed_two = to_low(rms_norm(middle, gain_two))
    all_rows = lax.all_gather(
        normed_two.reshape(seq_dev * local_len, width), "sp", axis=0, tiled=True
    )
    gate_out = project(all_rows, gate_part)
    up_out = project(all_rows, up_part)
    hidden = to_low(jax.nn.silu(gate_out) * up_out)
    mixed = (
        lax.psum_scatter(
            project(hidden, down_part).astype(jnp.bfloat16), "sp", scatter_dimension=0, tiled=True
        )
        .astype(jnp.float32)
        .reshape(seq_dev, local_len, width)
    )
    block_out = ((middle + mixed) * valid_rows[..., None]).astype(jnp.bfloat16)
    res_grad = cotangent.astype(jnp.float32) * valid_rows[..., None]
    grad_rows = lax.all_gather(
        to_low(res_grad).reshape(seq_dev * local_len, width), "sp", axis=0, tiled=True
    )
    down_wgrad = jnp.einsum("rf,rd->fd", hidden, grad_rows, preferred_element_type=jnp.float32)
    hidden_grad = jnp.einsum("rd,fd->rf", grad_rows, down_part, preferred_element_type=jnp.float32)
    unused, pull = jax.vjp(lambda gate_in, up_in: jax.nn.silu(gate_in) * up_in, gate_out, up_out)
    gate_grad, up_grad = pull(hidden_grad)
    gate_grad = to_low(gate_grad)
    up_grad = to_low(up_grad)
    gate_wgrad = jnp.einsum("rd,rf->df", all_rows, gate_grad, preferred_element_type=jnp.float32)
    up_wgrad = jnp.einsum("rd,rf->df", all_rows, up_grad, preferred_element_type=jnp.float32)
    normed_terms = jnp.einsum(
        "rf,df->rd", gate_grad, gate_part, preferred_element_type=jnp.float32
    ) + jnp.einsum("rf,df->rd", up_grad, up_part, preferred_element_type=jnp.float32)
    normed_two_grad = (
        lax.psum_scatter(normed_terms.astype(jnp.bfloat16), "sp", scatter_dimension=0, tiled=True)
        .astype(jnp.float32)
        .reshape(seq_dev, local_len, width)
    )
    unused, pull = jax.vjp(rms_norm, middle, gain_two)
    middle_norm_grad, gain_two_grad = pull(normed_two_grad)
    middle_grad = res_grad + middle_norm_grad
    branch_grad = to_low(middle_grad)
    output_wgrad = jnp.einsum(
        "scf,scd->fd", attended, branch_grad, preferred_element_type=jnp.float32
    )
    attended_grad = to_low(
        jnp.einsum("scd,fd->scf", branch_grad, output_full, preferred_element_type=jnp.float32)
    ).reshape(seq_dev, local_len, HEADS, HD)
    head_grad = lax.all_to_all(attended_grad, "sp", split_axis=2, concat_axis=1, tiled=True)
    query_grads = []
    key_grads = []
    value_grads = []
    for sequence in range(seq_dev):
        one_query, one_key, one_value = attend_backward(
            head_query[sequence],
            head_key[sequence],
            head_value[sequence],
            head_grad[sequence],
            log_sums[sequence],
            lengths[sequence],
            attn_block,
        )
        query_grads.append(to_low(one_query))
        key_grads.append(to_low(one_key))
        value_grads.append(to_low(one_value))
    back_query, back_key, back_value = (
        lax.all_to_all(jnp.stack(query_grads), "sp", split_axis=1, concat_axis=2, tiled=True),
        lax.all_to_all(jnp.stack(key_grads), "sp", split_axis=1, concat_axis=2, tiled=True),
        lax.all_to_all(jnp.stack(value_grads), "sp", split_axis=1, concat_axis=2, tiled=True),
    )
    key_sum = back_key.astype(jnp.float32).reshape(seq_dev, local_len, KV, group, HD).sum(axis=3)
    value_sum = (
        back_value.astype(jnp.float32).reshape(seq_dev, local_len, KV, group, HD).sum(axis=3)
    )
    query_proj_grad = to_low(
        rope_back(back_query.astype(jnp.float32), cos_table, sin_table)
    ).reshape(seq_dev, local_len, HEADS * HD)
    key_proj_grad = to_low(rope_back(key_sum, cos_table, sin_table)).reshape(
        seq_dev, local_len, KV * HD
    )
    value_proj_grad = to_low(value_sum).reshape(seq_dev, local_len, KV * HD)
    query_wgrad = jnp.einsum(
        "scd,scf->df", normed_one, query_proj_grad, preferred_element_type=jnp.float32
    )
    key_wgrad = jnp.einsum(
        "scd,scf->df", normed_one, key_proj_grad, preferred_element_type=jnp.float32
    )
    value_wgrad = jnp.einsum(
        "scd,scf->df", normed_one, value_proj_grad, preferred_element_type=jnp.float32
    )
    normed_one_grad = jnp.einsum(
        "scf,df->scd", query_proj_grad, query_full, preferred_element_type=jnp.float32
    )
    normed_one_grad = normed_one_grad + jnp.einsum(
        "scf,df->scd", key_proj_grad, key_full, preferred_element_type=jnp.float32
    )
    normed_one_grad = normed_one_grad + jnp.einsum(
        "scf,df->scd", value_proj_grad, value_full, preferred_element_type=jnp.float32
    )
    unused, pull = jax.vjp(rms_norm, resid, gain_one)
    resid_norm_grad, gain_one_grad = pull(normed_one_grad)
    input_grad = (middle_grad + resid_norm_grad).astype(jnp.bfloat16)
    shards = (
        lax.psum_scatter(query_wgrad, ("dp", "sp"), scatter_dimension=0, tiled=True),
        lax.psum_scatter(key_wgrad, ("dp", "sp"), scatter_dimension=0, tiled=True),
        lax.psum_scatter(value_wgrad, ("dp", "sp"), scatter_dimension=0, tiled=True),
        lax.psum_scatter(output_wgrad, ("dp", "sp"), scatter_dimension=0, tiled=True),
        lax.psum_scatter(gain_one_grad, ("dp", "sp"), scatter_dimension=0, tiled=True),
        lax.psum_scatter(gain_two_grad, ("dp", "sp"), scatter_dimension=0, tiled=True),
    )
    feed_shards = (
        lax.psum_scatter(
            gate_wgrad.astype(jnp.bfloat16), "dp", scatter_dimension=0, tiled=True
        ).astype(jnp.float32),
        lax.psum_scatter(
            up_wgrad.astype(jnp.bfloat16), "dp", scatter_dimension=0, tiled=True
        ).astype(jnp.float32),
        lax.psum_scatter(
            down_wgrad.astype(jnp.bfloat16), "dp", scatter_dimension=1, tiled=True
        ).astype(jnp.float32),
    )
    local_sums = jnp.stack(
        [
            jnp.sum(jnp.where(valid_rows[..., None], member * member, 0.0), axis=(1, 2))
            for member in (resid, branch, mixed)
        ]
    )
    summed = lax.psum(local_sums, "sp")
    branch_norms = jnp.sqrt(summed / (lengths.astype(jnp.float32) * width))
    return (
        block_out,
        input_grad,
        shards[0],
        shards[1],
        shards[2],
        shards[3],
        feed_shards[0],
        feed_shards[1],
        feed_shards[2],
        shards[4],
        shards[5],
        branch_norms,
    )


def solution(mesh):
    in_specs = (
        P("dp", "sp", None),
        P("dp", "sp", None),
        P("dp"),
        P(("dp", "sp"), None),
        P(("dp", "sp"), None),
        P(("dp", "sp"), None),
        P(("dp", "sp"), None),
        P("dp", "sp"),
        P("dp", "sp"),
        P("sp", "dp"),
        P(("dp", "sp")),
        P(("dp", "sp")),
    )
    out_specs = (
        P("dp", "sp", None),
        P("dp", "sp", None),
        P(("dp", "sp"), None),
        P(("dp", "sp"), None),
        P(("dp", "sp"), None),
        P(("dp", "sp"), None),
        P("dp", "sp"),
        P("dp", "sp"),
        P("sp", "dp"),
        P(("dp", "sp")),
        P(("dp", "sp")),
        P(None, "dp"),
    )
    return jax.shard_map(body, mesh=mesh, in_specs=in_specs, out_specs=out_specs, check_vma=False)
```

profile of v0, /device:TPU:0, one launch (start us, length us, event | category | flops | bytes accessed | tf_op | source)
XLA Modules:
  0.0 2654.9 jit_solution(3752361866947182295)
XLA Ops:
  11.7 42.0 %all-reduce.9 = (bf16[2048]{0:T(1024)(128)(2,1)S(1)}, bf16[2048]{0:T(1024)(128)(2,1)}) all-reduce(bf16[2048]{0:T(1024)(128)(2,1)S(1)} %dynamic-update-slice, bf16[2048]{0:T(1024)(128)(2,1)S(1)} %dynamic-update-slice.1), channel_id=1, replica_groups=mesh['dp'=8,'sp'=4] {'dp','sp'}, use_global_device_ids=true, to_apply=%add.4 | all-reduce | flops 4096 | bytes 16384
  77.8 47.0 %all-gather.14.cloned.1.call-done = bf16[2048,256]{1,0:T(8,128)(2,1)} async-done(((bf16[64,256]{1,0:T(8,128)(2,1)}), bf16[2048,256]{1,0:T(8,128)(2,1)}) %all-gather.14.cloned.1.call-update) | async-done | bytes 1048592 | tf_op jit(solution)/shard_map/all_gather | solution.py:143
  136.0 77.2 %all-gather.10.cloned.1.call-done = bf16[2048,2048]{1,0:T(8,128)(2,1)} async-done(((bf16[64,2048]{1,0:T(8,128)(2,1)}), bf16[2048,2048]{1,0:T(8,128)(2,1)}) %all-gather.10.cloned.1.call-update) | async-done | bytes 8388624 | tf_op jit(solution)/shard_map/all_gather | solution.py:141
  268.3 12.5 all-to-all-done
  294.4 126.1 %while.54 = (s32[]{:T(128)}, bf16[3,512,8,64]{1,3,2,0:T(8,128)(2,1)}, f32[3,8,512,1]{2,1,3,0:T(8,128)}, s32[3]{0:T(128)S(1)}, s32[]{:T(128)}, /*index=5*/bf16[3,...) while((s32[]{:T(128)}, ...), condition=%wide.region_4.5_spmd, body=%wide.region_1.4_spmd.sunk | while | flops 1687943168 | bytes 82975872 | solution.py:74
  296.9 14.4 fusion.231
  311.3 12.2 fusion.232
  323.5 12.8 fusion.233
  339.5 14.4 fusion.231
  365.6 12.8 fusion.233
  381.4 14.1 fusion.231
  407.2 12.7 fusion.233
  430.6 115.2 %while.55 = (s32[]{:T(128)}, bf16[3,512,8,64]{1,3,2,0:T(8,128)(2,1)}, f32[3,8,512,1]{2,1,3,0:T(8,128)S(1)}, s32[3]{0:T(128)S(1)}, s32[]{:T(128)}, /*index=5*/bf1...) while((s32[]{:T(128)}, ...), condition=%wide.region_8.9_spmd, body=%wide.region_5.8_spmd.sunk | while | flops 1687943168 | bytes 82975872 | solution.py:74
  433.3 11.9 fusion.237
  456.9 12.2 fusion.239
  471.7 11.9 fusion.237
  495.3 12.2 fusion.239
  533.6 12.2 fusion.239
  578.6 36.7 %all-to-all-done.3 = bf16[4,2,196608]{2,1,0:T(2,128)(2,1)S(1)} async-done(((bf16[4,2,196608]{2,1,0:T(2,128)(2,1)}), bf16[4,2,196608]{2,1,0:T(2,128)(2,1)S(1)}, u32[]{:S(2)}, u32[]{:S(2)}) %all-to-all-start.3) | async-done | bytes 3145760 | tf_op jit(solution)/shard_map/all_to_all | solution.py:193
  633.1 12.2 multiply_reduce_fusion.2
  654.1 76.7 %all-gather.18.cloned.1.call-done = bf16[3072,2048]{1,0:T(8,128)(2,1)} async-done(((bf16[768,2048]{1,0:T(8,128)(2,1)}), bf16[3072,2048]{1,0:T(8,128)(2,1)}) %all-gather.18.cloned.1.call-update) | async-done | bytes 12582928 | tf_op jit(solution)/shard_map/all_gather | solution.py:199
  730.8 25.9 fusion.146
  756.7 69.0 %all-gather.20.cloned.1.call-done = bf16[2048,1408]{1,0:T(8,128)(2,1)} async-done(((bf16[256,1408]{1,0:T(8,128)(2,1)}), bf16[2048,1408]{1,0:T(8,128)(2,1)}) %all-gather.20.cloned.1.call-update) | async-done | bytes 5767184 | tf_op jit(solution)/shard_map/all_gather | solution.py:157
  825.6 25.7 fusion.145
  851.4 68.1 %all-gather.24.cloned.1.call-done = bf16[1408,2048]{1,0:T(8,128)(2,1)} async-done(((bf16[1408,256]{1,0:T(8,128)(2,1)}), bf16[1408,2048]{1,0:T(8,128)(2,1)}) %all-gather.24.cloned.1.call-update) | async-done | bytes 5767184 | tf_op jit(solution)/shard_map/all_gather | solution.py:159
  919.5 82.5 %all-gather.26.cloned.1.call-done = bf16[3072,2048]{1,0:T(8,128)(2,1)} async-done(((bf16[768,2048]{1,0:T(8,128)(2,1)}), bf16[3072,2048]{1,0:T(8,128)(2,1)}) %all-gather.26.cloned.1.call-update) | async-done | bytes 12582928 | tf_op jit(solution)/shard_map/all_gather | solution.py:214
  1001.9 36.4 %multiply_convert_fusion.2 = (bf16[3072,1408]{1,0:T(8,128)(2,1)}, bf16[3072,1408]{1,0:T(8,128)(2,1)}, bf16[3072,1408]{1,0:T(8,128)(2,1)}) fusion(f32[3072,1408]{1,0:T(8,128)} %fusion.145, f32[3072,1408]{1,0:T(8,128)} %fusion.146, bf16[3072,2048]{1,0:T(8,128)(2,1)} %all-gather.26.cloned.1.call-done, bf16[1408,2048]{1,0:T(8,128)(2,1)} %all-gather.24.cloned.1.call-done), kind=kOutput, calls=%fused_computation.107 | convolution fusion | flops 17785946112 | bytes 78905344 | tf_op jit(solution)/shard_map/rd,fd->rf/dot_general | solution.py:218
  1038.4 26.4 fusion.147
  1064.8 28.1 %add_convert_fusion = bf16[3072,2048]{1,0:T(8,128)(2,1)} fusion(f32[3072,2048]{1,0:T(8,128)} %fusion.147, bf16[3072,1408]{1,0:T(8,128)(2,1)} %get-tuple-element.707, bf16[2048,1408]{1,0:T(8,128)(2,1)} %all-gather.22.cloned.1.call-done), kind=kOutput, calls=%fused_computation.103 | convolution fusion | flops 17729323008 | bytes 52166656 | tf_op jit(solution)/shard_map/rf,df->rd/dot_general | solution.py:227
  1092.9 25.2 convolution_convert_fusion
  1118.2 25.4 convolution_convert_fusion.1
  1143.7 26.4 convolution_convert_fusion.2
  1170.2 21.9 reduce-scatter.12.cloned.1.call-done
  1197.4 96.4 %reduce-scatter.10.cloned.1.call-done = bf16[768,2048]{1,0:T(8,128)(2,1)} async-done(((bf16[3072,2048]{1,0:T(8,128)(2,1)}), bf16[768,2048]{1,0:T(8,128)(2,1)}) %reduce-scatter.10.cloned.1.call-update) | async-done | bytes 3145744 | tf_op jit(solution)/shard_map/reduce_scatter | solution.py:206
  1323.9 26.4 convolution_convert_fusion.3
  1371.8 263.7 %while.56 = (s32[]{:T(128)}, f32[1536,8,64]{0,2,1:T(8,128)}, f32[1536,8,64]{0,2,1:T(8,128)}, bf16[3,512,8,64]{1,3,2,0:T(8,128)(2,1)}, bf16[3,512,8,64]{1,3,2,0:T...) while((s32[]{:T(128)}, f32[1536,8,64]{0,2,1:T(8,128)}, ...), condition=%wide.region_15.16_spmd.clone, body=%wide.region_13.15_spmd.clone.sunk | while | flops 4088920064 | bytes 210853040 | solution.py:112
  1387.1 18.2 multiply_reduce_fusion.5
  1405.3 22.1 multiply_convert_fusion.8
  1427.4 12.4 fusion.252
  1473.5 18.5 multiply_reduce_fusion.5
  1492.0 22.2 multiply_convert_fusion.8
  1514.2 13.2 fusion.252
  1562.3 18.2 multiply_reduce_fusion.5
  1580.6 21.9 multiply_convert_fusion.8
  1602.5 13.5 fusion.252
  1646.1 270.5 %while.57 = (s32[]{:T(128)}, f32[1536,8,64]{0,2,1:T(8,128)}, f32[1536,8,64]{0,2,1:T(8,128)}, bf16[3,512,8,64]{1,3,2,0:T(8,128)(2,1)}, bf16[3,512,8,64]{1,3,2,0:T...) while((s32[]{:T(128)}, f32[1536,8,64]{0,2,1:T(8,128)}, ...), condition=%wide.region_18.19_spmd.clone, body=%wide.region_16.18_spmd.clone.sunk | while | flops 4088920064 | bytes 210853040 | solution.py:112
  1661.5 22.0 multiply_reduce_fusion.6
  1683.4 21.4 multiply_convert_fusion.9
  1704.9 12.3 fusion.266
  1750.4 21.9 multiply_reduce_fusion.6
  1772.4 21.4 multiply_convert_fusion.9
  1793.8 13.2 fusion.266
  1841.2 21.9 multiply_reduce_fusion.6
  1863.1 21.4 multiply_convert_fusion.9
  1884.6 13.2 fusion.266
  1938.2 40.3 %all_to_all.102 = bf16[4,2,196608]{2,1,0:T(2,128)(2,1)} all-to-all(bf16[4,2,196608]{2,1,0:T(2,128)(2,1)S(1)} %reshape.491), channel_id=1, replica_groups=mesh['dp'=8,'sp'=4] {'sp'}, dimensions={0} | all-to-all | bytes 6291456 | tf_op jit(solution)/shard_map/all_to_all | solution.py:262
  2029.2 49.3 %all_to_all.103 = bf16[4,2,196608]{2,1,0:T(2,128)(2,1)} all-to-all(bf16[4,2,196608]{2,1,0:T(2,128)(2,1)} %reshape.489), channel_id=1, replica_groups=mesh['dp'=8,'sp'=4] {'sp'}, dimensions={0} | all-to-all | bytes 6291456 | tf_op jit(solution)/shard_map/all_to_all | solution.py:263
  2101.4 13.1 convolution_bitcast_fusion
  2154.1 49.4 %all_to_all.104 = bf16[4,2,196608]{2,1,0:T(2,128)(2,1)} all-to-all(bf16[4,2,196608]{2,1,0:T(2,128)(2,1)} %reshape.487), channel_id=1, replica_groups=mesh['dp'=8,'sp'=4] {'sp'}, dimensions={0} | all-to-all | bytes 6291456 | tf_op jit(solution)/shard_map/all_to_all | solution.py:261
  2237.1 12.9 convolution_bitcast_fusion.1
  2270.4 16.6 fusion.97
  2298.7 44.0 %all-reduce.8 = (f32[2048]{0:T(1024)S(1)}, f32[2048]{0:T(1024)S(1)}) all-reduce(f32[2048]{0:T(1024)S(1)} %get-tuple-element.612, f32[2048]{0:T(1024)S(1)} %copy-done.26), channel_id=11, replica_groups=mesh['dp'=8,'sp'=4] {'dp','sp'}, use_global_device_ids=true, to_apply=%region_30.31.clone | all-reduce | flops 4096 | bytes 32768
  2351.4 109.9 %reduce-scatter.20.cloned.1.call-done = f32[64,2048]{1,0:T(8,128)} async-done(((f32[2048,2048]{1,0:T(8,128)}), f32[64,2048]{1,0:T(8,128)}) %reduce-scatter.20.cloned.1.call-update) | async-done | bytes 524304 | tf_op jit(solution)/shard_map/reduce_scatter | solution.py:301
  2461.3 186.5 %reduce-scatter.14.cloned.1.call-done = f32[64,2048]{1,0:T(8,128)} async-done(((f32[2048,2048]{1,0:T(8,128)}), f32[64,2048]{1,0:T(8,128)}) %reduce-scatter.14.cloned.1.call-update) | async-done | bytes 524304 | tf_op jit(solution)/shard_map/reduce_scatter | solution.py:298
  (370 shorter events, 745.7 us)
Async XLA Ops:
  7.2 60.1 %all-gather.12.cloned.1.call-start = ((), (), s32[]{:S(2)}) async-start(), calls=%async_computation.18 | async-start | bytes 1081344 | tf_op jit(solution)/shard_map/all_gather | solution.py:142
  7.9 117.0 %all-gather.14.cloned.1.call-start = ((), (), s32[]{:S(2)}) async-start(), calls=%async_computation.19 | async-start | bytes 1081344 | tf_op jit(solution)/shard_map/all_gather | solution.py:143
  8.7 204.5 %all-gather.10.cloned.1.call-start = ((), (), s32[]{:S(2)}) async-start(), calls=%async_computation.17 | async-start | bytes 8650752 | tf_op jit(solution)/shard_map/all_gather | solution.py:141
  9.4 623.7 %all-gather.16.cloned.1.call-start = ((), (), s32[]{:S(2)}) async-start(), calls=%async_computation.20 | async-start | bytes 8650752 | tf_op jit(solution)/shard_map/all_gather | solution.py:144
  53.7 159.5 %copy-start.24 = (f32[2048]{0:T(1024)}, f32[2048]{0:T(1024)S(1)}, u32[]{:S(2)}) copy-start(f32[2048]{0:T(1024)S(1)} %convert_element_type.224) | copy-start | bytes 24580
  54.6 169.4 %copy-start.11 = (f32[384,64]{0,1:T(8,128)}, f32[384,64]{0,1:T(8,128)S(1)}, u32[]{:S(2)}) copy-start(f32[384,64]{0,1:T(8,128)S(1)} %pad_maximum_fusion.4) | copy-start | bytes 294916
  54.6 169.3 %copy-start.13 = (f32[384,64]{0,1:T(8,128)}, f32[384,64]{0,1:T(8,128)S(1)}, u32[]{:S(2)}) copy-start(f32[384,64]{0,1:T(8,128)S(1)} %pad_maximum_fusion.5) | copy-start | bytes 294916
  57.9 155.3 %copy-start.33 = (f32[2,384]{1,0:T(2,128)}, f32[2,384]{1,0:T(2,128)S(1)}, u32[]{:S(2)}) copy-start(f32[2,384]{1,0:T(2,128)S(1)} %fusion.126) | copy-start | bytes 9220
  70.8 54.1 %copy-start.6 = (bf16[2,384,2048]{2,1,0:T(8,128)(2,1)S(1)}, bf16[2,384,2048]{2,1,0:T(8,128)(2,1)}, u32[]{:S(2)}) copy-start(bf16[2,384,2048]{2,1,0:T(8,128)(2,1)} %param.20) | copy-start | bytes 9437188
  73.2 55.0 %all-to-all-start.1 = ((bf16[2,384,32,64]{1,3,0,2:T(8,128)(2,1)}), bf16[2,384,32,64]{1,3,0,2:T(8,128)(2,1)}, u32[]{:S(2)}, u32[]{:S(2)}) async-start(bf16[2,384,32,64]{1,3,0,2:T(8,128)(2,1)} %bitcast.357), calls=%async_computation.1 | async-start | bytes 6291456 | tf_op jit(solution)/shard_map/all_to_all | solution.py:178
  131.3 96.3 %all-to-all-start.2 = ((bf16[2,384,32,64]{1,3,0,2:T(8,128)(2,1)}), bf16[2,384,32,64]{1,3,0,2:T(8,128)(2,1)}, u32[]{:S(2)}, u32[]{:S(2)}) async-start(bf16[2,384,32,64]{1,3,0,2:T(8,128)(2,1)} %bitcast.356), calls=%async_computation.2 | async-start | bytes 6291456 | tf_op jit(solution)/shard_map/all_to_all | solution.py:179
  225.5 6.8 copy-start.37
  227.6 53.2 %all-to-all-start = ((bf16[2,384,32,64]{1,3,0,2:T(8,128)(2,1)}), bf16[2,384,32,64]{1,3,0,2:T(8,128)(2,1)S(1)}, u32[]{:S(2)}, u32[]{:S(2)}) async-start(bf16[2,384,32,64]{1,3,0,2:T(8,128)(2,1)} %copy.241), calls=%async_computation | async-start | bytes 6291456 | tf_op jit(solution)/shard_map/all_to_all | solution.py:177
  231.8 422.3 %all-gather.22.cloned.1.call-start = ((), (), s32[]{:S(2)}) async-start(), calls=%async_computation.23 | async-start | bytes 6488064 | tf_op jit(solution)/shard_map/all_gather | solution.py:158
  420.5 10.1 copy-start
  420.5 10.1 copy-start.2
  545.9 11.8 copy-start.19
  545.9 11.8 copy-start.46
  566.9 11.5 copy-start.40
  566.9 11.6 copy-start.31
  566.9 11.6 copy-start.38
  574.7 40.6 %all-to-all-start.3 = ((bf16[4,2,196608]{2,1,0:T(2,128)(2,1)}), bf16[4,2,196608]{2,1,0:T(2,128)(2,1)S(1)}, u32[]{:S(2)}, u32[]{:S(2)}) async-start(bf16[4,2,196608]{2,1,0:T(2,128)(2,1)} %reshape.485), calls=%async_computation.3 | async-start | bytes 6291456 | tf_op jit(solution)/shard_map/all_to_all | solution.py:193
  578.4 152.4 %all-gather.18.cloned.1.call-start = ((), (), s32[]{:S(2)}) async-start(), calls=%async_computation.21 | async-start | bytes 15728640 | tf_op jit(solution)/shard_map/all_gather | solution.py:199
  578.5 67.4 %copy-start.20 = (f32[2048]{0:T(1024)}, f32[2048]{0:T(1024)S(1)}, u32[]{:S(2)}) copy-start(f32[2048]{0:T(1024)S(1)} %convert_element_type.234) | copy-start | bytes 24580
  578.6 54.5 %copy-start.42 = (pred[2,384]{1,0:T(4,128)(4,1)}, pred[2,384]{1,0:T(4,128)(4,1)S(1)}, u32[]{:S(2)}) copy-start(pred[2,384]{1,0:T(4,128)(4,1)S(1)} %get-tuple-element.696) | copy-start | bytes 2308
  578.6 73.2 %copy-start.29 = (f32[2,384]{1,0:T(2,128)}, f32[2,384]{1,0:T(2,128)S(1)}, u32[]{:S(2)}) copy-start(f32[2,384]{1,0:T(2,128)S(1)} %get-tuple-element.695) | copy-start | bytes 9220
  620.6 12.4 copy-start.7
  645.9 4.3 copy-start.22
  647.9 3.9 copy-start.9
  650.2 175.5 %all-gather.20.cloned.1.call-start = ((), (), s32[]{:S(2)}) async-start(), calls=%async_computation.22 | async-start | bytes 6488064 | tf_op jit(solution)/shard_map/all_gather | solution.py:157
  650.9 268.6 %all-gather.24.cloned.1.call-start = ((), (), s32[]{:S(2)}) async-start(), calls=%async_computation.24 | async-start | bytes 6488064 | tf_op jit(solution)/shard_map/all_gather | solution.py:159
  651.7 350.3 %all-gather.26.cloned.1.call-start = ((), (), s32[]{:S(2)}) async-start(), calls=%async_computation.26 | async-start | bytes 15728640 | tf_op jit(solution)/shard_map/all_gather | solution.py:214
  654.0 538.1 %reduce-scatter.12.cloned.1.call-start = ((), (), s32[]{:S(2)}) async-start(), calls=%async_computation.27 | async-start | bytes 15728640 | tf_op jit(solution)/shard_map/reduce_scatter | solution.py:229
  1092.9 200.9 %reduce-scatter.10.cloned.1.call-start = ((), (), s32[]{:S(2)}) async-start(), calls=%async_computation.25 | async-start | bytes 15728640 | tf_op jit(solution)/shard_map/reduce_scatter | solution.py:206
  1118.1 1133.8 %reduce-scatter.26.cloned.1.call-start = ((), (), s32[]{:S(2)}) async-start(), calls=%async_computation.34 | async-start | bytes 6488064 | tf_op jit(solution)/shard_map/reduce_scatter | solution.py:312
  1143.6 48.5 %copy-start.21 = (f32[2048]{0:T(1024)S(1)}, f32[2048]{0:T(1024)}, u32[]{:S(2)}) copy-start(f32[2048]{0:T(1024)} %copy-done.20) | copy-start | bytes 24580
  1143.6 48.4 %copy-start.23 = (f32[2,384]{1,0:T(2,128)S(1)}, f32[2,384]{1,0:T(2,128)}, u32[]{:S(2)}) copy-start(f32[2,384]{1,0:T(2,128)} %copy-done.22) | copy-start | bytes 9220
  1143.6 1110.6 %reduce-scatter.24.cloned.1.call-start = ((), (), s32[]{:S(2)}) async-start(), calls=%async_computation.33 | async-start | bytes 6488064 | tf_op jit(solution)/shard_map/reduce_scatter | solution.py:309
  1170.1 27.3 %copy-start.36 = (f32[2,384]{1,0:T(2,128)S(1)}, f32[2,384]{1,0:T(2,128)}, u32[]{:S(2)}) copy-start(f32[2,384]{1,0:T(2,128)} %copy-done.35) | copy-start | bytes 9220
  1170.1 123.7 %copy-start.10 = (bf16[2,384,2048]{2,1,0:T(8,128)(2,1)S(1)}, bf16[2,384,2048]{2,1,0:T(8,128)(2,1)}, u32[]{:S(2)}) copy-start(bf16[2,384,2048]{2,1,0:T(8,128)(2,1)} %param.21) | copy-start | bytes 9437188
  1170.1 123.7 %copy-start.30 = (f32[2,384]{1,0:T(2,128)S(1)}, f32[2,384]{1,0:T(2,128)}, u32[]{:S(2)}) copy-start(f32[2,384]{1,0:T(2,128)} %copy-done.29) | copy-start | bytes 9220
  1300.9 2.6 copy-start.5
  1320.1 40.6 %all-to-all-start.4 = ((bf16[2,384,32,64]{1,3,0,2:T(8,128)(2,1)}), bf16[2,384,32,64]{1,3,0,2:T(8,128)(2,1)S(1)}, u32[]{:S(2)}, u32[]{:S(2)}) async-start(bf16[2,384,32,64]{1,3,0,2:T(8,128)(2,1)} %copy.260), calls=%async_computation.6 | async-start | bytes 6291456 | tf_op jit(solution)/shard_map/all_to_all | solution.py:243
  1323.8 963.2 %reduce-scatter.22.cloned.1.call-start = ((), (), s32[]{:S(2)}) async-start(), calls=%async_computation.32 | async-start | bytes 6488064 | tf_op jit(solution)/shard_map/reduce_scatter | solution.py:306
  1350.3 1001.2 %reduce-scatter.16.cloned.1.call-start = ((), (), s32[]{:S(2)}) async-start(), calls=%async_computation.29 | async-start | bytes 2162688 | tf_op jit(solution)/shard_map/reduce_scatter | solution.py:299
  1363.4 8.4 copy-start.47
  1635.5 10.6 copy-start.1
  1635.5 10.6 copy-start.3
  1986.0 11.4 copy-start.14
  1986.0 12.9 copy-start.12
  1986.0 15.2 copy-start.8
  1986.0 15.2 copy-start.25
  1986.0 15.1 copy-start.34
  2003.9 347.5 %reduce-scatter.18.cloned.1.call-start = ((), (), s32[]{:S(2)}) async-start(), calls=%async_computation.30 | async-start | bytes 2162688 | tf_op jit(solution)/shard_map/reduce_scatter | solution.py:300
  2101.3 360.0 %reduce-scatter.20.cloned.1.call-start = ((), (), s32[]{:S(2)}) async-start(), calls=%async_computation.31 | async-start | bytes 17301504 | tf_op jit(solution)/shard_map/reduce_scatter | solution.py:301
  2114.5 533.3 %reduce-scatter.14.cloned.1.call-start = ((), (), s32[]{:S(2)}) async-start(), calls=%async_computation.28 | async-start | bytes 17301504 | tf_op jit(solution)/shard_map/reduce_scatter | solution.py:298
  2254.3 12.2 copy-start.16
  2261.4 5.2 copy-start.18
  2261.4 9.0 copy-start.43
  2270.4 16.7 copy-start.41
  2270.4 16.7 copy-start.44
  2270.4 28.4 %copy-start.26 = (f32[2048]{0:T(1024)S(1)}, f32[2048]{0:T(1024)}, u32[]{:S(2)}) copy-start(f32[2048]{0:T(1024)} %get-tuple-element.610) | copy-start | bytes 24580
  2270.4 73.5 %copy-start.45 = (f32[2]{0:T(128)S(1)}, f32[2]{0:T(128)}, u32[]{:S(2)}) copy-start(f32[2]{0:T(128)} %convert_multiply_fusion.7) | copy-start | bytes 28
  2270.4 74.2 %copy-start.28 = (f32[2,384]{1,0:T(2,128)S(1)}, f32[2,384]{1,0:T(2,128)}, u32[]{:S(2)}) copy-start(f32[2,384]{1,0:T(2,128)} %copy-done.27) | copy-start | bytes 9220
  (7 other events, 6.7 us)
Sparse Core Ops, SparseCore 0:
  10.9 56.3 all-gather.11
  70.2 54.6 all-gather.13
  127.7 85.4 all-gather.9
  215.9 88.0 all-gather.15
  306.1 91.2 all-gather.21
  650.3 80.4 all-gather.17
  732.9 92.6 all-gather.19
  827.7 91.7 all-gather.23
  921.6 80.2 all-gather.25
  1093.0 99.0 reduce-scatter.11
  1194.7 99.0 reduce-scatter.9
  1297.3 110.3 reduce-scatter.25
  1411.3 109.7 reduce-scatter.23
  1524.6 109.7 reduce-scatter.21
  2004.0 137.0 reduce-scatter.15
  2143.9 133.4 reduce-scatter.17
  2280.2 181.0 reduce-scatter.19
  2464.0 183.7 reduce-scatter.13
where the time goes:
time: 2670 us; the launch traced here: 2650 us
  waiting for transfers between devices  909 us (34%)
  matrix products  877 us (33%)
  other arithmetic  315 us (12%)
  local copies, waits for them, and re-layouts  282 us (11%)
  blocking collectives  234 us (9%)
    dot_general x12, matrix products, score_block(): jnp.einsum('qhd,khd->hqk', query_block, keys, preferred_element_type=jnp....  199 us
    reduce_scatter x1, waiting for transfers between devices, body(): lax.psum_scatter(query_wgrad, ('dp', 'sp'), scatter_dimension=0, tiled=True)  187 us
    convert_element_type x12, other arithmetic, to_low(): return values.astype(jnp.bfloat16)  143 us
    reduce_scatter x1, waiting for transfers between devices, body(): lax.psum_scatter(output_wgrad, ('dp', 'sp'), scatter_dimension=0, tiled=T...  110 us
    dot_general x7, matrix products, project(): jnp.einsum('...d,df->...f', left, right, preferred_element_type=jnp.float32)  105 us
    reduce_scatter x1, waiting for transfers between devices, body(): lax.psum_scatter(project(hidden, down_part).astype(jnp.bfloat16), 'sp', s...  96.4 us
    unnamed x2, blocking collectives  86 us
    all_gather x1, waiting for transfers between devices, body(): lax.all_gather(to_low(res_grad).reshape(seq_dev * local_len, width), 'sp'...  82.5 us
  transfers between devices with their start and end apart: 23, of which 14 were waited for; matrix products, arithmetic and copies ran while one was open for 52% of the time, Pallas kernels for 0%

commit v1 on v0

v1 whole, which is shorter than its diff:
```python
import functools

import jax
import jax.numpy as jnp
from jax import lax
from jax.experimental import pallas as pl
from jax.experimental.pallas import tpu as pltpu
from jax.experimental.layout import Layout, with_layout_constraint
from jax.sharding import PartitionSpec as P

HEADS = 32
KV = 4
HD = 64
HALF = HD // 2
EPS = 1e-05
F32 = jnp.float32
BF16 = jnp.bfloat16
SCALE = HD ** (-0.5)
NEG = -1e30


def dot(left, right, left_dim, right_dim):
    return lax.dot_general(
        left, right, (((left_dim,), (right_dim,)), ((), ())), preferred_element_type=F32
    )


def swap(values, bit, count, axis="sp"):
    return lax.ppermute(values, axis, [(i, i ^ bit) for i in range(count)])


def order_of(count):
    order = [0]
    bit = count // 2
    while bit:
        order += [member ^ bit for member in order]
        bit //= 2
    return order


def spread(block, count, axis="sp", stop=1):
    parts = list(block) if isinstance(block, (list, tuple)) else [block]
    bit = count // (2 * len(parts))
    while bit >= stop:
        parts += [swap(part, bit, count, axis) for part in parts]
        bit //= 2
    return parts


def after(values, *others):
    return lax.optimization_barrier((values,) + others)[0]


def gather_rows(block, count):
    return jnp.concatenate(spread(block, count), axis=0)


def gather_bits(stack, count, high, low):
    me = lax.axis_index("dp")
    bit = high
    while bit >= low:
        got = swap(stack, bit, count, "dp")
        stack = widen(stack, got, (me & bit) != 0)
        bit //= 2
    return stack, got


def widen(mine, other, odd):
    first = jnp.where(odd, other, mine)
    second = jnp.where(odd, mine, other)
    return jnp.stack([first, second], axis=1).reshape((-1,) + mine.shape[1:])


def halve(left, bit, count, axis="dp"):
    side = (lax.axis_index(axis) & bit) // bit
    pairs = left.reshape((left.shape[0] // 2, 2) + left.shape[1:])
    leaving = lax.dynamic_index_in_dim(pairs, 1 - side, 1, False)
    staying = lax.dynamic_index_in_dim(pairs, side, 1, False)
    return staying, swap(leaving, bit, count, axis)


def join(staying, got):
    return staying.astype(F32) + got.astype(F32)


def finish(left, bit, count, axis="dp"):
    kind = left.dtype
    while bit < count:
        left = join(*halve(left.astype(kind), bit, count, axis))
        bit *= 2
    return left[0].astype(F32)


def blocks_of(values, count):
    return values.reshape((count, values.shape[0] // count) + values.shape[1:])


def reduce_near(product, rows, count):
    half = rows // 2
    got = swap(product(half, rows).astype(BF16), 1, count)
    return product(0, half) + got.astype(F32)


def reduce_pair(keep, send, count):
    return keep.astype(F32) + swap(send, 1, count).astype(F32)


def reduce_far(left, count):
    bit = 2
    while bit < count:
        half = left.shape[0] // 2
        got = swap(left[half:].astype(BF16), bit, count)
        left = left[:half] + got.astype(F32)
        bit *= 2
    return left


def flip_blocks(values, count, to_absolute):
    me = lax.axis_index("sp")
    order = order_of(count)
    size = values.shape[-1] // count
    blocks = [values[..., j * size : (j + 1) * size] for j in range(count)]
    if to_absolute:
        blocks = [blocks[order.index(offset)] for offset in range(count)]
    bit = 1
    while bit < count:
        odd = (me & bit) != 0
        blocks = [jnp.where(odd, blocks[j ^ bit], blocks[j]) for j in range(count)]
        bit *= 2
    if not to_absolute:
        blocks = [blocks[offset] for offset in order]
    return jnp.concatenate(blocks, axis=-1)


def row_major(values):
    return with_layout_constraint(values, Layout(major_to_minor=tuple(range(values.ndim))))


def block_of(length):
    for size in (256, 128):
        if length % size == 0:
            return size
    return length


def forward_kernel(block, len_ref, q_ref, k_ref, v_ref, out_ref, lse_ref):
    full = q_ref.shape[-1]
    length = len_ref[0]
    key_at = lax.broadcasted_iota(jnp.int32, (block, block), 0)
    row_at = lax.broadcasted_iota(jnp.int32, (block, block), 1)
    for step in range(full // block):
        start = step * block
        here = slice(start, start + block)
        queries = q_ref[0, :, here]
        near = jnp.dot(k_ref[here, :], queries, preferred_element_type=F32)
        near = jnp.where((key_at <= row_at) & (key_at + start < length), near, NEG)
        top = jnp.max(near, axis=0, keepdims=True)
        if start:
            far = jnp.dot(k_ref[0:start, :], queries, preferred_element_type=F32)
            top = jnp.maximum(top, jnp.max(far, axis=0, keepdims=True))
        near = jnp.exp(near - top)
        total = jnp.sum(near, axis=0, keepdims=True)
        result = jnp.dot(v_ref[:, here], near.astype(BF16), preferred_element_type=F32)
        if start:
            far = jnp.exp(far - top)
            total = total + jnp.sum(far, axis=0, keepdims=True)
            result = result + jnp.dot(
                v_ref[:, 0:start], far.astype(BF16), preferred_element_type=F32
            )
        out_ref[0, :, here] = (result / total).astype(BF16)
        lse_ref[0, :, here] = top + jnp.log(total)


def attend_forward(queries, keys, values_t, length):
    heads, _, full = queries.shape
    block = block_of(full)
    return pl.pallas_call(
        functools.partial(forward_kernel, block),
        grid=(heads,),
        in_specs=[
            pl.BlockSpec(memory_space=pltpu.SMEM),
            pl.BlockSpec((1, HD, full), lambda h: (h, 0, 0)),
            pl.BlockSpec((full, HD), lambda h: (0, 0)),
            pl.BlockSpec((HD, full), lambda h: (0, 0)),
        ],
        out_specs=[
            pl.BlockSpec((1, HD, full), lambda h: (h, 0, 0)),
            pl.BlockSpec((1, 1, full), lambda h: (h, 0, 0)),
        ],
        out_shape=[
            jax.ShapeDtypeStruct((heads, HD, full), BF16),
            jax.ShapeDtypeStruct((heads, 1, full), F32),
        ],
        compiler_params=pltpu.CompilerParams(vmem_limit_bytes=48 * 2**20),
        cost_estimate=pl.CostEstimate(
            flops=2 * heads * full * full * HD,
            bytes_accessed=heads * full * HD * 4,
            transcendentals=heads * full,
        ),
    )(length, queries, keys, values_t)


def backward_kernel(
    block, len_ref, q_ref, grad_ref, k_ref, kt_ref, v_ref, lse_ref, delta_ref, gq_ref, gk_ref, gv_ref, acc_ref
):
    full = q_ref.shape[-1]
    length = len_ref[0]

    @pl.when(pl.program_id(0) == 0)
    def _():
        gk_ref[...] = jnp.zeros_like(gk_ref)
        gv_ref[...] = jnp.zeros_like(gv_ref)

    key_at = lax.broadcasted_iota(jnp.int32, (block, block), 0)
    row_at = lax.broadcasted_iota(jnp.int32, (block, block), 1)
    for step in range(full // block):
        start = step * block
        here = slice(start, start + block)
        pieces = [(start, start + block, True)]
        if start + block < full:
            pieces.append((start + block, full, False))
        for low, high, edge in pieces:
            rows = slice(low, high)
            queries = q_ref[0, :, rows]
            grads = grad_ref[0, :, rows]
            scores = jnp.dot(k_ref[here, :], queries, preferred_element_type=F32)
            probs = jnp.exp(scores - lse_ref[0, :, rows])
            if edge:
                probs = jnp.where((key_at <= row_at) & (key_at + start < length), probs, 0.0)
            prob_grad = jnp.dot(v_ref[here, :], grads, preferred_element_type=F32)
            score_grad = (probs * (prob_grad - delta_ref[0, :, rows])).astype(BF16)
            gk_ref[here, :] += dot(score_grad, queries, 1, 1)
            gv_ref[here, :] += dot(probs.astype(BF16), grads, 1, 1)
            part = jnp.dot(kt_ref[:, here], score_grad, preferred_element_type=F32)
            if step == 0:
                acc_ref[:, rows] = part
            else:
                acc_ref[:, rows] += part
    gq_ref[0] = (acc_ref[...] * SCALE).astype(BF16)


def attend_backward(queries, grads, keys, keys_t, values, lse, delta, length):
    heads, _, full = queries.shape
    block = block_of(full)
    per_head = pl.BlockSpec((1, HD, full), lambda h: (h, 0, 0))
    per_row = pl.BlockSpec((1, 1, full), lambda h: (h, 0, 0))
    whole = pl.BlockSpec((full, HD), lambda h: (0, 0))
    return pl.pallas_call(
        functools.partial(backward_kernel, block),
        grid=(heads,),
        in_specs=[
            pl.BlockSpec(memory_space=pltpu.SMEM),
            per_head,
            per_head,
            whole,
            pl.BlockSpec((HD, full), lambda h: (0, 0)),
            whole,
            per_row,
            per_row,
        ],
        out_specs=[per_head, whole, whole],
        out_shape=[
            jax.ShapeDtypeStruct((heads, HD, full), BF16),
            jax.ShapeDtypeStruct((full, HD), F32),
            jax.ShapeDtypeStruct((full, HD), F32),
        ],
        scratch_shapes=[pltpu.VMEM((HD, full), F32)],
        compiler_params=pltpu.CompilerParams(vmem_limit_bytes=48 * 2**20),
        cost_estimate=pl.CostEstimate(
            flops=4 * heads * full * full * HD,
            bytes_accessed=heads * full * HD * 6,
            transcendentals=heads * full,
        ),
    )(length, queries, grads, keys, keys_t, values, lse, delta)


TILE = 256


def tiles_of(hidden):
    if hidden % 128:
        return [(0, hidden)]
    return [(low, min(low + TILE, hidden)) for low in range(0, hidden, TILE)]


def interleave(gate, up):
    return jnp.concatenate(
        [array[:, low:high] for low, high in tiles_of(gate.shape[1]) for array in (gate, up)], axis=1
    )


def separate(both):
    pieces = tiles_of(both.shape[1] // 2)
    gate = [both[:, 2 * low : low + high] for low, high in pieces]
    up = [both[:, low + high : 2 * high] for low, high in pieces]
    return jnp.concatenate(gate, axis=1), jnp.concatenate(up, axis=1)


def activate(gate, up, grad):
    sig = 1.0 / (1.0 + jnp.exp(-gate))
    act = gate * sig
    slope = sig * (1.0 + gate * (1.0 - sig))
    return (act * up).astype(BF16), (grad * up * slope).astype(BF16), (grad * act).astype(BF16)


def feed_kernel(last, blocks, *refs):
    n2_parts, grad_parts = refs[:blocks], refs[blocks : 2 * blocks]
    refs = refs[2 * blocks :]
    gu_ref, down_ref, hid_ref, out_ref, n2_out, grad_out = refs[:6]
    refs = refs[6:]
    n2_ref, grad_ref, in_sems, out_sems = refs
    part = n2_parts[0].shape[0]
    step = pl.program_id(0)
    count = pl.num_programs(0)

    def arriving(j):
        here = pl.ds(j * part, part)
        return (
            pltpu.make_async_copy(n2_parts[j], n2_ref.at[here], in_sems.at[2 * j]),
            pltpu.make_async_copy(grad_parts[j], grad_ref.at[here], in_sems.at[2 * j + 1]),
        )

    def leaving():
        return (
            pltpu.make_async_copy(n2_ref, n2_out, out_sems.at[0]),
            pltpu.make_async_copy(grad_ref, grad_out, out_sems.at[1]),
        )

    def run(size, first):
        if first:
            for j in range(blocks):
                for copy in arriving(j):
                    copy.start()
        for j in range(blocks):
            here = slice(j * part, (j + 1) * part)
            if first:
                for copy in arriving(j):
                    copy.wait()
            values = n2_ref[here, :]
            if size == TILE:
                gate = jnp.dot(values, gu_ref[:, :size], preferred_element_type=F32)
                up = jnp.dot(values, gu_ref[:, size : 2 * size], preferred_element_type=F32)
            else:
                both = jnp.dot(values, gu_ref[:, : 2 * size], preferred_element_type=F32)
                gate, up = both[:, :size], both[:, size:]
            grad = jnp.dot(grad_ref[here, :], down_ref[:, :size], preferred_element_type=F32)
            hid, gate_grad, up_grad = activate(gate, up, grad)
            hid_ref[here, :size] = hid
            out_ref[here, :size] = gate_grad
            out_ref[here, size : 2 * size] = up_grad
        if first:
            for copy in leaving():
                copy.start()

    @pl.when(step == 0)
    def _():
        run(TILE, True)

    @pl.when((step > 0) & (step < count - 1))
    def _():
        run(TILE, False)

    @pl.when(step == count - 1)
    def _():
        run(last, False)
        for copy in leaving():
            copy.wait()


def feed(n2_parts, grad_parts, gu_w, down_t):
    blocks = len(n2_parts)
    part, width = n2_parts[0].shape
    rows = blocks * part
    hidden = down_t.shape[1]
    pieces = tiles_of(hidden)
    if hidden % 128 or len(pieces) < 3:
        n2 = jnp.concatenate(n2_parts, axis=0)
        grad = jnp.concatenate(grad_parts, axis=0)
        gate_w, up_w = separate(gu_w)
        hid, gate_grad, up_grad = activate(
            dot(n2, gate_w, 1, 0), dot(n2, up_w, 1, 0), dot(grad, down_t, 1, 0)
        )
        return hid, interleave(gate_grad, up_grad), n2, grad
    last = pieces[-1][1] - pieces[-1][0]
    hbm = pl.BlockSpec(memory_space=pl.ANY)
    return pl.pallas_call(
        functools.partial(feed_kernel, last, blocks),
        grid=(len(pieces),),
        in_specs=[hbm] * (2 * blocks)
        + [
            pl.BlockSpec((width, 2 * TILE), lambda j: (0, j)),
            pl.BlockSpec((width, TILE), lambda j: (0, j)),
        ],
        out_specs=[
            pl.BlockSpec((rows, TILE), lambda j: (0, j)),
            pl.BlockSpec((rows, 2 * TILE), lambda j: (0, j)),
            hbm,
            hbm,
        ],
        out_shape=[
            jax.ShapeDtypeStruct((rows, hidden), BF16),
            jax.ShapeDtypeStruct((rows, 2 * hidden), BF16),
            jax.ShapeDtypeStruct((rows, width), BF16),
            jax.ShapeDtypeStruct((rows, width), BF16),
        ],
        scratch_shapes=[
            pltpu.VMEM((rows, width), BF16),
            pltpu.VMEM((rows, width), BF16),
            pltpu.SemaphoreType.DMA((2 * blocks,)),
            pltpu.SemaphoreType.DMA((2,)),
        ],
        compiler_params=pltpu.CompilerParams(vmem_limit_bytes=56 * 2**20),
        cost_estimate=pl.CostEstimate(
            flops=rows * width * hidden,
            bytes_accessed=4 * rows * width,
            transcendentals=rows,
        ),
    )(*n2_parts, *grad_parts, gu_w, down_t)


def rotate(values, cos, sin):
    one, two = values[:, :HALF], values[:, HALF:]
    return jnp.concatenate([one * cos - two * sin, two * cos + one * sin], axis=1)


def rotate_back(grad, cos, sin):
    one, two = grad[:, :HALF], grad[:, HALF:]
    return jnp.concatenate([one * cos + two * sin, two * cos - one * sin], axis=1)


def fits(part):
    return part % 128 == 0


def place(at_ref, j, part):
    return pl.ds(pl.multiple_of(at_ref[j] * part, 128), part)


SMALL = pl.CostEstimate(flops=1000000, bytes_accessed=1000000, transcendentals=1000)
PARAMS = pltpu.CompilerParams(vmem_limit_bytes=56 * 2**20)
IN_HBM = pl.BlockSpec(memory_space=pl.ANY)
IN_VMEM = pl.BlockSpec(memory_space=pltpu.VMEM)
IN_SMEM = pl.BlockSpec(memory_space=pltpu.SMEM)


def fetch(parts, buf_ref, sems):
    part = parts[0].shape[0]
    return [
        pltpu.make_async_copy(source, buf_ref.at[pl.ds(j * part, part)], sems.at[j])
        for j, source in enumerate(parts)
    ]


def project_kernel(blocks, at_ref, *refs):
    parts = refs[:blocks]
    gain_ref, w_ref, cos_ref, sin_ref = refs[blocks : blocks + 4]
    n1_out, q_ref, kt_ref, vt_ref, k_ref, v_ref, buf_ref, in_sems, out_sems = refs[blocks + 4 :]
    part = parts[0].shape[0]
    heads = q_ref.shape[0]
    coming = fetch(parts, buf_ref, in_sems)
    for copy in coming:
        copy.start()
    leaving = []
    for j in range(blocks):
        coming[j].wait()
        for low in range(j * part, (j + 1) * part, 128):
            here = slice(low, low + 128)
            values = buf_ref[here, :].astype(F32)
            scale = lax.rsqrt(jnp.mean(values * values, axis=-1, keepdims=True) + EPS)
            buf_ref[here, :] = (values * scale * gain_ref[...]).astype(BF16)
        rows = pl.ds(j * part, part)
        leaving.append(pltpu.make_async_copy(buf_ref.at[rows], n1_out.at[rows], out_sems.at[j]))
        leaving[-1].start()
        proj = dot(w_ref[...], buf_ref[j * part : (j + 1) * part, :], 1, 1)
        cos = cos_ref[:, j * part : (j + 1) * part][None]
        sin = sin_ref[:, j * part : (j + 1) * part][None]
        there = place(at_ref, j, part)
        cut = heads * HD
        q = rotate(proj[:cut].reshape(heads, HD, part), cos, sin) * SCALE
        q_ref[:, :, there] = q.astype(BF16)
        k = rotate(proj[cut : cut + HD].reshape(1, HD, part), cos, sin)[0]
        v = proj[cut + HD :]
        kt_ref[:, there] = k.astype(BF16)
        vt_ref[:, there] = v.astype(BF16)
        k_ref[there, :] = k.T.astype(BF16)
        v_ref[there, :] = v.T.astype(BF16)
    for copy in leaving:
        copy.wait()


def project(parts, at, gain, w_t, cos, sin, heads):
    blocks = len(parts)
    part, width = parts[0].shape
    full = blocks * part
    if not fits(part):
        cut = heads * HD
        values = jnp.concatenate(parts, axis=0).astype(F32)
        scale = lax.rsqrt(jnp.mean(values * values, axis=-1, keepdims=True) + EPS)
        n1 = (values * scale * gain).astype(BF16)
        proj = dot(w_t, n1, 1, 1)
        q = rotate(proj[:cut].reshape(heads, HD, full), cos[None], sin[None]) * SCALE
        k = rotate(proj[cut : cut + HD].reshape(1, HD, full), cos[None], sin[None])
        both = jnp.concatenate([q.reshape(cut, full), k[0], proj[cut + HD :]], axis=0).astype(BF16)
        both = flip_blocks(both, blocks, True)
        k_t, v_t = both[cut : cut + HD], both[cut + HD :]
        return n1, both[:cut].reshape(heads, HD, full), k_t, v_t, k_t.T, v_t.T
    flat = jax.ShapeDtypeStruct((HD, full), BF16)
    tall = jax.ShapeDtypeStruct((full, HD), BF16)
    return pl.pallas_call(
        functools.partial(project_kernel, blocks),
        in_specs=[IN_SMEM] + [IN_HBM] * blocks + [IN_VMEM] * 4,
        out_specs=[IN_HBM] + [IN_VMEM] * 5,
        out_shape=[
            jax.ShapeDtypeStruct((full, width), BF16),
            jax.ShapeDtypeStruct((heads, HD, full), BF16),
            flat,
            flat,
            tall,
            tall,
        ],
        scratch_shapes=[
            pltpu.VMEM((full, width), BF16),
            pltpu.SemaphoreType.DMA((blocks,)),
            pltpu.SemaphoreType.DMA((blocks,)),
        ],
        compiler_params=PARAMS,
        cost_estimate=SMALL,
    )(at, *parts, gain, w_t, cos, sin)


def merge_kernel(blocks, at_ref, att_ref, w_ref, keep_ref, send_ref):
    part = att_ref.shape[1] // blocks
    for j in range(blocks):
        mine = att_ref[:, place(at_ref, j, part)]
        product = dot(mine, w_ref[...], 0, 0).astype(BF16)
        target, slot = (keep_ref, j) if j < blocks // 2 else (send_ref, j - blocks // 2)
        target[slot * part : (slot + 1) * part, :] = product


def merge_heads(att, at, out_w, blocks):
    cut, full = att.shape
    half = full // 2
    width = out_w.shape[1]
    if not fits(full // blocks):
        product = dot(flip_blocks(att, blocks, False), out_w, 0, 0).astype(BF16)
        return product[:half], product[half:]
    return pl.pallas_call(
        functools.partial(merge_kernel, blocks),
        in_specs=[IN_SMEM, IN_VMEM, IN_VMEM],
        out_specs=[IN_VMEM, IN_VMEM],
        out_shape=[jax.ShapeDtypeStruct((half, width), BF16)] * 2,
        compiler_params=PARAMS,
        cost_estimate=SMALL,
    )(at, att, out_w)


def split_kernel(blocks, has_sum, at_ref, *refs):
    parts = refs[:blocks]
    w_ref, att_ref = refs[blocks : blocks + 2]
    refs = refs[blocks + 2 :]
    if has_sum:
        sum_ref, refs = refs[0], refs[1:]
    grad_ref, delta_ref, wgrad_ref, buf_ref, acc_ref, sems = refs
    part = parts[0].shape[0]
    heads = att_ref.shape[0]
    coming = fetch(parts, buf_ref, sems)
    for copy in coming:
        copy.start()
    for j in range(blocks):
        coming[j].wait()
        rows = buf_ref[j * part : (j + 1) * part, :]
        there = place(at_ref, j, part)
        att = att_ref[:, :, there]
        grad = dot(w_ref[...], rows, 1, 1).astype(BF16).reshape(heads, HD, part)
        grad_ref[:, :, there] = grad
        delta_ref[:, :, there] = jnp.sum(
            grad.astype(F32) * att.astype(F32), axis=1, keepdims=True
        )
        share = jnp.dot(att.reshape(heads * HD, part), rows, preferred_element_type=F32)
        if j:
            acc_ref[...] += share
        elif has_sum:
            acc_ref[...] = sum_ref[...] + share
        else:
            acc_ref[...] = share
    wgrad_ref[...] = acc_ref[...].astype(wgrad_ref.dtype)


def split_heads(parts, at, out_w, att, so_far):
    blocks = len(parts)
    part, width = parts[0].shape
    heads, _, full = att.shape
    kind = F32 if so_far is None else BF16
    if not fits(part):
        rows = jnp.concatenate(parts, axis=0)
        grad = flip_blocks(dot(out_w, rows, 1, 1).astype(BF16), blocks, True)
        grad = grad.reshape(heads, HD, full)
        delta = jnp.sum(grad.astype(F32) * att.astype(F32), axis=1, keepdims=True)
        wgrad = dot(flip_blocks(att.reshape(heads * HD, full), blocks, False), rows, 1, 0)
        return grad, delta, (wgrad if so_far is None else so_far + wgrad).astype(kind)
    more = [] if so_far is None else [so_far]
    return pl.pallas_call(
        functools.partial(split_kernel, blocks, bool(more)),
        in_specs=[IN_SMEM] + [IN_HBM] * blocks + [IN_VMEM] * (2 + len(more)),
        out_specs=[IN_VMEM] * 3,
        out_shape=[
            jax.ShapeDtypeStruct((heads, HD, full), BF16),
            jax.ShapeDtypeStruct((heads, 1, full), F32),
            jax.ShapeDtypeStruct((heads * HD, width), kind),
        ],
        scratch_shapes=[
            pltpu.VMEM((full, width), BF16),
            pltpu.VMEM((heads * HD, width), F32),
            pltpu.SemaphoreType.DMA((blocks,)),
        ],
        compiler_params=PARAMS,
        cost_estimate=SMALL,
    )(at, *parts, out_w, att, *more)


def return_kernel(blocks, has_sum, at_ref, *refs):
    gq_ref, gk_ref, gv_ref, cos_ref, sin_ref, w_ref, n1_in = refs[:7]
    refs = refs[7:]
    if has_sum:
        sum_ref, refs = refs[0], refs[1:]
    keep_ref, send_ref, wgrad_ref, buf_ref, acc_ref, sems = refs
    heads, _, full = gq_ref.shape
    part = full // blocks
    coming = fetch([n1_in.at[pl.ds(j * part, part)] for j in range(blocks)], buf_ref, sems)
    for copy in coming:
        copy.start()
    for j in range(blocks):
        there = place(at_ref, j, part)
        cos = cos_ref[:, j * part : (j + 1) * part][None]
        sin = sin_ref[:, j * part : (j + 1) * part][None]
        gq = rotate_back(gq_ref[:, :, there].astype(F32), cos, sin)
        gk = rotate_back(gk_ref[there, :].T[None], cos, sin)[0]
        grad = jnp.concatenate(
            [
                gq.reshape(heads * HD, part).astype(BF16),
                gk.astype(BF16),
                gv_ref[there, :].T.astype(BF16),
            ],
            axis=0,
        )
        product = dot(grad, w_ref[...], 0, 0).astype(BF16)
        target, slot = (keep_ref, j) if j < blocks // 2 else (send_ref, j - blocks // 2)
        target[slot * part : (slot + 1) * part, :] = product
        coming[j].wait()
        share = jnp.dot(grad, buf_ref[j * part : (j + 1) * part, :], preferred_element_type=F32)
        if j:
            acc_ref[...] += share
        elif has_sum:
            acc_ref[...] = sum_ref[...] + share
        else:
            acc_ref[...] = share
    if has_sum:
        groups, _, columns = wgrad_ref.shape
        for d in range(groups):
            wgrad_ref[d] = acc_ref[:, d * columns : (d + 1) * columns].astype(BF16)
    else:
        wgrad_ref[...] = acc_ref[...]


def return_rows(gq, gk, gv, at, cos, sin, w_t, n1, so_far, groups):
    heads, _, full = gq.shape
    blocks = at.shape[0]
    columns, width = w_t.shape
    half = full // 2
    last = so_far is not None
    if not fits(full // blocks):
        back = jnp.concatenate([gq.reshape(heads * HD, full).astype(F32), gk.T, gv.T], axis=0)
        back = flip_blocks(back, blocks, False)
        turned = rotate_back(
            back[: heads * HD + HD].reshape(heads + 1, HD, full), cos[None], sin[None]
        )
        grad = jnp.concatenate(
            [turned.reshape(heads * HD + HD, full), back[heads * HD + HD :]], axis=0
        ).astype(BF16)
        product = dot(grad, w_t, 0, 0).astype(BF16)
        wgrad = dot(grad, n1, 1, 0)
        if last:
            wgrad = (so_far + wgrad).astype(BF16)
            wgrad = wgrad.reshape(columns, groups, width // groups).transpose(1, 0, 2)
        return product[:half], product[half:], wgrad
    more = [so_far] if last else []
    shape = (groups, columns, width // groups) if last else (columns, width)
    return pl.pallas_call(
        functools.partial(return_kernel, blocks, last),
        in_specs=[IN_SMEM] + [IN_VMEM] * 6 + [IN_HBM] + [IN_VMEM] * len(more),
        out_specs=[IN_VMEM] * 3,
        out_shape=[
            jax.ShapeDtypeStruct((half, width), BF16),
            jax.ShapeDtypeStruct((half, width), BF16),
            jax.ShapeDtypeStruct(shape, BF16 if last else F32),
        ],
        scratch_shapes=[
            pltpu.VMEM((full, width), BF16),
            pltpu.VMEM((columns, width), F32),
            pltpu.SemaphoreType.DMA((blocks,)),
        ],
        compiler_params=PARAMS,
        cost_estimate=SMALL,
    )(at, gq, gk, gv, cos, sin, w_t, n1, *more)


def body(
    tokens,
    cotangent,
    lengths,
    query_weight,
    key_weight,
    value_weight,
    output_weight,
    gate_weight,
    up_weight,
    down_weight,
    attention_gain,
    feed_gain,
):
    seqs, local, width = tokens.shape
    sp = lax.axis_size("sp")
    dp = lax.axis_size("dp")
    me = lax.axis_index("sp")
    full = local * sp
    heads = HEADS // sp
    own_rows = query_weight.shape[0]
    dp_rows = own_rows * sp
    q_cols = heads * HD
    order = order_of(sp)
    hidden = gate_weight.shape[1]

    positions = me * local + jnp.arange(local)
    valid = positions[None, :] < lengths[:, None]

    def pick(array, target):
        head = target * KV // sp
        return array[:, head * HD : (head + 1) * HD]

    extra = jnp.concatenate(
        [attention_gain[:, None], feed_gain[:, None], jnp.zeros((own_rows, 126), BF16)], axis=1
    )
    to_send = jnp.stack(
        [
            jnp.concatenate(
                [
                    query_weight[:, t * q_cols : (t + 1) * q_cols],
                    pick(key_weight, t),
                    pick(value_weight, t),
                    extra,
                ],
                axis=1,
            )
            for t in range(sp)
        ]
    )
    proj_cols = q_cols + 2 * HD
    in_block = lax.all_to_all(to_send, "sp", 0, 0, tiled=True).reshape(dp_rows, proj_cols + 128)
    total = dp * sp
    there = [(n, (n % dp) * sp + n // dp) for n in range(total)]
    back = [(b, a) for a, b in there]
    out_block = lax.ppermute(output_weight, ("dp", "sp"), there)
    out_cols = own_rows * width // dp_rows
    attn_mine = jnp.concatenate([in_block, out_block.reshape(dp_rows, out_cols)], axis=1)
    attn_all = row_major(lax.all_gather(row_major(attn_mine), "dp", axis=0, tiled=True))
    there_is = jnp.isfinite(in_block[0, 0].astype(F32))

    def later(array):
        return jnp.where(there_is, array, jnp.zeros_like(array))

    half = dp // 2
    gu_mine = interleave(gate_weight, up_weight)
    gu_w = row_major(lax.all_gather(row_major(gu_mine), "dp", axis=0, tiled=True))
    held = later(tokens)
    cot_local = jnp.where(valid[..., None], cotangent, jnp.zeros_like(cotangent))
    rows_far, cot_far = [], []
    chain = []
    for source, far in ((held, rows_far), (cot_local, cot_far)):
        for s in range(seqs):
            far.append(spread(after(source[s], *chain), sp, "sp", 2))
            chain = far[-1][1:]
    rows_all = [spread(far, sp) for far in rows_far]
    cot_parts = [spread(far, sp) for far in cot_far]
    down_a, _ = gather_bits(after(down_weight.T, attn_all)[None], dp, half, half)
    down_b, down_far = gather_bits(down_a, dp, half // 2, 2)
    down_c, down_near = gather_bits(down_b, dp, 1, 1)
    proj_t = attn_all[:, :proj_cols].T
    gains = attn_all[:, proj_cols : proj_cols + 2].astype(F32)
    gain_one, gain_two = gains[:, 0], gains[:, 1]
    out_w = attn_all[:, proj_cols + 128 :].reshape(q_cols, width)
    down_t = down_c.reshape(width, hidden)
    rows_all[0][0] = after(rows_all[0][0], *rows_far[-1])
    early = [[part for far in cot_far for part in far], []]

    row_pos = jnp.concatenate([(me ^ member) * local + jnp.arange(local) for member in order])
    frequency = jnp.power(10000.0, -2.0 * jnp.arange(HALF).astype(F32) / HD)
    angles = frequency[:, None] * row_pos.astype(F32)[None, :]
    cos, sin = jnp.cos(angles), jnp.sin(angles)
    at = jnp.stack([me ^ member for member in order]).astype(jnp.int32)

    def norm(values, gain):
        scale = lax.rsqrt(jnp.mean(values * values, axis=-1, keepdims=True) + EPS)
        return values * scale * gain

    def norm_back(grad, values, gain):
        scale = lax.rsqrt(jnp.mean(values * values, axis=-1, keepdims=True) + EPS)
        scaled = grad * gain
        return scale * scaled - values * scale**3 * jnp.mean(scaled * values, axis=-1, keepdims=True)

    normed_one, saved, branches, middles, normed_two, n2_far = [], [], [], [], [], []
    for s in range(seqs):
        length = lengths[s : s + 1]
        parts = list(rows_all[s])
        if s:
            parts[0] = after(parts[0], begun)
        n1, q, k_t, v_t, k, v = project(parts, at, gain_one[None], proj_t, cos, sin, heads)
        normed_one.append(n1)
        q = after(q, *cot_parts[s], *early[min(s, 1)], *branches)
        att, lse = attend_forward(q, k, v_t, length)
        if s:
            normed_two.append(spread([after(part, att) for part in n2_far[-1]], sp))
        flat = att.reshape(q_cols, full)
        flat = after(flat, *normed_two[-1], gu_w, down_near) if s else after(flat, down_far)
        begun = reduce_pair(*merge_heads(flat, at, out_w, sp), sp)
        branch = reduce_far(begun, sp)
        middle = tokens[s].astype(F32) + branch
        n2_far.append(spread(norm(middle, gain_two).astype(BF16), sp, "sp", 2))
        saved.append((q, k, k_t, v, att, lse))
        branches.append(branch)
        middles.append(middle)

    def mlp_near(hid, keep):
        return reduce_near(
            lambda lo, hi: dot((hid if lo else keep)[lo:hi], down_t, 1, 1), full, sp
        )

    begun_mixed = []
    hiddens, gu_grads, n2_grads, middle_grads, grad_rows, cot_all = [], [], [], [], [], []
    down_wgrad = 0.0
    for s in range(seqs):
        n2 = [after(part, begun) for part in normed_two[s]]
        made = feed(n2, cot_parts[s], gu_w, down_t)
        hid, gu_grad, normed_two[s], cot_all_s = made
        cot_all.append(cot_all_s)
        hiddens.append(hid)
        gu_grads.append(gu_grad)
        if s < seqs - 1:
            low, high = n2_far[s + 1][0], n2_far[s + 1]
            hid = after(hid, low)
            down_wgrad = row_major(dot(cot_all[s], hid, 0, 0))
            begun_mixed.append(mlp_near(hid, hid))
            high = high + [down_wgrad, begun_mixed[0]]
        else:
            low, high = n2_grads[0], [n2_grads[0]]
        send, keep = after(gu_grad, low), after(gu_grad, *high)
        begun = reduce_near(
            lambda lo, hi: dot((keep if lo == 0 else send)[lo:hi], gu_w, 1, 1), full, sp
        )
        n2_grads.append(reduce_far(begun, sp))
        if s < seqs - 1:
            normed_two.append(spread(n2_far[s + 1], sp))
    gu_wgrad = 0.0
    for s in range(seqs):
        held = after(n2_grads[s], gu_grads[-1]) if s == 0 else after(n2_grads[s], gu_wgrad)
        middle_grads.append(cot_local[s].astype(F32) + norm_back(held, middles[s], gain_two))
        parts = spread(middle_grads[s].astype(BF16), sp, "sp", 2)
        far_rows = parts[1:]
        if s == 0:
            gu_wgrad = dot(after(normed_two[0], begun, middle_grads[0]), gu_grads[0], 0, 0)
            parts = [after(part, gu_wgrad) for part in parts]
        grad_rows.append(spread(parts, sp))
        if s == 0:
            for t in range(1, seqs):
                gu_wgrad = gu_wgrad + dot(after(normed_two[t], *grad_rows[0]), gu_grads[t], 0, 0)
            gu_wgrad = gu_wgrad.astype(BF16)
    rows = after(cot_all[-1], middle_grads[-1])
    down_wgrad = down_wgrad + dot(rows, hiddens[-1], 0, 0)
    down_wgrad = down_wgrad.astype(BF16)
    hid = after(hiddens[-1], down_wgrad)
    begun_mixed.append(mlp_near(hid, after(hid, *far_rows)))

    feed_wgrad = jnp.concatenate([gu_wgrad, down_wgrad], axis=1)
    feed_grad = row_major(
        lax.psum_scatter(row_major(feed_wgrad), "dp", scatter_dimension=0, tiled=True)
    )

    def norm_sums(mixed):
        sums = jnp.stack(
            [
                jnp.stack(
                    [
                        jnp.sum(jnp.where(valid[s][:, None], member[s] * member[s], 0.0))
                        for s in range(seqs)
                    ]
                )
                for member in ([tokens[s].astype(F32) for s in range(seqs)], branches, mixed)
            ]
        )
        bit = 1
        while bit < sp:
            sums = sums + swap(sums, bit, sp)
            bit *= 2
        return sums

    proj_wgrad = None
    out_wgrad = None
    input_grads = []
    for s in range(seqs):
        q, k, k_t, v, att, lse = saved[s]
        rows = list(grad_rows[s])
        rows[0] = after(rows[0], mark) if s else after(rows[0], *far_rows, *begun_mixed)
        att_grad, delta, out_wgrad = split_heads(rows, at, out_w, att, out_wgrad)
        if s:
            q = after(q, begun)
            staying, got = halve(blocks_of(out_wgrad, dp), 1, dp)
        gq, gk, gv = attend_backward(q, att_grad, k, k_t, v, lse, delta, lengths[s : s + 1])
        mark = gq
        if s == 0:
            mixed = [reduce_far(after(begun_mixed[0], att_grad), sp)]
            gq = after(gq, mixed[0])
            mixed += [reduce_far(after(begun_mixed[t], mark), sp) for t in range(1, seqs)]
        else:
            gq = after(gq, got, *mixed, n1_grad)
        keep, send, proj_wgrad = return_rows(
            gq, gk, gv, at, cos, sin, proj_t, normed_one[s], proj_wgrad, dp
        )
        begun = reduce_pair(keep, send, sp)
        if s == 0:
            n1_grad = reduce_far(begun, sp)
        else:
            out_grad = finish(join(staying, after(got, mark)).astype(BF16), 2, dp)
            sums = norm_sums(mixed)
            n1_grad = reduce_far(after(begun, sums), sp)
        rest = norm_back(n1_grad, tokens[s].astype(F32), gain_one)
        input_grads.append((middle_grads[s] + rest).astype(BF16))
    input_grad = jnp.stack(input_grads)
    feed_grad = after(feed_grad, n1_grad).astype(F32)
    gate_out, up_out = separate(feed_grad[:, : 2 * hidden])
    down_out = feed_grad[:, 2 * hidden :].T
    staying, got = halve(proj_wgrad, 1, dp)
    left = join(staying, after(got, begun)).astype(BF16)
    staying, got = halve(left, 2, dp)
    left = join(staying, after(got, n1_grad)).astype(BF16)
    proj_grad = finish(left, 4, dp)
    out_grad = lax.ppermute(out_grad.astype(BF16), ("dp", "sp"), back).astype(F32)

    block_out = jnp.stack(
        [((middles[s] + mixed[s]) * valid[s][:, None]).astype(BF16) for s in range(seqs)]
    )
    proj_grad = proj_grad.astype(BF16).reshape(proj_cols, sp, own_rows).transpose(1, 0, 2)
    proj_grad = lax.all_to_all(proj_grad, "sp", 0, 0, tiled=True).astype(F32)
    query_grad = proj_grad[:, :q_cols].transpose(2, 0, 1).reshape(own_rows, HEADS * HD)

    def kv_grad(array):
        copies = array.reshape(KV, sp // KV, HD, own_rows).sum(axis=1)
        return copies.transpose(2, 0, 1).reshape(own_rows, KV * HD)

    key_grad = kv_grad(proj_grad[:, q_cols : q_cols + HD])
    value_grad = kv_grad(proj_grad[:, q_cols + HD :])

    def rowwise(weight, grad):
        return jnp.sum(weight.astype(F32) * grad, axis=1)

    gain_one_grad = (
        rowwise(query_weight, query_grad)
        + rowwise(key_weight, key_grad)
        + rowwise(value_weight, value_grad)
    ) / attention_gain.astype(F32)
    shares = rowwise(gate_weight, gate_out) + rowwise(up_weight, up_out)
    gain_two_grad = finish(blocks_of(shares, sp), 1, sp, "sp") / feed_gain.astype(F32)

    branch_norms = jnp.sqrt(sums / (lengths.astype(F32) * width))
    return (
        block_out,
        input_grad,
        query_grad,
        key_grad,
        value_grad,
        out_grad,
        gate_out,
        up_out,
        down_out,
        gain_one_grad,
        gain_two_grad,
        branch_norms,
    )


def solution(mesh):
    rows = P(("dp", "sp"), None)
    gain = P(("dp", "sp"))
    seq = P("dp", "sp", None)
    in_specs = (
        seq, seq, P("dp"), rows, rows, rows, rows,
        P("dp", "sp"), P("dp", "sp"), P("sp", "dp"), gain, gain,
    )
    out_specs = (
        seq, seq, rows, rows, rows, rows,
        P("dp", "sp"), P("dp", "sp"), P("sp", "dp"), gain, gain, P(None, "dp"),
    )
    return jax.shard_map(body, mesh=mesh, in_specs=in_specs, out_specs=out_specs, check_vma=False)
```

time: 2670 us -> 1170 us (0.44)
  matrix products: 877 us -> 171 us
  waiting for transfers between devices: 909 us -> 410 us
  Pallas kernels: 0 us -> 306 us
  blocking collectives: 234 us -> 0 us
  other arithmetic: 315 us -> 101 us
  local copies, waits for them, and re-layouts: 282 us -> 108 us
    dot_general x63 -> x12, matrix products: 877 us -> 171 us  [dot(): lax.dot_general(left, right, (((left_dim,), (right_dim,)), ((), ())), pre...]
    all_gather x9 -> x2, waiting for transfers between devices: 430 us -> 0.01 us  [the longest x1 0.01 us: body(): lax.all_gather(row_major(attn_mine), 'dp', axis=0, tiled=True)]
    reduce_scatter x9 -> x1, waiting for transfers between devices: 415 us -> 0.01 us  [body(): lax.psum_scatter(row_major(feed_wgrad), 'dp', scatter_dimension=0, tiled=...]
    ppermute x0 -> x55, waiting for transfers between devices: none -> 400 us  [the longest x53 400 us: swap(): return lax.ppermute(values, axis, [(i, i ^ bit) for i in range(count)])]
    pallas_call x0 -> x14, Pallas kernels: none -> 306 us  [the longest x2 75.3 us: feed(): pl.pallas_call(functools.partial(feed_kernel, last, blocks), grid=(len(pi...]
    convert_element_type x19 -> x17, other arithmetic: 157 us -> 16.6 us  [the longest x2 7.15 us: body(): parts = spread(middle_grads[s].astype(BF16), sp, 'sp', 2)]
    all_to_all x3 -> x0, blocking collectives: 139 us -> none  [the longest x1 49.4 us: body(): lax.all_to_all(jnp.stack(query_grads), 'sp', split_axis=1, concat_axis=2,...]
    unnamed x2 -> x0, blocking collectives: 86 us -> none
  transfers between devices with their start and end apart: 23 -> 60, of which waited for: 14 -> 26; matrix products, arithmetic and copies ran while one was open for 52% -> 24% of each run, Pallas kernels for 0% -> 26%
where the time goes in v1:
time: 1170 us; the launch traced here: 1160 us
  waiting for transfers between devices  410 us (35%)
  Pallas kernels  306 us (26%)
  matrix products  171 us (15%)
  local copies, waits for them, and re-layouts  108 us (9%)
  other arithmetic  101 us (9%)
  starting transfers between devices  47.4 us (4%)
  between operations  16.5 us (1%)
    ppermute x53, waiting for transfers between devices, swap(): return lax.ppermute(values, axis, [(i, i ^ bit) for i in range(count)])  400 us
    dot_general x12, matrix products, dot(): lax.dot_general(left, right, (((left_dim,), (right_dim,)), ((), ())), pre...  171 us
    pallas_call x2, Pallas kernels, feed(): pl.pallas_call(functools.partial(feed_kernel, last, blocks), grid=(len(pi...  75.3 us
    pallas_call x2, Pallas kernels, attend_backward(): pl.pallas_call(functools.partial(backward_kernel, block), grid=(heads,),...  70.3 us
    unnamed x245, local copies, waits for them, and re-layouts  61.6 us
    pallas_call x2, Pallas kernels, attend_forward(): pl.pallas_call(functools.partial(forward_kernel, block), grid=(heads,), i...  50.9 us
    ppermute x53, starting transfers between devices, swap(): return lax.ppermute(values, axis, [(i, i ^ bit) for i in range(count)])  37.1 us
    pallas_call x2, Pallas kernels, return_rows(): pl.pallas_call(functools.partial(return_kernel, blocks, last), in_specs=[...  35.7 us
  transfers between devices with their start and end apart: 60, of which 26 were waited for; matrix products, arithmetic and copies ran while one was open for 24% of the time, Pallas kernels for 26%

profile of v1, /device:TPU:0, one launch (start us, length us, event | category | flops | bytes accessed | tf_op | source)
XLA Modules:
  0.0 1160.3 jit_solution(13556228294125828551)
XLA Ops:
  11.9 4.2 all-to-all-start
  17.7 5.9 all-to-all-done
  47.8 13.8 %collective-permute-start = (bf16[384,2048]{1,0:T(8,128)(2,1)}, bf16[384,2048]{1,0:T(8,128)(2,1)}, u32[]{:S(2)}, u32[]{:S(2)}) collective-permute-start(bf16[384,2048]{1,0:T(8,128)(2,1)} %get-tuple-element.104.refs_0_), channel_id=1, source_target_pairs={{0,2},{1,3},{2,0},{3,1},{4,6},{5,7},{6,4},{7,5},{8,10},{9,11},{10,... | collective-permute-start | bytes 4718600 | tf_op jit(solution)/shard_map/ppermute | solution.py:29
  61.6 34.5 %collective-permute-done.refs_1_ = bf16[384,2048]{1,0:T(8,128)(2,1)} collective-permute-done((bf16[384,2048]{1,0:T(8,128)(2,1)}, bf16[384,2048]{1,0:T(8,128)(2,1)}, u32[]{:S(2)}, u32[]{:S(2)}) %collective-permute-start) | collective-permute-done | bytes 1572896 | tf_op jit(solution)/shard_map/ppermute | solution.py:29
  103.5 30.7 %collective-permute-done.1.refs_1_ = bf16[384,2048]{1,0:T(8,128)(2,1)} collective-permute-done((bf16[384,2048]{1,0:T(8,128)(2,1)}, bf16[384,2048]{1,0:T(8,128)(2,1)}, u32[]{:S(2)}, u32[]{:S(2)}) %collective-permute-start.1) | collective-permute-done | bytes 1572896 | tf_op jit(solution)/shard_map/ppermute | solution.py:29
  139.5 31.4 %collective-permute-done.5.refs_5_ = bf16[384,2048]{1,0:T(8,128)(2,1)} collective-permute-done((bf16[384,2048]{1,0:T(8,128)(2,1)}, bf16[384,2048]{1,0:T(8,128)(2,1)}, u32[]{:S(2)}, u32[]{:S(2)}) %collective-permute-start.5) | collective-permute-done | bytes 1572896 | tf_op jit(solution)/shard_map/ppermute | solution.py:29
  172.4 39.3 %collective-permute-done.9 = bf16[1,256,1408]{2,1,0:T(8,128)(2,1)} collective-permute-done((bf16[1,256,1408]{2,1,0:T(8,128)(2,1)}, bf16[1,256,1408]{2,1,0:T(8,128)(2,1)}, u32[]{:S(2)}, u32[]{:S(2)}) %collective-permute-start.9) | collective-permute-done | bytes 720928 | tf_op jit(solution)/shard_map/ppermute | solution.py:29
  220.5 4.6 reshape.267.w_ref.refs_4_
  225.0 3.7 slice.360
  228.8 4.5 copy.75
  235.8 12.9 %shard_map.211 = (bf16[1536,2048]{1,0:T(8,128)(2,1)}, bf16[8,64,1536]{2,1,0:T(8,128)(2,1)}, bf16[64,1536]{1,0:T(8,128)(2,1)}, bf16[64,1536]{1,0:T(8,128)(2,1)}, ...) custom-call(s32[4]{0:T(128)} %pad_add_fusion.at_ref, bf16[384,2048]{1,0:T(8,128)(2,1)} %get-tuple-element.104.refs_0_, ...), custom_call_target="tpu_custom_call" | custom-call | flops 1000000 | bytes 1000000 | tf_op jit(solution)/shard_map/pallas_call | solution.py:509
  252.2 25.5 %shard_map.212 = (bf16[8,64,1536]{2,1,0:T(8,128)(2,1)S(1)}, f32[8,1,1536]{2,1,0:T(1,128)S(1)}) custom-call(s32[1]{0:T(128)} %get-tuple-element.309.len_ref, bf16[8,64,1536]{2,1,0:T(8,128)(2,1)S(1)} %copy-done.8, bf16[1536,64]{1,0:T(8,128)(2,1)S(1)} %copy-done.12, bf16[64,1536]{1,0:T(8,128)(2,1)S(1)} %copy-done.20), custom_call_target="tpu_custom_call" | custom-call | flops 2415919104 | bytes 3145728 | tf_op jit(solution)/shard_map/pallas_call | solution.py:177
  278.9 42.9 %collective-permute-done.10 = bf16[2,256,1408]{2,1,0:T(8,128)(2,1)} collective-permute-done((bf16[2,256,1408]{2,1,0:T(8,128)(2,1)}, bf16[2,256,1408]{2,1,0:T(8,128)(2,1)}, u32[]{:S(2)}, u32[]{:S(2)}) %collective-permute-start.10) | collective-permute-done | bytes 1441824 | tf_op jit(solution)/shard_map/ppermute | solution.py:29
  321.8 7.2 shard_map.213
  329.0 5.9 collective-permute-done.11
  345.0 33.7 %collective-permute-done.12 = bf16[384,2048]{1,0:T(8,128)(2,1)} collective-permute-done((bf16[384,2048]{1,0:T(8,128)(2,1)}, bf16[384,2048]{1,0:T(8,128)(2,1)}, u32[]{:S(2)}, u32[]{:S(2)}) %collective-permute-start.12) | collective-permute-done | bytes 1572896 | tf_op jit(solution)/shard_map/ppermute | solution.py:29
  385.2 13.6 %shard_map.214 = (bf16[1536,2048]{1,0:T(8,128)(2,1)}, bf16[8,64,1536]{2,1,0:T(8,128)(2,1)}, bf16[64,1536]{1,0:T(8,128)(2,1)}, bf16[64,1536]{1,0:T(8,128)(2,1)}, ...) custom-call(s32[4]{0:T(128)} %pad_add_fusion.at_ref, bf16[384,2048]{1,0:T(8,128)(2,1)} %get-tuple-element.116.refs_0_, ...), custom_call_target="tpu_custom_call" | custom-call | flops 1000000 | bytes 1000000 | tf_op jit(solution)/shard_map/pallas_call | solution.py:509
  402.2 25.3 %shard_map.215 = (bf16[8,64,1536]{2,1,0:T(8,128)(2,1)S(1)}, f32[8,1,1536]{2,1,0:T(1,128)S(1)}) custom-call(s32[1]{0:T(128)} %get-tuple-element.310.len_ref, bf16[8,64,1536]{2,1,0:T(8,128)(2,1)S(1)} %copy-done.10, bf16[1536,64]{1,0:T(8,128)(2,1)S(1)} %copy-done.15, bf16[64,1536]{1,0:T(8,128)(2,1)S(1)} %copy-done.21), custom_call_target="tpu_custom_call" | custom-call | flops 2415919104 | bytes 3145728 | tf_op jit(solution)/shard_map/pallas_call | solution.py:177
  429.2 19.8 %collective-permute-done.20 = bf16[4,256,1408]{2,1,0:T(8,128)(2,1)} collective-permute-done((bf16[4,256,1408]{2,1,0:T(8,128)(2,1)S(1)}, bf16[4,256,1408]{2,1,0:T(8,128)(2,1)}, u32[]{:S(2)}, u32[]{:S(2)}) %collective-permute-start.20) | collective-permute-done | bytes 2883616 | tf_op jit(solution)/shard_map/ppermute | solution.py:29
  450.2 7.2 shard_map.216
  457.5 6.0 collective-permute-done.21
  463.5 4.2 convert_add_fusion.6
  477.9 37.7 %shard_map.217 = (bf16[1536,1408]{1,0:T(8,128)(2,1)}, bf16[1536,2816]{1,0:T(8,128)(2,1)}, bf16[1536,2048]{1,0:T(8,128)(2,1)}, bf16[1536,2048]{1,0:T(8,128)(2,1)}) custom-call(bf16[384,2048]{1,0:T(8,128)(2,1)} %copy-done.51, bf16[384,2048]{1,0:T(8,128)(2,1)} %collective-permute-done.17.refs_1_, bf16[384,2048]{1,0:T(8,128)(2,1)} %copy-done.69, ...), custom_call_target="tpu_custom_call" | custom-call | flops 4429185024 | bytes 12582912 | tf_op jit(solution)/shard_map/pallas_call | solution.py:386
  515.7 3.2 multiply_reduce_fusion.2
  523.1 6.5 convolution_convert_fusion.1
  529.7 14.4 %fusion.12 = bf16[768,2048]{1,0:T(8,128)(2,1)} fusion(bf16[2048,2816]{1,0:T(8,128)(2,1)} %all-gather.5.cloned.1.call-done.refs_8_, bf16[1536,2816]{1,0:T(8,128)(2,1)} %get-tuple-element.135), kind=kOutput, calls=%fused_computation.32 | convolution fusion | flops 8859942912 | bytes 19005440 | tf_op jit(solution)/shard_map/dot_general | solution.py:23
  544.5 15.9 %fusion.60 = f32[2048,1408]{1,0:T(8,128)} fusion(bf16[1536,2048]{1,0:T(8,128)(2,1)} %get-tuple-element.134, bf16[1536,1408]{1,0:T(8,128)(2,1)} %get-tuple-element.132), kind=kOutput, calls=%fused_computation.203 | convolution fusion | flops 8858370048 | bytes 22151168 | tf_op jit(solution)/shard_map/dot_general | solution.py:23
  560.5 9.0 convert_add_fusion.5
  569.5 13.7 %convert_add_fusion.4 = f32[768,2048]{1,0:T(8,128)S(1)} fusion(bf16[768,2048]{1,0:T(8,128)(2,1)} %collective-permute-done.25, bf16[2048,2816]{1,0:T(8,128)(2,1)} %all-gather.5.cloned.1.call-done.refs_8_, bf16[1536,2816]{1,0:T(8,128)(2,1)} %get-tuple-element.135), kind=kOutput, calls=%fused_computation.7 | convolution fusion | flops 8861515776 | bytes 25296896 | tf_op jit(solution)/shard_map/dot_general | solution.py:23
  591.2 37.6 %shard_map.218 = (bf16[1536,1408]{1,0:T(8,128)(2,1)}, bf16[1536,2816]{1,0:T(8,128)(2,1)}, bf16[1536,2048]{1,0:T(8,128)(2,1)}, bf16[1536,2048]{1,0:T(8,128)(2,1)}) custom-call(bf16[384,2048]{1,0:T(8,128)(2,1)} %copy-done.52, bf16[384,2048]{1,0:T(8,128)(2,1)} %copy-done.71, bf16[384,2048]{1,0:T(8,128)(2,1)} %copy-done.70, bf16[384,2048]{1,0:T(8,128)(2,1)} %copy-done.72, ...), custom_call_target="tpu_custom_call" | custom-call | flops 4429185024 | bytes 12582912 | tf_op jit(solution)/shard_map/pallas_call | solution.py:386
  631.7 15.5 %fusion.15 = bf16[768,2048]{1,0:T(8,128)(2,1)} fusion(bf16[2048,2816]{1,0:T(8,128)(2,1)} %all-gather.5.cloned.1.call-done.refs_8_, bf16[1536,2816]{1,0:T(8,128)(2,1)} %get-tuple-element.144), kind=kOutput, calls=%fused_computation.33 | convolution fusion | flops 8859942912 | bytes 19005440 | tf_op jit(solution)/shard_map/dot_general | solution.py:23
  647.3 6.8 fusion.9
  654.2 4.4 fusion.55
  659.2 13.2 %convert_add_fusion.3 = f32[768,2048]{1,0:T(8,128)} fusion(bf16[768,2048]{1,0:T(8,128)(2,1)} %collective-permute-done.29, bf16[2048,2816]{1,0:T(8,128)(2,1)S(1)} %bitcast.184, bf16[1536,2816]{1,0:T(8,128)(2,1)} %get-tuple-element.144), kind=kOutput, calls=%fused_computation.6 | convolution fusion | flops 8861515776 | bytes 25296896 | tf_op jit(solution)/shard_map/dot_general | solution.py:23
  672.4 25.8 %fusion.61 = f32[2048,2816]{1,0:T(8,128)} fusion(bf16[1536,2048]{1,0:T(8,128)(2,1)} %get-tuple-element.145, bf16[1536,2816]{1,0:T(8,128)(2,1)} %get-tuple-element.135), kind=kOutput, calls=%fused_computation.204 | convolution fusion | flops 17716740096 | bytes 38010880 | tf_op jit(solution)/shard_map/dot_general | solution.py:23
  705.3 24.5 %add_convert_fusion = bf16[2048,2816]{1,0:T(8,128)(2,1)S(1)} fusion(f32[2048,2816]{1,0:T(8,128)} %fusion.61, bf16[1536,2048]{1,0:T(8,128)(2,1)} %get-tuple-element.149, bf16[1536,2816]{1,0:T(8,128)(2,1)} %get-tuple-element.144), kind=kOutput, calls=%fused_computation | convolution fusion | flops 17728274432 | bytes 49545216 | tf_op jit(solution)/shard_map/dot_general | solution.py:23
  729.8 7.2 collective-permute-done.30
  743.5 15.7 %add_convert_fusion.1 = bf16[2048,1408]{1,0:T(8,128)(2,1)S(1)} fusion(f32[2048,1408]{1,0:T(8,128)} %fusion.60, bf16[1536,2048]{1,0:T(8,128)(2,1)} %get-tuple-element.153, bf16[1536,1408]{1,0:T(8,128)(2,1)} %get-tuple-element.155), kind=kOutput, calls=%fused_computation.2 | convolution fusion | flops 8864137216 | bytes 27918336 | tf_op jit(solution)/shard_map/dot_general | solution.py:23
  759.2 6.8 pad_maximum_fusion
  766.1 7.9 convolution_convert_fusion
  775.6 35.3 %collective-permute-done.34.refs_1_ = bf16[384,2048]{1,0:T(8,128)(2,1)S(1)} collective-permute-done((bf16[384,2048]{1,0:T(8,128)(2,1)S(1)}, bf16[384,2048]{1,0:T(8,128)(2,1)S(1)}, u32[]{:S(2)}, u32[]{:S(2)}) %collective-permute-start.34) | collective-permute-done | bytes 1572896 | tf_op jit(solution)/shard_map/ppermute | solution.py:29
  812.1 8.8 convert_add_fusion.2
  820.9 15.2 %shard_map.219 = (bf16[8,64,1536]{2,1,0:T(8,128)(2,1)}, f32[8,1,1536]{2,1,0:T(1,128)}, f32[512,2048]{1,0:T(8,128)}) custom-call(s32[4]{0:T(128)} %pad_add_fusion.at_ref, bf16[384,2048]{1,0:T(8,128)(2,1)} %get-tuple-element.156.refs_0_, bf16[384,2048]{1,0:T(8,128)(2,1)} %collective-permute-done.31.refs_1_, bf16[384,2048]{1,0:T(8,128)(2,1)} %copy-done.73, ...), custom_call_target="tpu_custom_call" | custom-call | flops 1000000 | bytes 1000000 | tf_op jit(solution)/shard_map/pallas_call | solution.py:602
  839.9 35.5 %shard_map.220 = (bf16[8,64,1536]{2,1,0:T(8,128)(2,1)S(1)}, f32[1536,64]{1,0:T(8,128)S(1)}, f32[1536,64]{1,0:T(8,128)S(1)}) custom-call(s32[1]{0:T(128)} %get-tuple-element.309.len_ref, bf16[8,64,1536]{2,1,0:T(8,128)(2,1)S(1)} %copy-done.9, bf16[8,64,1536]{2,1,0:T(8,128)(2,1)} %get-tuple-element.157.grad_ref, bf16[1536,64]{1,0:T(8,128)(2,1)S(1)} %copy-done.13, ...), custom_call_target="tpu_custom_call" | custom-call | flops 4831838208 | bytes 4718592 | tf_op jit(solution)/shard_map/pallas_call | solution.py:248
  875.5 5.5 select_reduce_fusion.1
  881.0 17.5 %shard_map.221 = (bf16[768,2048]{1,0:T(8,128)(2,1)}, bf16[768,2048]{1,0:T(8,128)(2,1)}, f32[640,2048]{1,0:T(8,128)}) custom-call(s32[4]{0:T(128)} %pad_add_fusion.at_ref, bf16[8,64,1536]{2,1,0:T(8,128)(2,1)} %copy-done.3, f32[1536,64]{1,0:T(8,128)} %copy-done.6, f32[1536,64]{1,0:T(8,128)} %copy-done.7, f32[32,1536]{1,0:T(8,128)} %get-tuple-element.298.refs_6_.refs_3_, ...), custom_call_target="tpu_custom_call" | custom-call | flops 1000000 | bytes 1000000 | tf_op jit(solution)/shard_map/pallas_call | solution.py:688
  899.2 3.6 slice.505
  903.1 5.0 collective-permute-done.38
  913.9 17.2 %shard_map.222 = (bf16[8,64,1536]{2,1,0:T(8,128)(2,1)}, f32[8,1,1536]{2,1,0:T(1,128)}, bf16[512,2048]{1,0:T(8,128)(2,1)}) custom-call(s32[4]{0:T(128)} %pad_add_fusion.at_ref, bf16[384,2048]{1,0:T(8,128)(2,1)} %copy-done.56, bf16[384,2048]{1,0:T(8,128)(2,1)} %copy-done.75, bf16[384,2048]{1,0:T(8,128)(2,1)} %collective-permute-done.40.refs_2_, ...), custom_call_target="tpu_custom_call" | custom-call | flops 1000000 | bytes 1000000 | tf_op jit(solution)/shard_map/pallas_call | solution.py:602
  934.0 6.4 collective-permute-done.37
  940.5 4.5 select_reduce_fusion
  945.0 34.7 %shard_map.223 = (bf16[8,64,1536]{2,1,0:T(8,128)(2,1)S(1)}, f32[1536,64]{1,0:T(8,128)S(1)}, f32[1536,64]{1,0:T(8,128)S(1)}) custom-call(s32[1]{0:T(128)} %get-tuple-element.310.len_ref, bf16[8,64,1536]{2,1,0:T(8,128)(2,1)S(1)} %copy-done.11, bf16[8,64,1536]{2,1,0:T(8,128)(2,1)} %get-tuple-element.174.grad_ref, bf16[1536,64]{1,0:T(8,128)(2,1)S(1)} %copy-done.16, ...), custom_call_target="tpu_custom_call" | custom-call | flops 4831838208 | bytes 4718592 | tf_op jit(solution)/shard_map/pallas_call | solution.py:248
  979.8 4.6 slice_add_fusion
  984.4 18.2 %shard_map.224 = (bf16[768,2048]{1,0:T(8,128)(2,1)}, bf16[768,2048]{1,0:T(8,128)(2,1)}, bf16[8,640,256]{2,1,0:T(8,128)(2,1)}) custom-call(s32[4]{0:T(128)} %pad_add_fusion.at_ref, bf16[8,64,1536]{2,1,0:T(8,128)(2,1)} %copy-done.2, f32[1536,64]{1,0:T(8,128)} %copy-done.4, f32[1536,64]{1,0:T(8,128)} %copy-done.5, ...), custom_call_target="tpu_custom_call" | custom-call | flops 1000000 | bytes 1000000 | tf_op jit(solution)/shard_map/pallas_call | solution.py:688
  1010.7 3.3 collective-permute-done.45
  1014.1 36.4 %collective-permute-done.50 = bf16[2,64,2048]{2,1,0:T(8,128)(2,1)S(1)} collective-permute-done((bf16[2,64,2048]{2,1,0:T(8,128)(2,1)S(1)}, bf16[2,64,2048]{2,1,0:T(8,128)(2,1)S(1)}, u32[]{:S(2)}, u32[]{:S(2)}) %collective-permute-start.50) | collective-permute-done | bytes 524320 | tf_op jit(solution)/shard_map/ppermute | solution.py:29
  1053.9 27.8 %collective-permute-done.51 = bf16[1,64,2048]{2,1,0:T(8,128)(2,1)S(1)} collective-permute-done((bf16[1,64,2048]{2,1,0:T(8,128)(2,1)S(1)}, bf16[1,64,2048]{2,1,0:T(8,128)(2,1)S(1)}, u32[]{:S(2)}, u32[]{:S(2)}) %collective-permute-start.51) | collective-permute-done | bytes 262176 | tf_op jit(solution)/shard_map/ppermute | solution.py:29
  1090.2 3.5 collective-permute-done.46
  1093.7 4.6 fusion.28
  1098.3 15.2 %collective-permute-done.48 = bf16[2,640,256]{2,1,0:T(8,128)(2,1)} collective-permute-done((bf16[2,640,256]{2,1,0:T(8,128)(2,1)}, bf16[2,640,256]{2,1,0:T(8,128)(2,1)}, u32[]{:S(2)}, u32[]{:S(2)}) %collective-permute-start.48) | collective-permute-done | bytes 655392 | tf_op jit(solution)/shard_map/ppermute | solution.py:29
  1115.0 3.2 fusion.46
  1120.1 11.0 collective-permute-done.49
  1132.2 3.5 all-to-all-start.1
  1137.6 4.7 all-to-all-done.1
  (458 shorter events, 175.6 us)
Async XLA Ops:
  11.9 11.7 %all-to-all-start = ((bf16[4,64,768]{2,1,0:T(8,128)(2,1)}), bf16[4,64,768]{2,1,0:T(8,128)(2,1)S(1)}, u32[]{:S(2)}, u32[]{:S(2)}) async-start(bf16[4,64,768]{2,1,0:T(8,128)(2,1)} %pad_maximum_fusion.6), calls=%async_computation | async-start | bytes 786432 | tf_op jit(solution)/shard_map/all_to_all | solution.py:758
  16.1 122.1 %all-gather.3.cloned.1.call-start = ((), (), s32[]{:S(2)}) async-start(), calls=%async_computation.3 | async-start | bytes 5898240 | tf_op jit(solution)/shard_map/all_gather | solution.py:765
  16.1 0.7 collective-permute-start.4
  25.5 424.7 %all-gather.5.cloned.1.call-start = ((), (), s32[]{:S(2)}) async-start(), calls=%async_computation.4 | async-start | bytes 12976128 | tf_op jit(solution)/shard_map/all_gather | solution.py:773
  44.2 1099.2 %reduce-scatter.2.cloned.1.call-start = ((), (), s32[]{:S(2)}) async-start(), calls=%async_computation.5 | async-start | bytes 19464192 | tf_op jit(solution)/shard_map/reduce_scatter | solution.py:884
  45.7 52.9 %copy-start.95 = (s32[2]{0:T(128)S(1)}, s32[2]{0:T(128)}, u32[]{:S(2)}) copy-start(s32[2]{0:T(128)} %param.14) | copy-start | bytes 28
  47.8 48.3 %collective-permute-start = (bf16[384,2048]{1,0:T(8,128)(2,1)}, bf16[384,2048]{1,0:T(8,128)(2,1)}, u32[]{:S(2)}, u32[]{:S(2)}) collective-permute-start(bf16[384,2048]{1,0:T(8,128)(2,1)} %get-tuple-element.104.refs_0_), channel_id=1, source_target_pairs={{0,2},{1,3},{2,0},{3,1},{4,6},{5,7},{6,4},{7,5},{8,10},{9,11},{10,... | collective-permute-start | bytes 4718600 | tf_op jit(solution)/shard_map/ppermute | solution.py:29
  96.1 38.0 %collective-permute-start.1 = (bf16[384,2048]{1,0:T(8,128)(2,1)}, bf16[384,2048]{1,0:T(8,128)(2,1)}, u32[]{:S(2)}, u32[]{:S(2)}) collective-permute-start(bf16[384,2048]{1,0:T(8,128)(2,1)} %get-tuple-element.116.refs_0_), channel_id=1, source_target_pairs={{0,2},{1,3},{2,0},{3,1},{4,6},{5,7},{6,4},{7,5},{8,10},{9,11},{10,... | collective-permute-start | bytes 4718600 | tf_op jit(solution)/shard_map/ppermute | solution.py:29
  134.1 36.7 %collective-permute-start.5 = (bf16[384,2048]{1,0:T(8,128)(2,1)}, bf16[384,2048]{1,0:T(8,128)(2,1)}, u32[]{:S(2)}, u32[]{:S(2)}) collective-permute-start(bf16[384,2048]{1,0:T(8,128)(2,1)} %get-tuple-element.106.refs_4_), channel_id=1, source_target_pairs={{0,2},{1,3},{2,0},{3,1},{4,6},{5,7},{6,4},{7,5},{8,10},{9,11},{10,... | collective-permute-start | bytes 4718600 | tf_op jit(solution)/shard_map/ppermute | solution.py:29
  135.9 79.4 %collective-permute-start.2 = (bf16[384,2048]{1,0:T(8,128)(2,1)}, bf16[384,2048]{1,0:T(8,128)(2,1)}, u32[]{:S(2)}, u32[]{:S(2)}) collective-permute-start(bf16[384,2048]{1,0:T(8,128)(2,1)} %get-tuple-element.104.refs_0_), channel_id=1, source_target_pairs={{0,1},{1,0},{2,3},{3,2},{4,5},{5,4},{6,7},{7,6},{8,9},{9,8},{10,11... | collective-permute-start | bytes 4718600 | tf_op jit(solution)/shard_map/ppermute | solution.py:29
  138.1 73.6 %collective-permute-start.9 = (bf16[1,256,1408]{2,1,0:T(8,128)(2,1)}, bf16[1,256,1408]{2,1,0:T(8,128)(2,1)}, u32[]{:S(2)}, u32[]{:S(2)}) collective-permute-start(bf16[1,256,1408]{2,1,0:T(8,128)(2,1)} %bitcast.196), channel_id=1, source_target_pairs={{0,16},{4,20},{8,24},{12,28},{16,0},{20,4},{24,8},{28,12},{1,17},{... | collective-permute-start | bytes 2162696 | tf_op jit(solution)/shard_map/ppermute | solution.py:29
  138.8 97.0 %collective-permute-start.3 = (bf16[384,2048]{1,0:T(8,128)(2,1)}, bf16[384,2048]{1,0:T(8,128)(2,1)}, u32[]{:S(2)}, u32[]{:S(2)}) collective-permute-start(bf16[384,2048]{1,0:T(8,128)(2,1)} %collective-permute-done.refs_1_), channel_id=1, source_target_pairs={{0,1},{1,0},{2,3},{3,2},{4,5},{5,4},{6,7},{7,6},{8,9},{9,8},{10,11... | collective-permute-start | bytes 4718600 | tf_op jit(solution)/shard_map/ppermute | solution.py:29
  139.4 109.4 %collective-permute-start.6 = (bf16[384,2048]{1,0:T(8,128)(2,1)}, bf16[384,2048]{1,0:T(8,128)(2,1)}, u32[]{:S(2)}, u32[]{:S(2)}) collective-permute-start(bf16[384,2048]{1,0:T(8,128)(2,1)} %get-tuple-element.106.refs_4_), channel_id=1, source_target_pairs={{0,1},{1,0},{2,3},{3,2},{4,5},{5,4},{6,7},{7,6},{8,9},{9,8},{10,11... | collective-permute-start | bytes 4718600 | tf_op jit(solution)/shard_map/ppermute | solution.py:29
  170.9 78.0 %collective-permute-start.8 = (bf16[384,2048]{1,0:T(8,128)(2,1)}, bf16[384,2048]{1,0:T(8,128)(2,1)}, u32[]{:S(2)}, u32[]{:S(2)}) collective-permute-start(bf16[384,2048]{1,0:T(8,128)(2,1)} %get-tuple-element.107.refs_4_), channel_id=1, source_target_pairs={{0,2},{1,3},{2,0},{3,1},{4,6},{5,7},{6,4},{7,5},{8,10},{9,11},{10,... | collective-permute-start | bytes 4718600 | tf_op jit(solution)/shard_map/ppermute | solution.py:29
  211.7 37.1 %collective-permute-start.7 = (bf16[384,2048]{1,0:T(8,128)(2,1)}, bf16[384,2048]{1,0:T(8,128)(2,1)}, u32[]{:S(2)}, u32[]{:S(2)}) collective-permute-start(bf16[384,2048]{1,0:T(8,128)(2,1)} %collective-permute-done.5.refs_5_), channel_id=1, source_target_pairs={{0,1},{1,0},{2,3},{3,2},{4,5},{5,4},{6,7},{7,6},{8,9},{9,8},{10,11... | collective-permute-start | bytes 4718600 | tf_op jit(solution)/shard_map/ppermute | solution.py:29
  215.3 106.5 %collective-permute-start.10 = (bf16[2,256,1408]{2,1,0:T(8,128)(2,1)}, bf16[2,256,1408]{2,1,0:T(8,128)(2,1)}, u32[]{:S(2)}, u32[]{:S(2)}) collective-permute-start(bf16[2,256,1408]{2,1,0:T(8,128)(2,1)} %maximum_bitcast_fusion), channel_id=1, source_target_pairs={{0,8},{4,12},{8,0},{12,4},{16,24},{20,28},{24,16},{28,20},{1,9},{5... | collective-permute-start | bytes 4325384 | tf_op jit(solution)/shard_map/ppermute | solution.py:29
  329.0 5.9 collective-permute-start.11
  341.9 36.8 %collective-permute-start.12 = (bf16[384,2048]{1,0:T(8,128)(2,1)}, bf16[384,2048]{1,0:T(8,128)(2,1)}, u32[]{:S(2)}, u32[]{:S(2)}) collective-permute-start(bf16[384,2048]{1,0:T(8,128)(2,1)} %slice.510), channel_id=1, source_target_pairs={{0,2},{1,3},{2,0},{3,1},{4,6},{5,7},{6,4},{7,5},{8,10},{9,11},{10,... | collective-permute-start | bytes 4718600 | tf_op jit(solution)/shard_map/ppermute | solution.py:29
  341.9 42.1 %collective-permute-start.13 = (bf16[384,2048]{1,0:T(8,128)(2,1)}, bf16[384,2048]{1,0:T(8,128)(2,1)S(1)}, u32[]{:S(2)}, u32[]{:S(2)}) collective-permute-start(bf16[384,2048]{1,0:T(8,128)(2,1)} %get-tuple-element.116.refs_0_), channel_id=1, source_target_pairs={{0,1},{1,0},{2,3},{3,2},{4,5},{5,4},{6,7},{7,6},{8,9},{9,8},{10,11... | collective-permute-start | bytes 4718600 | tf_op jit(solution)/shard_map/ppermute | solution.py:29
  342.1 43.2 %collective-permute-start.14 = (bf16[384,2048]{1,0:T(8,128)(2,1)}, bf16[384,2048]{1,0:T(8,128)(2,1)}, u32[]{:S(2)}, u32[]{:S(2)}) collective-permute-start(bf16[384,2048]{1,0:T(8,128)(2,1)} %collective-permute-done.1.refs_1_), channel_id=1, source_target_pairs={{0,1},{1,0},{2,3},{3,2},{4,5},{5,4},{6,7},{7,6},{8,9},{9,8},{10,11... | collective-permute-start | bytes 4718600 | tf_op jit(solution)/shard_map/ppermute | solution.py:29
  342.5 56.4 %collective-permute-start.15 = (bf16[384,2048]{1,0:T(8,128)(2,1)}, bf16[384,2048]{1,0:T(8,128)(2,1)}, u32[]{:S(2)}, u32[]{:S(2)}) collective-permute-start(bf16[384,2048]{1,0:T(8,128)(2,1)} %get-tuple-element.107.refs_4_), channel_id=1, source_target_pairs={{0,1},{1,0},{2,3},{3,2},{4,5},{5,4},{6,7},{7,6},{8,9},{9,8},{10,11... | collective-permute-start | bytes 4718600 | tf_op jit(solution)/shard_map/ppermute | solution.py:29
  342.6 56.3 %collective-permute-start.16 = (bf16[384,2048]{1,0:T(8,128)(2,1)}, bf16[384,2048]{1,0:T(8,128)(2,1)}, u32[]{:S(2)}, u32[]{:S(2)}) collective-permute-start(bf16[384,2048]{1,0:T(8,128)(2,1)} %collective-permute-done.8.refs_5_), channel_id=1, source_target_pairs={{0,1},{1,0},{2,3},{3,2},{4,5},{5,4},{6,7},{7,6},{8,9},{9,8},{10,11... | collective-permute-start | bytes 4718600 | tf_op jit(solution)/shard_map/ppermute | solution.py:29
  383.4 45.3 %collective-permute-start.17 = (bf16[384,2048]{1,0:T(8,128)(2,1)S(1)}, bf16[384,2048]{1,0:T(8,128)(2,1)}, u32[]{:S(2)}, u32[]{:S(2)}) collective-permute-start(bf16[384,2048]{1,0:T(8,128)(2,1)S(1)} %multiply_convert_fusion.3.refs_0_), channel_id=1, source_target_pairs={{0,2},{1,3},{2,0},{3,1},{4,6},{5,7},{6,4},{7,5},{8,10},{9,11},{10,... | collective-permute-start | bytes 4718600 | tf_op jit(solution)/shard_map/ppermute | solution.py:29
  385.2 63.8 %collective-permute-start.20 = (bf16[4,256,1408]{2,1,0:T(8,128)(2,1)S(1)}, bf16[4,256,1408]{2,1,0:T(8,128)(2,1)}, u32[]{:S(2)}, u32[]{:S(2)}) collective-permute-start(bf16[4,256,1408]{2,1,0:T(8,128)(2,1)S(1)} %bitcast.187), channel_id=1, source_target_pairs={{0,4},{4,0},{8,12},{12,8},{16,20},{20,16},{24,28},{28,24},{1,5},{5... | collective-permute-start | bytes 8650760 | tf_op jit(solution)/shard_map/ppermute | solution.py:29
  428.7 20.3 %collective-permute-start.18 = (bf16[384,2048]{1,0:T(8,128)(2,1)S(1)}, bf16[384,2048]{1,0:T(8,128)(2,1)S(1)}, u32[]{:S(2)}, u32[]{:S(2)}) collective-permute-start(bf16[384,2048]{1,0:T(8,128)(2,1)S(1)} %multiply_convert_fusion.3.refs_0_), channel_id=1, source_target_pairs={{0,1},{1,0},{2,3},{3,2},{4,5},{5,4},{6,7},{7,6},{8,9},{9,8},{10,11... | collective-permute-start | bytes 4718600 | tf_op jit(solution)/shard_map/ppermute | solution.py:29
  428.7 21.5 %collective-permute-start.19 = (bf16[384,2048]{1,0:T(8,128)(2,1)}, bf16[384,2048]{1,0:T(8,128)(2,1)}, u32[]{:S(2)}, u32[]{:S(2)}) collective-permute-start(bf16[384,2048]{1,0:T(8,128)(2,1)} %collective-permute-done.17.refs_1_), channel_id=1, source_target_pairs={{0,1},{1,0},{2,3},{3,2},{4,5},{5,4},{6,7},{7,6},{8,9},{9,8},{10,11... | collective-permute-start | bytes 4718600 | tf_op jit(solution)/shard_map/ppermute | solution.py:29
  457.5 6.0 collective-permute-start.21
  470.5 45.2 %collective-permute-start.22 = (bf16[384,2048]{1,0:T(8,128)(2,1)S(1)}, bf16[384,2048]{1,0:T(8,128)(2,1)S(1)}, u32[]{:S(2)}, u32[]{:S(2)}) collective-permute-start(bf16[384,2048]{1,0:T(8,128)(2,1)S(1)} %slice.509), channel_id=1, source_target_pairs={{0,2},{1,3},{2,0},{3,1},{4,6},{5,7},{6,4},{7,5},{8,10},{9,11},{10,... | collective-permute-start | bytes 4718600 | tf_op jit(solution)/shard_map/ppermute | solution.py:29
  520.9 69.1 %collective-permute-start.27 = (bf16[384,2048]{1,0:T(8,128)(2,1)S(1)}, bf16[384,2048]{1,0:T(8,128)(2,1)S(1)}, u32[]{:S(2)}, u32[]{:S(2)}) collective-permute-start(bf16[384,2048]{1,0:T(8,128)(2,1)S(1)} %multiply_convert_fusion.2.refs_0_), channel_id=1, source_target_pairs={{0,1},{1,0},{2,3},{3,2},{4,5},{5,4},{6,7},{7,6},{8,9},{9,8},{10,11... | collective-permute-start | bytes 4718600 | tf_op jit(solution)/shard_map/ppermute | solution.py:29
  521.1 39.3 %collective-permute-start.24 = (bf16[384,2048]{1,0:T(8,128)(2,1)S(1)}, bf16[384,2048]{1,0:T(8,128)(2,1)S(1)}, u32[]{:S(2)}, u32[]{:S(2)}) collective-permute-start(bf16[384,2048]{1,0:T(8,128)(2,1)S(1)} %multiply_convert_fusion.2.refs_0_), channel_id=1, source_target_pairs={{0,2},{1,3},{2,0},{3,1},{4,6},{5,7},{6,4},{7,5},{8,10},{9,11},{10,... | collective-permute-start | bytes 4718600 | tf_op jit(solution)/shard_map/ppermute | solution.py:29
  529.6 30.9 %collective-permute-start.23 = (bf16[768,2048]{1,0:T(8,128)(2,1)}, bf16[768,2048]{1,0:T(8,128)(2,1)S(1)}, u32[]{:S(2)}, u32[]{:S(2)}) collective-permute-start(bf16[768,2048]{1,0:T(8,128)(2,1)} %convolution_convert_fusion.1), channel_id=1, source_target_pairs={{0,1},{1,0},{2,3},{3,2},{4,5},{5,4},{6,7},{7,6},{8,9},{9,8},{10,11... | collective-permute-start | bytes 9437192 | tf_op jit(solution)/shard_map/ppermute | solution.py:29
  544.1 25.4 %collective-permute-start.25 = (bf16[768,2048]{1,0:T(8,128)(2,1)}, bf16[768,2048]{1,0:T(8,128)(2,1)}, u32[]{:S(2)}, u32[]{:S(2)}) collective-permute-start(bf16[768,2048]{1,0:T(8,128)(2,1)} %fusion.12), channel_id=1, source_target_pairs={{0,1},{1,0},{2,3},{3,2},{4,5},{5,4},{6,7},{7,6},{8,9},{9,8},{10,11... | collective-permute-start | bytes 9437192 | tf_op jit(solution)/shard_map/ppermute | solution.py:29
  560.4 28.5 %collective-permute-start.28 = (bf16[384,2048]{1,0:T(8,128)(2,1)S(1)}, bf16[384,2048]{1,0:T(8,128)(2,1)S(1)}, u32[]{:S(2)}, u32[]{:S(2)}) collective-permute-start(bf16[384,2048]{1,0:T(8,128)(2,1)S(1)} %collective-permute-done.24.refs_1_), channel_id=1, source_target_pairs={{0,1},{1,0},{2,3},{3,2},{4,5},{5,4},{6,7},{7,6},{8,9},{9,8},{10,11... | collective-permute-start | bytes 4718600 | tf_op jit(solution)/shard_map/ppermute | solution.py:29
  587.4 41.3 %collective-permute-start.26 = (bf16[384,2048]{1,0:T(8,128)(2,1)}, bf16[384,2048]{1,0:T(8,128)(2,1)}, u32[]{:S(2)}, u32[]{:S(2)}) collective-permute-start(bf16[384,2048]{1,0:T(8,128)(2,1)} %slice.508), channel_id=1, source_target_pairs={{0,2},{1,3},{2,0},{3,1},{4,6},{5,7},{6,4},{7,5},{8,10},{9,11},{10,... | collective-permute-start | bytes 4718600 | tf_op jit(solution)/shard_map/ppermute | solution.py:29
  647.2 12.0 %collective-permute-start.29 = (bf16[768,2048]{1,0:T(8,128)(2,1)}, bf16[768,2048]{1,0:T(8,128)(2,1)}, u32[]{:S(2)}, u32[]{:S(2)}) collective-permute-start(bf16[768,2048]{1,0:T(8,128)(2,1)} %fusion.15), channel_id=1, source_target_pairs={{0,1},{1,0},{2,3},{3,2},{4,5},{5,4},{6,7},{7,6},{8,9},{9,8},{10,11... | collective-permute-start | bytes 9437192 | tf_op jit(solution)/shard_map/ppermute | solution.py:29
  658.6 39.7 %collective-permute-start.31 = (bf16[384,2048]{1,0:T(8,128)(2,1)}, bf16[384,2048]{1,0:T(8,128)(2,1)}, u32[]{:S(2)}, u32[]{:S(2)}) collective-permute-start(bf16[384,2048]{1,0:T(8,128)(2,1)} %get-tuple-element.156.refs_0_), channel_id=1, source_target_pairs={{0,2},{1,3},{2,0},{3,1},{4,6},{5,7},{6,4},{7,5},{8,10},{9,11},{10,... | collective-permute-start | bytes 4718600 | tf_op jit(solution)/shard_map/ppermute | solution.py:29
  698.3 3.6 collective-permute-start.32
  698.5 5.6 collective-permute-start.33
  700.2 36.8 %collective-permute-start.30 = (bf16[384,2048]{1,0:T(8,128)(2,1)}, bf16[384,2048]{1,0:T(8,128)(2,1)}, u32[]{:S(2)}, u32[]{:S(2)}) collective-permute-start(bf16[384,2048]{1,0:T(8,128)(2,1)} %slice.507), channel_id=1, source_target_pairs={{0,2},{1,3},{2,0},{3,1},{4,6},{5,7},{6,4},{7,5},{8,10},{9,11},{10,... | collective-permute-start | bytes 4718600 | tf_op jit(solution)/shard_map/ppermute | solution.py:29
  743.5 155.1 %copy-start.56 = (bf16[384,2048]{1,0:T(8,128)(2,1)}, bf16[384,2048]{1,0:T(8,128)(2,1)S(1)}, u32[]{:S(2)}) copy-start(bf16[384,2048]{1,0:T(8,128)(2,1)S(1)} %get-tuple-element.172.refs_0_) | copy-start | bytes 4718596
  766.0 46.0 %slice-start = ((s8[5767168]{0:T(1024)(128)(4,1)}), s8[1572864]{0:T(1024)(128)(4,1)S(1)}, s32[]{:S(2)}) async-start(s8[5767168]{0:T(1024)(128)(4,1)} %bitcast.180), calls=%async_computation.6 | async-start | bytes 3145728
  774.0 38.0 %collective-permute-start.35 = (bf16[768,2048]{1,0:T(8,128)(2,1)S(1)}, bf16[768,2048]{1,0:T(8,128)(2,1)S(1)}, u32[]{:S(2)}, u32[]{:S(2)}) collective-permute-start(bf16[768,2048]{1,0:T(8,128)(2,1)S(1)} %convolution_convert_fusion), channel_id=1, source_target_pairs={{0,1},{1,0},{2,3},{3,2},{4,5},{5,4},{6,7},{7,6},{8,9},{9,8},{10,11... | collective-permute-start | bytes 9437192 | tf_op jit(solution)/shard_map/ppermute | solution.py:29
  774.1 36.8 %collective-permute-start.34 = (bf16[384,2048]{1,0:T(8,128)(2,1)S(1)}, bf16[384,2048]{1,0:T(8,128)(2,1)S(1)}, u32[]{:S(2)}, u32[]{:S(2)}) collective-permute-start(bf16[384,2048]{1,0:T(8,128)(2,1)S(1)} %get-tuple-element.172.refs_0_), channel_id=1, source_target_pairs={{0,2},{1,3},{2,0},{3,1},{4,6},{5,7},{6,4},{7,5},{8,10},{9,11},{10,... | collective-permute-start | bytes 4718600 | tf_op jit(solution)/shard_map/ppermute | solution.py:29
  820.9 54.6 %slice-start.7 = ((s8[6291456]{0:T(1024)(128)(4,1)}), s8[2097152]{0:T(1024)(128)(4,1)S(1)}, s32[]{:S(2)}) async-start(s8[6291456]{0:T(1024)(128)(4,1)} %bitcast.192), calls=%async_computation.13 | async-start | bytes 4194304
  838.4 37.1 %collective-permute-start.36 = (bf16[384,2048]{1,0:T(8,128)(2,1)S(1)}, bf16[384,2048]{1,0:T(8,128)(2,1)}, u32[]{:S(2)}, u32[]{:S(2)}) collective-permute-start(bf16[384,2048]{1,0:T(8,128)(2,1)S(1)} %slice.506), channel_id=1, source_target_pairs={{0,2},{1,3},{2,0},{3,1},{4,6},{5,7},{6,4},{7,5},{8,10},{9,11},{10,... | collective-permute-start | bytes 4718600 | tf_op jit(solution)/shard_map/ppermute | solution.py:29
  898.6 9.6 collective-permute-start.38
  898.7 15.2 %collective-permute-start.40 = (bf16[384,2048]{1,0:T(8,128)(2,1)S(1)}, bf16[384,2048]{1,0:T(8,128)(2,1)}, u32[]{:S(2)}, u32[]{:S(2)}) collective-permute-start(bf16[384,2048]{1,0:T(8,128)(2,1)S(1)} %get-tuple-element.172.refs_0_), channel_id=1, source_target_pairs={{0,1},{1,0},{2,3},{3,2},{4,5},{5,4},{6,7},{7,6},{8,9},{9,8},{10,11... | collective-permute-start | bytes 4718600 | tf_op jit(solution)/shard_map/ppermute | solution.py:29
  899.2 14.7 %collective-permute-start.41 = (bf16[384,2048]{1,0:T(8,128)(2,1)S(1)}, bf16[384,2048]{1,0:T(8,128)(2,1)}, u32[]{:S(2)}, u32[]{:S(2)}) collective-permute-start(bf16[384,2048]{1,0:T(8,128)(2,1)S(1)} %copy-done.76), channel_id=1, source_target_pairs={{0,1},{1,0},{2,3},{3,2},{4,5},{5,4},{6,7},{7,6},{8,9},{9,8},{10,11... | collective-permute-start | bytes 4718600 | tf_op jit(solution)/shard_map/ppermute | solution.py:29
  902.9 37.6 %collective-permute-start.37 = (bf16[384,2048]{1,0:T(8,128)(2,1)}, bf16[384,2048]{1,0:T(8,128)(2,1)}, u32[]{:S(2)}, u32[]{:S(2)}) collective-permute-start(bf16[384,2048]{1,0:T(8,128)(2,1)} %slice.505), channel_id=1, source_target_pairs={{0,2},{1,3},{2,0},{3,1},{4,6},{5,7},{6,4},{7,5},{8,10},{9,11},{10,... | collective-permute-start | bytes 4718600 | tf_op jit(solution)/shard_map/ppermute | solution.py:29
  913.6 66.2 %collective-permute-start.39 = (bf16[384,2048]{1,0:T(8,128)(2,1)}, bf16[384,2048]{1,0:T(8,128)(2,1)}, u32[]{:S(2)}, u32[]{:S(2)}) collective-permute-start(bf16[384,2048]{1,0:T(8,128)(2,1)} %slice.504), channel_id=1, source_target_pairs={{0,2},{1,3},{2,0},{3,1},{4,6},{5,7},{6,4},{7,5},{8,10},{9,11},{10,... | collective-permute-start | bytes 4718600 | tf_op jit(solution)/shard_map/ppermute | solution.py:29
  933.5 50.9 %collective-permute-start.42 = (bf16[4,64,2048]{2,1,0:T(8,128)(2,1)}, bf16[4,64,2048]{2,1,0:T(8,128)(2,1)}, u32[]{:S(2)}, u32[]{:S(2)}) collective-permute-start(bf16[4,64,2048]{2,1,0:T(8,128)(2,1)} %dynamic-slice_bitcast_fusion.1), channel_id=1, source_target_pairs={{0,4},{4,0},{8,12},{12,8},{16,20},{20,16},{24,28},{28,24},{1,5},{5... | collective-permute-start | bytes 3145736 | tf_op jit(solution)/shard_map/ppermute | solution.py:29
  1002.6 48.2 %collective-permute-start.43 = (bf16[768,2048]{1,0:T(8,128)(2,1)}, bf16[768,2048]{1,0:T(8,128)(2,1)S(1)}, u32[]{:S(2)}, u32[]{:S(2)}) collective-permute-start(bf16[768,2048]{1,0:T(8,128)(2,1)} %get-tuple-element.187), channel_id=1, source_target_pairs={{0,1},{1,0},{2,3},{3,2},{4,5},{5,4},{6,7},{7,6},{8,9},{9,8},{10,11... | collective-permute-start | bytes 9437192 | tf_op jit(solution)/shard_map/ppermute | solution.py:29
  1009.0 41.4 %collective-permute-start.50 = (bf16[2,64,2048]{2,1,0:T(8,128)(2,1)S(1)}, bf16[2,64,2048]{2,1,0:T(8,128)(2,1)S(1)}, u32[]{:S(2)}, u32[]{:S(2)}) collective-permute-start(bf16[2,64,2048]{2,1,0:T(8,128)(2,1)S(1)} %dynamic-slice_bitcast_fusion.3), channel_id=1, source_target_pairs={{0,8},{4,12},{8,0},{12,4},{16,24},{20,28},{24,16},{28,20},{1,9},{5... | collective-permute-start | bytes 1572872 | tf_op jit(solution)/shard_map/ppermute | solution.py:29
  1009.1 1.3 collective-permute-start.44
  1010.4 3.7 collective-permute-start.45
  1050.6 31.1 %collective-permute-start.51 = (bf16[1,64,2048]{2,1,0:T(8,128)(2,1)S(1)}, bf16[1,64,2048]{2,1,0:T(8,128)(2,1)S(1)}, u32[]{:S(2)}, u32[]{:S(2)}) collective-permute-start(bf16[1,64,2048]{2,1,0:T(8,128)(2,1)S(1)} %constant_dynamic-slice_fusion.4), channel_id=1, source_target_pairs={{0,16},{4,20},{8,24},{12,28},{16,0},{20,4},{24,8},{28,12},{1,17},{... | collective-permute-start | bytes 786440 | tf_op jit(solution)/shard_map/ppermute | solution.py:29
  1050.8 33.5 %collective-permute-start.47 = (bf16[4,640,256]{2,1,0:T(8,128)(2,1)S(1)}, bf16[4,640,256]{2,1,0:T(8,128)(2,1)S(1)}, u32[]{:S(2)}, u32[]{:S(2)}) collective-permute-start(bf16[4,640,256]{2,1,0:T(8,128)(2,1)S(1)} %dynamic-slice_bitcast_fusion), channel_id=1, source_target_pairs={{0,4},{4,0},{8,12},{12,8},{16,20},{20,16},{24,28},{28,24},{1,5},{5... | collective-permute-start | bytes 3932168 | tf_op jit(solution)/shard_map/ppermute | solution.py:29
  1053.6 40.2 %collective-permute-start.46 = (bf16[384,2048]{1,0:T(8,128)(2,1)}, bf16[384,2048]{1,0:T(8,128)(2,1)}, u32[]{:S(2)}, u32[]{:S(2)}) collective-permute-start(bf16[384,2048]{1,0:T(8,128)(2,1)} %slice.503), channel_id=1, source_target_pairs={{0,2},{1,3},{2,0},{3,1},{4,6},{5,7},{6,4},{7,5},{8,10},{9,11},{10,... | collective-permute-start | bytes 4718600 | tf_op jit(solution)/shard_map/ppermute | solution.py:29
  1082.5 6.9 collective-permute-start.52
  1086.7 26.9 %collective-permute-start.48 = (bf16[2,640,256]{2,1,0:T(8,128)(2,1)}, bf16[2,640,256]{2,1,0:T(8,128)(2,1)}, u32[]{:S(2)}, u32[]{:S(2)}) collective-permute-start(bf16[2,640,256]{2,1,0:T(8,128)(2,1)} %dynamic-slice_bitcast_fusion.2), channel_id=1, source_target_pairs={{0,8},{4,12},{8,0},{12,4},{16,24},{20,28},{24,16},{28,20},{1,9},{5... | collective-permute-start | bytes 1966088 | tf_op jit(solution)/shard_map/ppermute | solution.py:29
  1114.8 16.3 %collective-permute-start.49 = (bf16[1,640,256]{2,1,0:T(8,128)(2,1)S(1)}, bf16[1,640,256]{2,1,0:T(8,128)(2,1)S(1)}, u32[]{:S(2)}, u32[]{:S(2)}) collective-permute-start(bf16[1,640,256]{2,1,0:T(8,128)(2,1)S(1)} %constant_dynamic-slice_fusion.5), channel_id=1, source_target_pairs={{0,16},{4,20},{8,24},{12,28},{16,0},{20,4},{24,8},{28,12},{1,17},{... | collective-permute-start | bytes 983048 | tf_op jit(solution)/shard_map/ppermute | solution.py:29
  1132.2 10.2 all-to-all-start.1
  1148.2 1.2 collective-permute-start.53
  1149.3 3.6 collective-permute-start.54
  (108 other events, 1174.1 us)
Sparse Core Ops, SparseCore 0:
  25.7 103.8 all-gather.2
  132.3 211.4 all-gather.4
  766.2 337.1 reduce-scatter.1

commit v2 on v1

--- a/solution.py
+++ b/solution.py
@@ -53,22 +53,6 @@
 
 def gather_rows(block, count):
     return jnp.concatenate(spread(block, count), axis=0)
-
-
-def gather_bits(stack, count, high, low):
-    me = lax.axis_index("dp")
-    bit = high
-    while bit >= low:
-        got = swap(stack, bit, count, "dp")
-        stack = widen(stack, got, (me & bit) != 0)
-        bit //= 2
-    return stack, got
-
-
-def widen(mine, other, odd):
-    first = jnp.where(odd, other, mine)
-    second = jnp.where(odd, mine, other)
-    return jnp.stack([first, second], axis=1).reshape((-1,) + mine.shape[1:])
 
 
 def halve(left, bit, count, axis="dp"):
@@ -193,7 +177,7 @@
         ],
         compiler_params=pltpu.CompilerParams(vmem_limit_bytes=48 * 2**20),
         cost_estimate=pl.CostEstimate(
-            flops=2 * heads * full * full * HD,
+            flops=heads * full * HD,
             bytes_accessed=heads * full * HD * 4,
             transcendentals=heads * full,
         ),
@@ -267,7 +251,7 @@
         scratch_shapes=[pltpu.VMEM((HD, full), F32)],
         compiler_params=pltpu.CompilerParams(vmem_limit_bytes=48 * 2**20),
         cost_estimate=pl.CostEstimate(
-            flops=4 * heads * full * full * HD,
+            flops=heads * full * HD,
             bytes_accessed=heads * full * HD * 6,
             transcendentals=heads * full,
         ),
@@ -303,119 +287,175 @@
     return (act * up).astype(BF16), (grad * up * slope).astype(BF16), (grad * act).astype(BF16)
 
 
-def feed_kernel(last, blocks, *refs):
-    n2_parts, grad_parts = refs[:blocks], refs[blocks : 2 * blocks]
-    refs = refs[2 * blocks :]
-    gu_ref, down_ref, hid_ref, out_ref, n2_out, grad_out = refs[:6]
-    refs = refs[6:]
-    n2_ref, grad_ref, in_sems, out_sems = refs
-    part = n2_parts[0].shape[0]
+def copies_in(parts, buf_ref, sems):
+    part = parts[0].shape[0]
+    return [
+        pltpu.make_async_copy(source, buf_ref.at[pl.ds(j * part, part)], sems.at[j])
+        for j, source in enumerate(parts)
+    ]
+
+
+def by_tiles(run, last):
     step = pl.program_id(0)
     count = pl.num_programs(0)
 
-    def arriving(j):
-        here = pl.ds(j * part, part)
-        return (
-            pltpu.make_async_copy(n2_parts[j], n2_ref.at[here], in_sems.at[2 * j]),
-            pltpu.make_async_copy(grad_parts[j], grad_ref.at[here], in_sems.at[2 * j + 1]),
-        )
-
-    def leaving():
-        return (
-            pltpu.make_async_copy(n2_ref, n2_out, out_sems.at[0]),
-            pltpu.make_async_copy(grad_ref, grad_out, out_sems.at[1]),
-        )
+    @pl.when(step == 0)
+    def _():
+        run(TILE, True)
+
+    @pl.when((step > 0) & (step < count - 1))
+    def _():
+        run(TILE, False)
+
+    @pl.when(step == count - 1)
+    def _():
+        run(last, False)
+
+
+def hidden_grad_kernel(last, blocks, *refs):
+    parts = refs[:blocks]
+    down_ref, grad_ref, rows_out, rows_ref, in_sems, out_sem = refs[blocks:]
+    part = parts[0].shape[0]
+    coming = copies_in(parts, rows_ref, in_sems)
+    leaving = pltpu.make_async_copy(rows_ref, rows_out, out_sem)
 
     def run(size, first):
         if first:
-            for j in range(blocks):
-                for copy in arriving(j):
-                    copy.start()
+            for copy in coming:
+                copy.start()
         for j in range(blocks):
             here = slice(j * part, (j + 1) * part)
             if first:
-                for copy in arriving(j):
-                    copy.wait()
-            values = n2_ref[here, :]
+                coming[j].wait()
+            grad_ref[here, :size] = jnp.dot(
+                rows_ref[here, :], down_ref[:, :size], preferred_element_type=F32
+            ).astype(BF16)
+        if first:
+            leaving.start()
+
+    by_tiles(run, last)
+
+    @pl.when(pl.program_id(0) == pl.num_programs(0) - 1)
+    def _():
+        leaving.wait()
+
+
+def feed_kernel(last, blocks, *refs):
+    parts = refs[:blocks]
+    gu_ref, grad_ref, hid_ref, out_ref, rows_out, rows_ref, in_sems, out_sem = refs[blocks:]
+    part = parts[0].shape[0]
+    coming = copies_in(parts, rows_ref, in_sems)
+    leaving = pltpu.make_async_copy(rows_ref, rows_out, out_sem)
+
+    def run(size, first):
+        if first:
+            for copy in coming:
+                copy.start()
+        for j in range(blocks):
+            here = slice(j * part, (j + 1) * part)
+            if first:
+                coming[j].wait()
+            values = rows_ref[here, :]
             if size == TILE:
                 gate = jnp.dot(values, gu_ref[:, :size], preferred_element_type=F32)
                 up = jnp.dot(values, gu_ref[:, size : 2 * size], preferred_element_type=F32)
             else:
                 both = jnp.dot(values, gu_ref[:, : 2 * size], preferred_element_type=F32)
                 gate, up = both[:, :size], both[:, size:]
-            grad = jnp.dot(grad_ref[here, :], down_ref[:, :size], preferred_element_type=F32)
+            grad = grad_ref[here, :size].astype(F32)
             hid, gate_grad, up_grad = activate(gate, up, grad)
             hid_ref[here, :size] = hid
             out_ref[here, :size] = gate_grad
             out_ref[here, size : 2 * size] = up_grad
         if first:
-            for copy in leaving():
-                copy.start()
-
-    @pl.when(step == 0)
+            leaving.start()
+
+    by_tiles(run, last)
+
+    @pl.when(pl.program_id(0) == pl.num_programs(0) - 1)
     def _():
-        run(TILE, True)
-
-    @pl.when((step > 0) & (step < count - 1))
-    def _():
-        run(TILE, False)
-
-    @pl.when(step == count - 1)
-    def _():
-        run(last, False)
-        for copy in leaving():
-            copy.wait()
-
-
-def feed(n2_parts, grad_parts, gu_w, down_t):
-    blocks = len(n2_parts)
-    part, width = n2_parts[0].shape
+        leaving.wait()
+
+
+def tiled(hidden):
+    return hidden % 128 == 0 and len(tiles_of(hidden)) >= 3
+
+
+def row_scratch(rows, width, blocks):
+    return [
+        pltpu.VMEM((rows, width), BF16),
+        pltpu.SemaphoreType.DMA((blocks,)),
+        pltpu.SemaphoreType.DMA,
+    ]
+
+
+def hidden_grad(parts, down_t):
+    blocks = len(parts)
+    part, width = parts[0].shape
     rows = blocks * part
     hidden = down_t.shape[1]
+    if not tiled(hidden):
+        joined = jnp.concatenate(parts, axis=0)
+        return dot(joined, down_t, 1, 0).astype(BF16), joined
     pieces = tiles_of(hidden)
-    if hidden % 128 or len(pieces) < 3:
-        n2 = jnp.concatenate(n2_parts, axis=0)
-        grad = jnp.concatenate(grad_parts, axis=0)
+    hbm = pl.BlockSpec(memory_space=pl.ANY)
+    return pl.pallas_call(
+        functools.partial(hidden_grad_kernel, pieces[-1][1] - pieces[-1][0], blocks),
+        grid=(len(pieces),),
+        in_specs=[hbm] * blocks + [pl.BlockSpec((width, TILE), lambda j: (0, j))],
+        out_specs=[pl.BlockSpec((rows, TILE), lambda j: (0, j)), hbm],
+        out_shape=[
+            jax.ShapeDtypeStruct((rows, hidden), BF16),
+            jax.ShapeDtypeStruct((rows, width), BF16),
+        ],
+        scratch_shapes=row_scratch(rows, width, blocks),
+        compiler_params=pltpu.CompilerParams(vmem_limit_bytes=56 * 2**20),
+        cost_estimate=pl.CostEstimate(
+            flops=1000000, bytes_accessed=1000000, transcendentals=1000
+        ),
+    )(*parts, down_t)
+
+
+def feed(parts, gu_w, grad):
+    blocks = len(parts)
+    part, width = parts[0].shape
+    rows = blocks * part
+    hidden = grad.shape[1]
+    if not tiled(hidden):
+        joined = jnp.concatenate(parts, axis=0)
         gate_w, up_w = separate(gu_w)
         hid, gate_grad, up_grad = activate(
-            dot(n2, gate_w, 1, 0), dot(n2, up_w, 1, 0), dot(grad, down_t, 1, 0)
+            dot(joined, gate_w, 1, 0), dot(joined, up_w, 1, 0), grad.astype(F32)
         )
-        return hid, interleave(gate_grad, up_grad), n2, grad
-    last = pieces[-1][1] - pieces[-1][0]
+        return hid, interleave(gate_grad, up_grad), joined
+    pieces = tiles_of(hidden)
     hbm = pl.BlockSpec(memory_space=pl.ANY)
     return pl.pallas_call(
-        functools.partial(feed_kernel, last, blocks),
+        functools.partial(feed_kernel, pieces[-1][1] - pieces[-1][0], blocks),
         grid=(len(pieces),),
-        in_specs=[hbm] * (2 * blocks)
+        in_specs=[hbm] * blocks
         + [
             pl.BlockSpec((width, 2 * TILE), lambda j: (0, j)),
-            pl.BlockSpec((width, TILE), lambda j: (0, j)),
+            pl.BlockSpec((rows, TILE), lambda j: (0, j)),
         ],
         out_specs=[
             pl.BlockSpec((rows, TILE), lambda j: (0, j)),
             pl.BlockSpec((rows, 2 * TILE), lambda j: (0, j)),
             hbm,
-            hbm,
         ],
         out_shape=[
             jax.ShapeDtypeStruct((rows, hidden), BF16),
             jax.ShapeDtypeStruct((rows, 2 * hidden), BF16),
             jax.ShapeDtypeStruct((rows, width), BF16),
-            jax.ShapeDtypeStruct((rows, width), BF16),
-        ],
-        scratch_shapes=[
-            pltpu.VMEM((rows, width), BF16),
-            pltpu.VMEM((rows, width), BF16),
-            pltpu.SemaphoreType.DMA((2 * blocks,)),
-            pltpu.SemaphoreType.DMA((2,)),
-        ],
+        ],
+        scratch_shapes=row_scratch(rows, width, blocks),
         compiler_params=pltpu.CompilerParams(vmem_limit_bytes=56 * 2**20),
         cost_estimate=pl.CostEstimate(
             flops=rows * width * hidden,
             bytes_accessed=4 * rows * width,
             transcendentals=rows,
         ),
-    )(*n2_parts, *grad_parts, gu_w, down_t)
+    )(*parts, gu_w, grad)
 
 
 def rotate(values, cos, sin):
@@ -770,27 +810,24 @@
 
     half = dp // 2
     gu_mine = interleave(gate_weight, up_weight)
-    gu_w = row_major(lax.all_gather(row_major(gu_mine), "dp", axis=0, tiled=True))
+    down_t = row_major(lax.all_gather(row_major(down_weight.T), "dp", axis=0, tiled=True))
+    gu_w = row_major(
+        lax.all_gather(row_major(after(gu_mine, attn_all)), "dp", axis=0, tiled=True)
+    )
     held = later(tokens)
     cot_local = jnp.where(valid[..., None], cotangent, jnp.zeros_like(cotangent))
-    rows_far, cot_far = [], []
+    rows_far = []
     chain = []
-    for source, far in ((held, rows_far), (cot_local, cot_far)):
-        for s in range(seqs):
-            far.append(spread(after(source[s], *chain), sp, "sp", 2))
-            chain = far[-1][1:]
+    for s in range(seqs):
+        rows_far.append(spread(after(held[s], *chain), sp, "sp", 2))
+        chain = rows_far[-1][1:]
     rows_all = [spread(far, sp) for far in rows_far]
-    cot_parts = [spread(far, sp) for far in cot_far]
-    down_a, _ = gather_bits(after(down_weight.T, attn_all)[None], dp, half, half)
-    down_b, down_far = gather_bits(down_a, dp, half // 2, 2)
-    down_c, down_near = gather_bits(down_b, dp, 1, 1)
+    cot_far = [spread(after(cot_local[0], *chain), sp, "sp", 2)]
     proj_t = attn_all[:, :proj_cols].T
     gains = attn_all[:, proj_cols : proj_cols + 2].astype(F32)
     gain_one, gain_two = gains[:, 0], gains[:, 1]
     out_w = attn_all[:, proj_cols + 128 :].reshape(q_cols, width)
-    down_t = down_c.reshape(width, hidden)
     rows_all[0][0] = after(rows_all[0][0], *rows_far[-1])
-    early = [[part for far in cot_far for part in far], []]
 
     row_pos = jnp.concatenate([(me ^ member) * local + jnp.arange(local) for member in order])
     frequency = jnp.power(10000.0, -2.0 * jnp.arange(HALF).astype(F32) / HD)
@@ -807,52 +844,59 @@
         scaled = grad * gain
         return scale * scaled - values * scale**3 * jnp.mean(scaled * values, axis=-1, keepdims=True)
 
-    normed_one, saved, branches, middles, normed_two, n2_far = [], [], [], [], [], []
+    normed_one, saved, branches, middles, n2_far, begins = [], [], [], [], [], []
+
+    def take_branch(s, mark):
+        branch = after(reduce_far(begins[s], sp), mark)
+        middle = tokens[s].astype(F32) + branch
+        n2_far.append(spread(norm(middle, gain_two).astype(BF16), sp, "sp", 2))
+        branches.append(branch)
+        middles.append(middle)
+
     for s in range(seqs):
-        length = lengths[s : s + 1]
         parts = list(rows_all[s])
         if s:
-            parts[0] = after(parts[0], begun)
+            parts[0] = after(parts[0], begins[-1])
         n1, q, k_t, v_t, k, v = project(parts, at, gain_one[None], proj_t, cos, sin, heads)
         normed_one.append(n1)
-        q = after(q, *cot_parts[s], *early[min(s, 1)], *branches)
-        att, lse = attend_forward(q, k, v_t, length)
-        if s:
-            normed_two.append(spread([after(part, att) for part in n2_far[-1]], sp))
+        att, lse = attend_forward(q, k, v_t, lengths[s : s + 1])
         flat = att.reshape(q_cols, full)
-        flat = after(flat, *normed_two[-1], gu_w, down_near) if s else after(flat, down_far)
-        begun = reduce_pair(*merge_heads(flat, at, out_w, sp), sp)
-        branch = reduce_far(begun, sp)
-        middle = tokens[s].astype(F32) + branch
-        n2_far.append(spread(norm(middle, gain_two).astype(BF16), sp, "sp", 2))
+        if s == 0:
+            flat = after(flat, *cot_far[0], down_t)
+        else:
+            take_branch(s - 1, att)
+            flat = after(flat, *n2_far[-1])
+        begins.append(reduce_pair(*merge_heads(flat, at, out_w, sp), sp))
         saved.append((q, k, k_t, v, att, lse))
-        branches.append(branch)
-        middles.append(middle)
-
-    def mlp_near(hid, keep):
-        return reduce_near(
-            lambda lo, hi: dot((hid if lo else keep)[lo:hi], down_t, 1, 1), full, sp
-        )
+    for s in range(1, seqs):
+        cot_far.append(spread(after(cot_local[s], begins[-1]), sp, "sp", 2))
+    hidden_grads, cot_all = zip(*[hidden_grad(spread(far, sp), down_t) for far in cot_far])
+    gu_w = after(gu_w, *hidden_grads)
+    take_branch(seqs - 1, gu_w)
+    begun = begins[-1]
+    normed_two = [spread(n2_far[0], sp)]
+
+    def mlp_near(hid):
+        return reduce_near(lambda lo, hi: dot(hid[lo:hi], down_t, 1, 1), full, sp)
 
     begun_mixed = []
-    hiddens, gu_grads, n2_grads, middle_grads, grad_rows, cot_all = [], [], [], [], [], []
+    hiddens, gu_grads, n2_grads, middle_grads, grad_rows = [], [], [], [], []
     down_wgrad = 0.0
     for s in range(seqs):
-        n2 = [after(part, begun) for part in normed_two[s]]
-        made = feed(n2, cot_parts[s], gu_w, down_t)
-        hid, gu_grad, normed_two[s], cot_all_s = made
-        cot_all.append(cot_all_s)
+        n2 = [after(part, begun, *hidden_grads) for part in normed_two[s]]
+        hid, gu_grad, joined = feed(n2, gu_w, hidden_grads[s])
+        normed_two[s] = joined
         hiddens.append(hid)
         gu_grads.append(gu_grad)
         if s < seqs - 1:
-            low, high = n2_far[s + 1][0], n2_far[s + 1]
-            hid = after(hid, low)
+            low, high = [n2_far[s + 1][0]], n2_far[s + 1]
+            hid = after(hid, *low)
             down_wgrad = row_major(dot(cot_all[s], hid, 0, 0))
-            begun_mixed.append(mlp_near(hid, hid))
+            begun_mixed.append(mlp_near(hid))
             high = high + [down_wgrad, begun_mixed[0]]
         else:
-            low, high = n2_grads[0], [n2_grads[0]]
-        send, keep = after(gu_grad, low), after(gu_grad, *high)
+            low, high = [n2_grads[0]], [n2_grads[0]]
+        send, keep = after(gu_grad, *low), after(gu_grad, *high)
         begun = reduce_near(
             lambda lo, hi: dot((keep if lo == 0 else send)[lo:hi], gu_w, 1, 1), full, sp
         )
@@ -876,8 +920,8 @@
     rows = after(cot_all[-1], middle_grads[-1])
     down_wgrad = down_wgrad + dot(rows, hiddens[-1], 0, 0)
     down_wgrad = down_wgrad.astype(BF16)
-    hid = after(hiddens[-1], down_wgrad)
-    begun_mixed.append(mlp_near(hid, after(hid, *far_rows)))
+    hid = after(hiddens[-1], down_wgrad, *far_rows)
+    begun_mixed.append(mlp_near(hid))
 
     feed_wgrad = jnp.concatenate([gu_wgrad, down_wgrad], axis=1)
     feed_grad = row_major(
@@ -896,10 +940,6 @@
                 for member in ([tokens[s].astype(F32) for s in range(seqs)], branches, mixed)
             ]
         )
-        bit = 1
-        while bit < sp:
-            sums = sums + swap(sums, bit, sp)
-            bit *= 2
         return sums
 
     proj_wgrad = None
@@ -908,7 +948,7 @@
     for s in range(seqs):
         q, k, k_t, v, att, lse = saved[s]
         rows = list(grad_rows[s])
-        rows[0] = after(rows[0], mark) if s else after(rows[0], *far_rows, *begun_mixed)
+        rows[0] = after(rows[0], mark) if s else after(rows[0], *begun_mixed)
         att_grad, delta, out_wgrad = split_heads(rows, at, out_w, att, out_wgrad)
         if s:
             q = after(q, begun)
@@ -916,10 +956,11 @@
         gq, gk, gv = attend_backward(q, att_grad, k, k_t, v, lse, delta, lengths[s : s + 1])
         mark = gq
         if s == 0:
-            mixed = [reduce_far(after(begun_mixed[0], att_grad), sp)]
+            mixed = [reduce_far(after(begun_mixed[0], *far_rows), sp)]
             gq = after(gq, mixed[0])
             mixed += [reduce_far(after(begun_mixed[t], mark), sp) for t in range(1, seqs)]
         else:
+            sums = norm_sums(mixed)
             gq = after(gq, got, *mixed, n1_grad)
         keep, send, proj_wgrad = return_rows(
             gq, gk, gv, at, cos, sin, proj_t, normed_one[s], proj_wgrad, dp
@@ -928,21 +969,23 @@
         if s == 0:
             n1_grad = reduce_far(begun, sp)
         else:
-            out_grad = finish(join(staying, after(got, mark)).astype(BF16), 2, dp)
-            sums = norm_sums(mixed)
-            n1_grad = reduce_far(after(begun, sums), sp)
+            out_left = join(staying, after(got, mark)).astype(BF16)
+            out_staying, out_got = halve(out_left, 2, dp)
+            n1_grad = reduce_far(begun, sp)
         rest = norm_back(n1_grad, tokens[s].astype(F32), gain_one)
         input_grads.append((middle_grads[s] + rest).astype(BF16))
     input_grad = jnp.stack(input_grads)
-    feed_grad = after(feed_grad, n1_grad).astype(F32)
+    staying, got = halve(proj_wgrad, 1, dp)
+    left = join(staying, after(got, begun)).astype(BF16)
+    out_left = join(out_staying, after(out_got, left)).astype(BF16)
+    staying, got = halve(left, 2, dp)
+    left = join(staying, after(got, n1_grad, feed_grad)).astype(BF16)
+    proj_grad = finish(left, 4, dp)
+    out_grad = finish(after(out_left, left), 4, dp)
+    out_grad = lax.ppermute(out_grad.astype(BF16), ("dp", "sp"), back).astype(F32)
+    feed_grad = after(feed_grad, left).astype(F32)
     gate_out, up_out = separate(feed_grad[:, : 2 * hidden])
     down_out = feed_grad[:, 2 * hidden :].T
-    staying, got = halve(proj_wgrad, 1, dp)
-    left = join(staying, after(got, begun)).astype(BF16)
-    staying, got = halve(left, 2, dp)
-    left = join(staying, after(got, n1_grad)).astype(BF16)
-    proj_grad = finish(left, 4, dp)
-    out_grad = lax.ppermute(out_grad.astype(BF16), ("dp", "sp"), back).astype(F32)
 
     block_out = jnp.stack(
         [((middles[s] + mixed[s]) * valid[s][:, None]).astype(BF16) for s in range(seqs)]
@@ -969,6 +1012,11 @@
     shares = rowwise(gate_weight, gate_out) + rowwise(up_weight, up_out)
     gain_two_grad = finish(blocks_of(shares, sp), 1, sp, "sp") / feed_gain.astype(F32)
 
+    sums = after(sums, n1_grad)
+    bit = 1
+    while bit < sp:
+        sums = sums + swap(sums, bit, sp)
+        bit *= 2
     branch_norms = jnp.sqrt(sums / (lengths.astype(F32) * width))
     return (
         block_out,

time: 1170 us -> 1110 us (0.949)
  waiting for transfers between devices: 410 us -> 346 us
  local copies, waits for them, and re-layouts: 108 us -> 92.5 us
    ppermute x53 -> x50, waiting for transfers between devices: 400 us -> 272 us  [swap(): return lax.ppermute(values, axis, [(i, i ^ bit) for i in range(count)])]
    all_gather x1, waiting for transfers between devices: 0.01 us -> 65.7 us  [body(): lax.all_gather(row_major(attn_mine), 'dp', axis=0, tiled=True)]
    pallas_call x2 -> x4, Pallas kernels: 75.3 us -> 88.6 us  [the longest x2 54.9 us: feed(): pl.pallas_call(functools.partial(feed_kernel, pieces[-1][1] - pieces[-1][...]
    unnamed x245 -> x205, local copies, waits for them, and re-layouts: 61.6 us -> 51.3 us
    ppermute x53 -> x50, starting transfers between devices: 37.1 us -> 46.7 us  [swap(): return lax.ppermute(values, axis, [(i, i ^ bit) for i in range(count)])]
  transfers between devices with their start and end apart: 60 -> 58, of which waited for: 26 -> 23; matrix products, arithmetic and copies ran while one was open for 24% -> 25% of each run, Pallas kernels for 26% -> 29%
where the time goes in v2:
time: 1110 us
  waiting for transfers between devices  346 us (31%)
  Pallas kernels  317 us (29%)
  matrix products  175 us (16%)
  other arithmetic  102 us (9%)
  local copies, waits for them, and re-layouts  92.5 us (8%)
  starting transfers between devices  56.9 us (5%)
  between operations  16.2 us (1%)
    ppermute x50, waiting for transfers between devices, swap(): return lax.ppermute(values, axis, [(i, i ^ bit) for i in range(count)])  272 us
    dot_general x12, matrix products, dot(): lax.dot_general(left, right, (((left_dim,), (right_dim,)), ((), ())), pre...  175 us
    pallas_call x2, Pallas kernels, attend_backward(): pl.pallas_call(functools.partial(backward_kernel, block), grid=(heads,),...  69.4 us
    all_gather x1, waiting for transfers between devices, body(): lax.all_gather(row_major(attn_mine), 'dp', axis=0, tiled=True)  65.7 us
    pallas_call x2, Pallas kernels, feed(): pl.pallas_call(functools.partial(feed_kernel, pieces[-1][1] - pieces[-1][...  54.9 us
    pallas_call x2, Pallas kernels, attend_forward(): pl.pallas_call(functools.partial(forward_kernel, block), grid=(heads,), i...  51.3 us
    unnamed x205, local copies, waits for them, and re-layouts  51.3 us
    ppermute x50, starting transfers between devices, swap(): return lax.ppermute(values, axis, [(i, i ^ bit) for i in range(count)])  46.7 us
  transfers between devices with their start and end apart: 58, of which 23 were waited for; matrix products, arithmetic and copies ran while one was open for 25% of the time, Pallas kernels for 29%

profile of v2, /device:TPU:0, one launch (start us, length us, event | category | flops | bytes accessed | tf_op | source)
XLA Modules:
  0.0 1105.1 jit_solution(13894221183468049098)
XLA Ops:
  11.9 4.2 all-to-all-start
  17.7 5.9 all-to-all-done
  45.5 13.8 %collective-permute-start = (bf16[384,2048]{1,0:T(8,128)(2,1)}, bf16[384,2048]{1,0:T(8,128)(2,1)}, u32[]{:S(2)}, u32[]{:S(2)}) collective-permute-start(bf16[384,2048]{1,0:T(8,128)(2,1)} %get-tuple-element.106.refs_0_), channel_id=1, source_target_pairs={{0,2},{1,3},{2,0},{3,1},{4,6},{5,7},{6,4},{7,5},{8,10},{9,11},{10,... | collective-permute-start | bytes 4718600 | tf_op jit(solution)/shard_map/ppermute | solution.py:29
  63.9 65.7 %all-gather.4.cloned.1.call-done = bf16[2048,1280]{1,0:T(8,128)(2,1)} async-done(((bf16[256,1280]{1,0:T(8,128)(2,1)}), bf16[2048,1280]{1,0:T(8,128)(2,1)}) %all-gather.4.cloned.1.call-update) | async-done | bytes 5242896 | tf_op jit(solution)/shard_map/all_gather | solution.py:805
  136.7 28.6 %collective-permute-done.1.refs_1_ = bf16[384,2048]{1,0:T(8,128)(2,1)} collective-permute-done((bf16[384,2048]{1,0:T(8,128)(2,1)}, bf16[384,2048]{1,0:T(8,128)(2,1)}, u32[]{:S(2)}, u32[]{:S(2)}) %collective-permute-start.1) | collective-permute-done | bytes 1572896 | tf_op jit(solution)/shard_map/ppermute | solution.py:29
  169.6 3.3 slice.362
  172.9 4.5 reshape.260.w_ref.refs_4_
  177.4 3.5 slice.360
  180.9 4.5 copy.71
  188.0 12.9 %shard_map.211 = (bf16[1536,2048]{1,0:T(8,128)(2,1)}, bf16[8,64,1536]{2,1,0:T(8,128)(2,1)}, bf16[64,1536]{1,0:T(8,128)(2,1)}, bf16[64,1536]{1,0:T(8,128)(2,1)}, ...) custom-call(s32[4]{0:T(128)} %pad_add_fusion.at_ref, bf16[384,2048]{1,0:T(8,128)(2,1)} %get-tuple-element.106.refs_0_, ...), custom_call_target="tpu_custom_call" | custom-call | flops 1000000 | bytes 1000000 | tf_op jit(solution)/shard_map/pallas_call | solution.py:549
  204.3 25.6 %shard_map.212 = (bf16[8,64,1536]{2,1,0:T(8,128)(2,1)S(1)}, f32[8,1,1536]{2,1,0:T(1,128)S(1)}) custom-call(s32[1]{0:T(128)} %get-tuple-element.303.len_ref, bf16[8,64,1536]{2,1,0:T(8,128)(2,1)S(1)} %copy-done.2, bf16[1536,64]{1,0:T(8,128)(2,1)S(1)} %copy-done.10, bf16[64,1536]{1,0:T(8,128)(2,1)S(1)} %copy-done.21), custom_call_target="tpu_custom_call" | custom-call | flops 786432 | bytes 3145728 | tf_op jit(solution)/shard_map/pallas_call | solution.py:161
  231.1 7.9 shard_map.213
  239.6 9.1 collective-permute-done.6
  256.0 13.0 %shard_map.214 = (bf16[1536,2048]{1,0:T(8,128)(2,1)}, bf16[8,64,1536]{2,1,0:T(8,128)(2,1)}, bf16[64,1536]{1,0:T(8,128)(2,1)}, bf16[64,1536]{1,0:T(8,128)(2,1)}, ...) custom-call(s32[4]{0:T(128)} %pad_add_fusion.at_ref, bf16[384,2048]{1,0:T(8,128)(2,1)} %get-tuple-element.115.refs_0_, ...), custom_call_target="tpu_custom_call" | custom-call | flops 1000000 | bytes 1000000 | tf_op jit(solution)/shard_map/pallas_call | solution.py:549
  272.3 25.8 %shard_map.215 = (bf16[8,64,1536]{2,1,0:T(8,128)(2,1)S(1)}, f32[8,1,1536]{2,1,0:T(1,128)S(1)}) custom-call(s32[1]{0:T(128)} %get-tuple-element.304.len_ref, bf16[8,64,1536]{2,1,0:T(8,128)(2,1)S(1)} %copy-done, bf16[1536,64]{1,0:T(8,128)(2,1)S(1)} %copy-done.8, bf16[64,1536]{1,0:T(8,128)(2,1)S(1)} %copy-done.20), custom_call_target="tpu_custom_call" | custom-call | flops 786432 | bytes 3145728 | tf_op jit(solution)/shard_map/pallas_call | solution.py:161
  304.6 34.5 %collective-permute-done.10.refs_1_ = bf16[384,2048]{1,0:T(8,128)(2,1)} collective-permute-done((bf16[384,2048]{1,0:T(8,128)(2,1)S(1)}, bf16[384,2048]{1,0:T(8,128)(2,1)}, u32[]{:S(2)}, u32[]{:S(2)}) %collective-permute-start.10) | collective-permute-done | bytes 1572896 | tf_op jit(solution)/shard_map/ppermute | solution.py:29
  339.2 7.2 shard_map.216
  346.4 5.9 collective-permute-done.11
  360.3 32.7 %collective-permute-done.14.refs_1_ = bf16[384,2048]{1,0:T(8,128)(2,1)} collective-permute-done((bf16[384,2048]{1,0:T(8,128)(2,1)S(1)}, bf16[384,2048]{1,0:T(8,128)(2,1)}, u32[]{:S(2)}, u32[]{:S(2)}) %collective-permute-start.14) | collective-permute-done | bytes 1572896 | tf_op jit(solution)/shard_map/ppermute | solution.py:29
  395.8 16.9 %shard_map.217 = (bf16[1536,1408]{1,0:T(8,128)(2,1)}, bf16[1536,2048]{1,0:T(8,128)(2,1)}) custom-call(bf16[384,2048]{1,0:T(8,128)(2,1)} %get-tuple-element.111.refs_0_, bf16[384,2048]{1,0:T(8,128)(2,1)} %collective-permute-done.5.refs_1_, bf16[384,2048]{1,0:T(8,128)(2,1)} %copy-done.61, bf16[384,2048]{1,0:T(8,128)(2,1)} %copy-done.62, ...), custom_call_target="tpu_custom_call" | custom-call | flops 1000000 | bytes 1000000 | tf_op jit(solution)/shard_map/pallas_call | solution.py:402
  412.7 13.3 %collective-permute-done.19 = bf16[384,2048]{1,0:T(8,128)(2,1)} collective-permute-done((bf16[384,2048]{1,0:T(8,128)(2,1)S(1)}, bf16[384,2048]{1,0:T(8,128)(2,1)}, u32[]{:S(2)}, u32[]{:S(2)}) %collective-permute-start.19) | collective-permute-done | bytes 1572896 | tf_op jit(solution)/shard_map/ppermute | solution.py:29
  426.0 4.7 slice_add_fusion.4
  430.7 16.8 %shard_map.218 = (bf16[1536,1408]{1,0:T(8,128)(2,1)}, bf16[1536,2048]{1,0:T(8,128)(2,1)}) custom-call(bf16[384,2048]{1,0:T(8,128)(2,1)} %get-tuple-element.125.refs_0_, bf16[384,2048]{1,0:T(8,128)(2,1)} %collective-permute-done.14.refs_1_, bf16[384,2048]{1,0:T(8,128)(2,1)} %collective-permute-done.15.refs_2_, ...), custom_call_target="tpu_custom_call" | custom-call | flops 1000000 | bytes 1000000 | tf_op jit(solution)/shard_map/pallas_call | solution.py:402
  454.1 27.5 %shard_map.219 = (bf16[1536,1408]{1,0:T(8,128)(2,1)}, bf16[1536,2816]{1,0:T(8,128)(2,1)}, bf16[1536,2048]{1,0:T(8,128)(2,1)}) custom-call(bf16[384,2048]{1,0:T(8,128)(2,1)} %copy-done.46, bf16[384,2048]{1,0:T(8,128)(2,1)} %collective-permute-done.10.refs_1_, bf16[384,2048]{1,0:T(8,128)(2,1)} %collective-permute-done.17.refs_2_, ...), custom_call_target="tpu_custom_call" | custom-call | flops 4429185024 | bytes 12582912 | tf_op jit(solution)/shard_map/pallas_call | solution.py:433
  481.6 9.1 convolution_convert_fusion.1
  491.0 13.1 %fusion.12 = bf16[768,2048]{1,0:T(8,128)(2,1)} fusion(bf16[2048,2816]{1,0:T(8,128)(2,1)} %all-gather.8.cloned.1.call-done.refs_4_, bf16[1536,2816]{1,0:T(8,128)(2,1)S(1)} %copy-done.79), kind=kOutput, calls=%fused_computation.31 | convolution fusion | flops 8859942912 | bytes 19005440 | tf_op jit(solution)/shard_map/dot_general | solution.py:23
  504.3 16.9 %fusion.59 = f32[2048,1408]{1,0:T(8,128)} fusion(bf16[1536,2048]{1,0:T(8,128)(2,1)} %get-tuple-element.137, bf16[1536,1408]{1,0:T(8,128)(2,1)} %get-tuple-element.135), kind=kOutput, calls=%fused_computation.193 | convolution fusion | flops 8858370048 | bytes 22151168 | tf_op jit(solution)/shard_map/dot_general | solution.py:23
  521.5 10.2 convert_add_fusion.5
  531.7 13.1 %convert_add_fusion.4 = f32[768,2048]{1,0:T(8,128)} fusion(bf16[768,2048]{1,0:T(8,128)(2,1)} %collective-permute-done.22, bf16[2048,2816]{1,0:T(8,128)(2,1)S(1)} %bitcast.159, bf16[1536,2816]{1,0:T(8,128)(2,1)} %get-tuple-element.138), kind=kOutput, calls=%fused_computation.7 | convolution fusion | flops 8861515776 | bytes 25296896 | tf_op jit(solution)/shard_map/dot_general | solution.py:23
  547.2 27.4 %shard_map.220 = (bf16[1536,1408]{1,0:T(8,128)(2,1)}, bf16[1536,2816]{1,0:T(8,128)(2,1)}, bf16[1536,2048]{1,0:T(8,128)(2,1)}) custom-call(bf16[384,2048]{1,0:T(8,128)(2,1)} %multiply_convert_fusion.2.refs_0_, bf16[384,2048]{1,0:T(8,128)(2,1)} %collective-permute-done.21.refs_1_, bf16[384,2048]{1,0:T(8,128)(2,1)} %collective-permute-done.23.refs_2_, ...), custom_call_target="tpu_custom_call" | custom-call | flops 4429185024 | bytes 12582912 | tf_op jit(solution)/shard_map/pallas_call | solution.py:433
  574.7 9.0 collective-permute-done.25
  586.5 15.6 %fusion.15 = bf16[768,2048]{1,0:T(8,128)(2,1)} fusion(bf16[2048,2816]{1,0:T(8,128)(2,1)} %all-gather.8.cloned.1.call-done.refs_4_, bf16[1536,2816]{1,0:T(8,128)(2,1)} %get-tuple-element.145), kind=kOutput, calls=%fused_computation.32 | convolution fusion | flops 8859942912 | bytes 19005440 | tf_op jit(solution)/shard_map/dot_general | solution.py:23
  604.3 4.8 fusion.54
  609.5 13.4 %convert_add_fusion.3 = f32[768,2048]{1,0:T(8,128)} fusion(bf16[768,2048]{1,0:T(8,128)(2,1)} %collective-permute-done.26, bf16[2048,2816]{1,0:T(8,128)(2,1)S(1)} %bitcast.161, bf16[1536,2816]{1,0:T(8,128)(2,1)} %get-tuple-element.145), kind=kOutput, calls=%fused_computation.6 | convolution fusion | flops 8861515776 | bytes 25296896 | tf_op jit(solution)/shard_map/dot_general | solution.py:23
  622.9 25.3 %fusion.60 = f32[2048,2816]{1,0:T(8,128)} fusion(bf16[1536,2048]{1,0:T(8,128)(2,1)} %get-tuple-element.148, bf16[1536,2816]{1,0:T(8,128)(2,1)} %get-tuple-element.138), kind=kOutput, calls=%fused_computation.194 | convolution fusion | flops 17716740096 | bytes 38010880 | tf_op jit(solution)/shard_map/dot_general | solution.py:23
  655.2 24.9 %add_convert_fusion = bf16[2048,2816]{1,0:T(8,128)(2,1)S(1)} fusion(f32[2048,2816]{1,0:T(8,128)} %fusion.60, bf16[1536,2048]{1,0:T(8,128)(2,1)} %get-tuple-element.152, bf16[1536,2816]{1,0:T(8,128)(2,1)} %get-tuple-element.145), kind=kOutput, calls=%fused_computation | convolution fusion | flops 17728274432 | bytes 49545216 | tf_op jit(solution)/shard_map/dot_general | solution.py:23
  680.1 7.3 collective-permute-done.27
  689.9 3.8 fusion.23
  696.6 16.7 %add_convert_fusion.1 = bf16[2048,1408]{1,0:T(8,128)(2,1)} fusion(f32[2048,1408]{1,0:T(8,128)} %fusion.59, bf16[1536,2048]{1,0:T(8,128)(2,1)} %get-tuple-element.157, bf16[1536,1408]{1,0:T(8,128)(2,1)} %get-tuple-element.158), kind=kOutput, calls=%fused_computation.2 | convolution fusion | flops 8864137216 | bytes 27918336 | tf_op jit(solution)/shard_map/dot_general | solution.py:23
  713.3 9.8 pad_maximum_fusion
  725.0 34.3 %collective-permute-done.31.refs_1_ = bf16[384,2048]{1,0:T(8,128)(2,1)} collective-permute-done((bf16[384,2048]{1,0:T(8,128)(2,1)}, bf16[384,2048]{1,0:T(8,128)(2,1)}, u32[]{:S(2)}, u32[]{:S(2)}) %collective-permute-start.31) | collective-permute-done | bytes 1572896 | tf_op jit(solution)/shard_map/ppermute | solution.py:29
  759.3 8.0 convolution_convert_fusion
  769.4 35.1 %collective-permute-done.32 = bf16[384,2048]{1,0:T(8,128)(2,1)S(1)} collective-permute-done((bf16[384,2048]{1,0:T(8,128)(2,1)S(1)}, bf16[384,2048]{1,0:T(8,128)(2,1)S(1)}, u32[]{:S(2)}, u32[]{:S(2)}) %collective-permute-start.32) | collective-permute-done | bytes 1572896 | tf_op jit(solution)/shard_map/ppermute | solution.py:29
  807.7 8.7 convert_add_fusion.2
  816.4 15.1 %shard_map.221 = (bf16[8,64,1536]{2,1,0:T(8,128)(2,1)}, f32[8,1,1536]{2,1,0:T(1,128)}, f32[512,2048]{1,0:T(8,128)}) custom-call(s32[4]{0:T(128)} %pad_add_fusion.at_ref, bf16[384,2048]{1,0:T(8,128)(2,1)} %get-tuple-element.159.refs_0_, bf16[384,2048]{1,0:T(8,128)(2,1)} %collective-permute-done.28.refs_1_, bf16[384,2048]{1,0:T(8,128)(2,1)} %copy-done.59, ...), custom_call_target="tpu_custom_call" | custom-call | flops 1000000 | bytes 1000000 | tf_op jit(solution)/shard_map/pallas_call | solution.py:642
  832.4 34.8 %shard_map.222 = (bf16[8,64,1536]{2,1,0:T(8,128)(2,1)S(1)}, f32[1536,64]{1,0:T(8,128)S(1)}, f32[1536,64]{1,0:T(8,128)S(1)}) custom-call(s32[1]{0:T(128)} %get-tuple-element.303.len_ref, bf16[8,64,1536]{2,1,0:T(8,128)(2,1)S(1)} %copy-done.3, bf16[8,64,1536]{2,1,0:T(8,128)(2,1)} %get-tuple-element.160.grad_ref, bf16[1536,64]{1,0:T(8,128)(2,1)S(1)} %copy-done.11, ...), custom_call_target="tpu_custom_call" | custom-call | flops 786432 | bytes 4718592 | tf_op jit(solution)/shard_map/pallas_call | solution.py:232
  870.1 17.2 %shard_map.223 = (bf16[768,2048]{1,0:T(8,128)(2,1)}, bf16[768,2048]{1,0:T(8,128)(2,1)}, f32[640,2048]{1,0:T(8,128)}) custom-call(s32[4]{0:T(128)} %pad_add_fusion.at_ref, bf16[8,64,1536]{2,1,0:T(8,128)(2,1)} %copy-done.7, f32[1536,64]{1,0:T(8,128)} %copy-done.14, f32[1536,64]{1,0:T(8,128)} %copy-done.15, f32[32,1536]{1,0:T(8,128)} %get-tuple-element.292.refs_6_.refs_3_, ...), custom_call_target="tpu_custom_call" | custom-call | flops 1000000 | bytes 1000000 | tf_op jit(solution)/shard_map/pallas_call | solution.py:728
  887.9 3.6 slice.512
  893.2 3.7 collective-permute-done.35
  904.0 16.1 %shard_map.224 = (bf16[8,64,1536]{2,1,0:T(8,128)(2,1)}, f32[8,1,1536]{2,1,0:T(1,128)}, bf16[512,2048]{1,0:T(8,128)(2,1)}) custom-call(s32[4]{0:T(128)} %pad_add_fusion.at_ref, bf16[384,2048]{1,0:T(8,128)(2,1)} %get-tuple-element.174.refs_0_, bf16[384,2048]{1,0:T(8,128)(2,1)} %collective-permute-done.31.refs_1_, ...), custom_call_target="tpu_custom_call" | custom-call | flops 1000000 | bytes 1000000 | tf_op jit(solution)/shard_map/pallas_call | solution.py:642
  921.6 7.5 collective-permute-done.34
  929.0 5.5 select_reduce_fusion
  934.6 34.6 %shard_map.225 = (bf16[8,64,1536]{2,1,0:T(8,128)(2,1)S(1)}, f32[1536,64]{1,0:T(8,128)S(1)}, f32[1536,64]{1,0:T(8,128)S(1)}) custom-call(s32[1]{0:T(128)} %get-tuple-element.304.len_ref, bf16[8,64,1536]{2,1,0:T(8,128)(2,1)S(1)} %copy-done.1, bf16[8,64,1536]{2,1,0:T(8,128)(2,1)} %get-tuple-element.176.grad_ref, bf16[1536,64]{1,0:T(8,128)(2,1)S(1)} %copy-done.9, ...), custom_call_target="tpu_custom_call" | custom-call | flops 786432 | bytes 4718592 | tf_op jit(solution)/shard_map/pallas_call | solution.py:232
  969.2 4.6 slice_add_fusion.1
  973.9 18.2 %shard_map.226 = (bf16[768,2048]{1,0:T(8,128)(2,1)}, bf16[768,2048]{1,0:T(8,128)(2,1)}, bf16[8,640,256]{2,1,0:T(8,128)(2,1)}) custom-call(s32[4]{0:T(128)} %pad_add_fusion.at_ref, bf16[8,64,1536]{2,1,0:T(8,128)(2,1)} %copy-done.6, f32[1536,64]{1,0:T(8,128)} %copy-done.12, f32[1536,64]{1,0:T(8,128)} %copy-done.13, ...), custom_call_target="tpu_custom_call" | custom-call | flops 1000000 | bytes 1000000 | tf_op jit(solution)/shard_map/pallas_call | solution.py:728
  998.2 4.4 convert_add_fusion
  1009.2 17.1 %collective-permute-done.42 = bf16[4,640,256]{2,1,0:T(8,128)(2,1)S(1)} collective-permute-done((bf16[4,640,256]{2,1,0:T(8,128)(2,1)S(1)}, bf16[4,640,256]{2,1,0:T(8,128)(2,1)S(1)}, u32[]{:S(2)}, u32[]{:S(2)}) %collective-permute-start.42) | collective-permute-done | bytes 1310752 | tf_op jit(solution)/shard_map/ppermute | solution.py:29
  1026.7 5.8 collective-permute-done.45
  1034.5 4.8 collective-permute-done.41
  1039.4 4.2 fusion.28
  1043.6 3.8 fusion.46
  1065.2 13.2 %collective-permute-done.46 = bf16[1,64,2048]{2,1,0:T(8,128)(2,1)} collective-permute-done((bf16[1,64,2048]{2,1,0:T(8,128)(2,1)S(1)}, bf16[1,64,2048]{2,1,0:T(8,128)(2,1)}, u32[]{:S(2)}, u32[]{:S(2)}) %collective-permute-start.46) | collective-permute-done | bytes 262176 | tf_op jit(solution)/shard_map/ppermute | solution.py:29
  1081.7 3.6 collective-permute-done.44
  1086.3 3.6 all-to-all-start.1
  (410 shorter events, 173.4 us)
Async XLA Ops:
  11.9 11.7 %all-to-all-start = ((bf16[4,64,768]{2,1,0:T(8,128)(2,1)}), bf16[4,64,768]{2,1,0:T(8,128)(2,1)S(1)}, u32[]{:S(2)}, u32[]{:S(2)}) async-start(bf16[4,64,768]{2,1,0:T(8,128)(2,1)} %pad_maximum_fusion.4), calls=%async_computation | async-start | bytes 786432 | tf_op jit(solution)/shard_map/all_to_all | solution.py:798
  16.1 113.5 %all-gather.4.cloned.1.call-start = ((), (), s32[]{:S(2)}) async-start(), calls=%async_computation.3 | async-start | bytes 5898240 | tf_op jit(solution)/shard_map/all_gather | solution.py:805
  16.1 0.7 collective-permute-start.4
  25.5 205.6 %all-gather.6.cloned.1.call-start = ((), (), s32[]{:S(2)}) async-start(), calls=%async_computation.4 | async-start | bytes 6488064 | tf_op jit(solution)/shard_map/all_gather | solution.py:813
  27.9 419.6 %all-gather.8.cloned.1.call-start = ((), (), s32[]{:S(2)}) async-start(), calls=%async_computation.5 | async-start | bytes 12976128 | tf_op jit(solution)/shard_map/all_gather | solution.py:815
  43.4 87.8 %copy-start.75 = (s32[2]{0:T(128)S(1)}, s32[2]{0:T(128)}, u32[]{:S(2)}) copy-start(s32[2]{0:T(128)} %param.14) | copy-start | bytes 28
  45.5 84.1 %collective-permute-start = (bf16[384,2048]{1,0:T(8,128)(2,1)}, bf16[384,2048]{1,0:T(8,128)(2,1)}, u32[]{:S(2)}, u32[]{:S(2)}) collective-permute-start(bf16[384,2048]{1,0:T(8,128)(2,1)} %get-tuple-element.106.refs_0_), channel_id=1, source_target_pairs={{0,2},{1,3},{2,0},{3,1},{4,6},{5,7},{6,4},{7,5},{8,10},{9,11},{10,... | collective-permute-start | bytes 4718600 | tf_op jit(solution)/shard_map/ppermute | solution.py:29
  129.6 925.9 %reduce-scatter.2.cloned.1.call-start = ((), (), s32[]{:S(2)}) async-start(), calls=%async_computation.6 | async-start | bytes 19464192 | tf_op jit(solution)/shard_map/reduce_scatter | solution.py:928
  129.7 35.7 %collective-permute-start.1 = (bf16[384,2048]{1,0:T(8,128)(2,1)}, bf16[384,2048]{1,0:T(8,128)(2,1)}, u32[]{:S(2)}, u32[]{:S(2)}) collective-permute-start(bf16[384,2048]{1,0:T(8,128)(2,1)} %get-tuple-element.115.refs_0_), channel_id=1, source_target_pairs={{0,2},{1,3},{2,0},{3,1},{4,6},{5,7},{6,4},{7,5},{8,10},{9,11},{10,... | collective-permute-start | bytes 4718600 | tf_op jit(solution)/shard_map/ppermute | solution.py:29
  136.2 51.8 %collective-permute-start.2 = (bf16[384,2048]{1,0:T(8,128)(2,1)}, bf16[384,2048]{1,0:T(8,128)(2,1)}, u32[]{:S(2)}, u32[]{:S(2)}) collective-permute-start(bf16[384,2048]{1,0:T(8,128)(2,1)} %get-tuple-element.106.refs_0_), channel_id=1, source_target_pairs={{0,1},{1,0},{2,3},{3,2},{4,5},{5,4},{6,7},{7,6},{8,9},{9,8},{10,11... | collective-permute-start | bytes 4718600 | tf_op jit(solution)/shard_map/ppermute | solution.py:29
  136.2 51.8 %collective-permute-start.3 = (bf16[384,2048]{1,0:T(8,128)(2,1)}, bf16[384,2048]{1,0:T(8,128)(2,1)}, u32[]{:S(2)}, u32[]{:S(2)}) collective-permute-start(bf16[384,2048]{1,0:T(8,128)(2,1)} %collective-permute-done.refs_1_), channel_id=1, source_target_pairs={{0,1},{1,0},{2,3},{3,2},{4,5},{5,4},{6,7},{7,6},{8,9},{9,8},{10,11... | collective-permute-start | bytes 4718600 | tf_op jit(solution)/shard_map/ppermute | solution.py:29
  165.3 65.8 %collective-permute-start.5 = (bf16[384,2048]{1,0:T(8,128)(2,1)}, bf16[384,2048]{1,0:T(8,128)(2,1)}, u32[]{:S(2)}, u32[]{:S(2)}) collective-permute-start(bf16[384,2048]{1,0:T(8,128)(2,1)} %get-tuple-element.111.refs_0_), channel_id=1, source_target_pairs={{0,2},{1,3},{2,0},{3,1},{4,6},{5,7},{6,4},{7,5},{8,10},{9,11},{10,... | collective-permute-start | bytes 4718600 | tf_op jit(solution)/shard_map/ppermute | solution.py:29
  239.0 9.7 collective-permute-start.6
  239.0 15.9 %collective-permute-start.8 = (bf16[384,2048]{1,0:T(8,128)(2,1)S(1)}, bf16[384,2048]{1,0:T(8,128)(2,1)S(1)}, u32[]{:S(2)}, u32[]{:S(2)}) collective-permute-start(bf16[384,2048]{1,0:T(8,128)(2,1)S(1)} %copy-done.45), channel_id=1, source_target_pairs={{0,1},{1,0},{2,3},{3,2},{4,5},{5,4},{6,7},{7,6},{8,9},{9,8},{10,11... | collective-permute-start | bytes 4718600 | tf_op jit(solution)/shard_map/ppermute | solution.py:29
  239.5 16.5 %collective-permute-start.9 = (bf16[384,2048]{1,0:T(8,128)(2,1)}, bf16[384,2048]{1,0:T(8,128)(2,1)}, u32[]{:S(2)}, u32[]{:S(2)}) collective-permute-start(bf16[384,2048]{1,0:T(8,128)(2,1)} %collective-permute-done.1.refs_1_), channel_id=1, source_target_pairs={{0,1},{1,0},{2,3},{3,2},{4,5},{5,4},{6,7},{7,6},{8,9},{9,8},{10,11... | collective-permute-start | bytes 4718600 | tf_op jit(solution)/shard_map/ppermute | solution.py:29
  254.7 43.4 %collective-permute-start.7 = (bf16[384,2048]{1,0:T(8,128)(2,1)S(1)}, bf16[384,2048]{1,0:T(8,128)(2,1)S(1)}, u32[]{:S(2)}, u32[]{:S(2)}) collective-permute-start(bf16[384,2048]{1,0:T(8,128)(2,1)S(1)} %slice.517), channel_id=1, source_target_pairs={{0,2},{1,3},{2,0},{3,1},{4,6},{5,7},{6,4},{7,5},{8,10},{9,11},{10,... | collective-permute-start | bytes 4718600 | tf_op jit(solution)/shard_map/ppermute | solution.py:29
  302.7 91.4 %copy-start.46 = (bf16[384,2048]{1,0:T(8,128)(2,1)}, bf16[384,2048]{1,0:T(8,128)(2,1)S(1)}, u32[]{:S(2)}) copy-start(bf16[384,2048]{1,0:T(8,128)(2,1)S(1)} %multiply_convert_fusion.3.refs_0_) | copy-start | bytes 4718596
  302.7 36.5 %collective-permute-start.10 = (bf16[384,2048]{1,0:T(8,128)(2,1)S(1)}, bf16[384,2048]{1,0:T(8,128)(2,1)}, u32[]{:S(2)}, u32[]{:S(2)}) collective-permute-start(bf16[384,2048]{1,0:T(8,128)(2,1)S(1)} %multiply_convert_fusion.3.refs_0_), channel_id=1, source_target_pairs={{0,2},{1,3},{2,0},{3,1},{4,6},{5,7},{6,4},{7,5},{8,10},{9,11},{10,... | collective-permute-start | bytes 4718600 | tf_op jit(solution)/shard_map/ppermute | solution.py:29
  346.4 5.9 collective-permute-start.11
  355.6 37.4 %collective-permute-start.14 = (bf16[384,2048]{1,0:T(8,128)(2,1)S(1)}, bf16[384,2048]{1,0:T(8,128)(2,1)}, u32[]{:S(2)}, u32[]{:S(2)}) collective-permute-start(bf16[384,2048]{1,0:T(8,128)(2,1)S(1)} %copy-done.44), channel_id=1, source_target_pairs={{0,2},{1,3},{2,0},{3,1},{4,6},{5,7},{6,4},{7,5},{8,10},{9,11},{10,... | collective-permute-start | bytes 4718600 | tf_op jit(solution)/shard_map/ppermute | solution.py:29
  357.4 35.6 %collective-permute-start.12 = (bf16[384,2048]{1,0:T(8,128)(2,1)}, bf16[384,2048]{1,0:T(8,128)(2,1)S(1)}, u32[]{:S(2)}, u32[]{:S(2)}) collective-permute-start(bf16[384,2048]{1,0:T(8,128)(2,1)} %get-tuple-element.111.refs_0_), channel_id=1, source_target_pairs={{0,1},{1,0},{2,3},{3,2},{4,5},{5,4},{6,7},{7,6},{8,9},{9,8},{10,11... | collective-permute-start | bytes 4718600 | tf_op jit(solution)/shard_map/ppermute | solution.py:29
  357.4 36.7 %collective-permute-start.13 = (bf16[384,2048]{1,0:T(8,128)(2,1)}, bf16[384,2048]{1,0:T(8,128)(2,1)S(1)}, u32[]{:S(2)}, u32[]{:S(2)}) collective-permute-start(bf16[384,2048]{1,0:T(8,128)(2,1)} %collective-permute-done.5.refs_1_), channel_id=1, source_target_pairs={{0,1},{1,0},{2,3},{3,2},{4,5},{5,4},{6,7},{7,6},{8,9},{9,8},{10,11... | collective-permute-start | bytes 4718600 | tf_op jit(solution)/shard_map/ppermute | solution.py:29
  358.5 67.5 %collective-permute-start.19 = (bf16[384,2048]{1,0:T(8,128)(2,1)S(1)}, bf16[384,2048]{1,0:T(8,128)(2,1)}, u32[]{:S(2)}, u32[]{:S(2)}) collective-permute-start(bf16[384,2048]{1,0:T(8,128)(2,1)S(1)} %slice.516), channel_id=1, source_target_pairs={{0,2},{1,3},{2,0},{3,1},{4,6},{5,7},{6,4},{7,5},{8,10},{9,11},{10,... | collective-permute-start | bytes 4718600 | tf_op jit(solution)/shard_map/ppermute | solution.py:29
  360.3 70.4 %collective-permute-start.15 = (bf16[384,2048]{1,0:T(8,128)(2,1)S(1)}, bf16[384,2048]{1,0:T(8,128)(2,1)}, u32[]{:S(2)}, u32[]{:S(2)}) collective-permute-start(bf16[384,2048]{1,0:T(8,128)(2,1)S(1)} %copy-done.44), channel_id=1, source_target_pairs={{0,1},{1,0},{2,3},{3,2},{4,5},{5,4},{6,7},{7,6},{8,9},{9,8},{10,11... | collective-permute-start | bytes 4718600 | tf_op jit(solution)/shard_map/ppermute | solution.py:29
  393.0 37.7 %collective-permute-start.16 = (bf16[384,2048]{1,0:T(8,128)(2,1)}, bf16[384,2048]{1,0:T(8,128)(2,1)}, u32[]{:S(2)}, u32[]{:S(2)}) collective-permute-start(bf16[384,2048]{1,0:T(8,128)(2,1)} %collective-permute-done.14.refs_1_), channel_id=1, source_target_pairs={{0,1},{1,0},{2,3},{3,2},{4,5},{5,4},{6,7},{7,6},{8,9},{9,8},{10,11... | collective-permute-start | bytes 4718600 | tf_op jit(solution)/shard_map/ppermute | solution.py:29
  393.0 54.5 %collective-permute-start.18 = (bf16[384,2048]{1,0:T(8,128)(2,1)}, bf16[384,2048]{1,0:T(8,128)(2,1)}, u32[]{:S(2)}, u32[]{:S(2)}) collective-permute-start(bf16[384,2048]{1,0:T(8,128)(2,1)} %collective-permute-done.10.refs_1_), channel_id=1, source_target_pairs={{0,1},{1,0},{2,3},{3,2},{4,5},{5,4},{6,7},{7,6},{8,9},{9,8},{10,11... | collective-permute-start | bytes 4718600 | tf_op jit(solution)/shard_map/ppermute | solution.py:29
  395.3 52.1 %collective-permute-start.17 = (bf16[384,2048]{1,0:T(8,128)(2,1)S(1)}, bf16[384,2048]{1,0:T(8,128)(2,1)}, u32[]{:S(2)}, u32[]{:S(2)}) collective-permute-start(bf16[384,2048]{1,0:T(8,128)(2,1)S(1)} %multiply_convert_fusion.3.refs_0_), channel_id=1, source_target_pairs={{0,1},{1,0},{2,3},{3,2},{4,5},{5,4},{6,7},{7,6},{8,9},{9,8},{10,11... | collective-permute-start | bytes 4718600 | tf_op jit(solution)/shard_map/ppermute | solution.py:29
  452.4 94.9 %collective-permute-start.23 = (bf16[384,2048]{1,0:T(8,128)(2,1)}, bf16[384,2048]{1,0:T(8,128)(2,1)}, u32[]{:S(2)}, u32[]{:S(2)}) collective-permute-start(bf16[384,2048]{1,0:T(8,128)(2,1)} %multiply_convert_fusion.2.refs_0_), channel_id=1, source_target_pairs={{0,1},{1,0},{2,3},{3,2},{4,5},{5,4},{6,7},{7,6},{8,9},{9,8},{10,11... | collective-permute-start | bytes 4718600 | tf_op jit(solution)/shard_map/ppermute | solution.py:29
  452.4 68.9 %collective-permute-start.21 = (bf16[384,2048]{1,0:T(8,128)(2,1)}, bf16[384,2048]{1,0:T(8,128)(2,1)}, u32[]{:S(2)}, u32[]{:S(2)}) collective-permute-start(bf16[384,2048]{1,0:T(8,128)(2,1)} %multiply_convert_fusion.2.refs_0_), channel_id=1, source_target_pairs={{0,2},{1,3},{2,0},{3,1},{4,6},{5,7},{6,4},{7,5},{8,10},{9,11},{10,... | collective-permute-start | bytes 4718600 | tf_op jit(solution)/shard_map/ppermute | solution.py:29
  490.7 30.8 %collective-permute-start.20 = (bf16[768,2048]{1,0:T(8,128)(2,1)}, bf16[768,2048]{1,0:T(8,128)(2,1)}, u32[]{:S(2)}, u32[]{:S(2)}) collective-permute-start(bf16[768,2048]{1,0:T(8,128)(2,1)} %convolution_convert_fusion.1), channel_id=1, source_target_pairs={{0,1},{1,0},{2,3},{3,2},{4,5},{5,4},{6,7},{7,6},{8,9},{9,8},{10,11... | collective-permute-start | bytes 9437192 | tf_op jit(solution)/shard_map/ppermute | solution.py:29
  504.1 27.6 %collective-permute-start.22 = (bf16[768,2048]{1,0:T(8,128)(2,1)}, bf16[768,2048]{1,0:T(8,128)(2,1)}, u32[]{:S(2)}, u32[]{:S(2)}) collective-permute-start(bf16[768,2048]{1,0:T(8,128)(2,1)} %fusion.12), channel_id=1, source_target_pairs={{0,1},{1,0},{2,3},{3,2},{4,5},{5,4},{6,7},{7,6},{8,9},{9,8},{10,11... | collective-permute-start | bytes 9437192 | tf_op jit(solution)/shard_map/ppermute | solution.py:29
  521.2 26.0 %collective-permute-start.24 = (bf16[384,2048]{1,0:T(8,128)(2,1)}, bf16[384,2048]{1,0:T(8,128)(2,1)}, u32[]{:S(2)}, u32[]{:S(2)}) collective-permute-start(bf16[384,2048]{1,0:T(8,128)(2,1)} %collective-permute-done.21.refs_1_), channel_id=1, source_target_pairs={{0,1},{1,0},{2,3},{3,2},{4,5},{5,4},{6,7},{7,6},{8,9},{9,8},{10,11... | collective-permute-start | bytes 4718600 | tf_op jit(solution)/shard_map/ppermute | solution.py:29
  546.9 36.7 %collective-permute-start.25 = (bf16[384,2048]{1,0:T(8,128)(2,1)S(1)}, bf16[384,2048]{1,0:T(8,128)(2,1)}, u32[]{:S(2)}, u32[]{:S(2)}) collective-permute-start(bf16[384,2048]{1,0:T(8,128)(2,1)S(1)} %slice.515), channel_id=1, source_target_pairs={{0,2},{1,3},{2,0},{3,1},{4,6},{5,7},{6,4},{7,5},{8,10},{9,11},{10,... | collective-permute-start | bytes 4718600 | tf_op jit(solution)/shard_map/ppermute | solution.py:29
  602.2 7.3 collective-permute-start.26
  609.1 39.1 %collective-permute-start.28 = (bf16[384,2048]{1,0:T(8,128)(2,1)}, bf16[384,2048]{1,0:T(8,128)(2,1)}, u32[]{:S(2)}, u32[]{:S(2)}) collective-permute-start(bf16[384,2048]{1,0:T(8,128)(2,1)} %get-tuple-element.159.refs_0_), channel_id=1, source_target_pairs={{0,2},{1,3},{2,0},{3,1},{4,6},{5,7},{6,4},{7,5},{8,10},{9,11},{10,... | collective-permute-start | bytes 4718600 | tf_op jit(solution)/shard_map/ppermute | solution.py:29
  648.2 4.4 collective-permute-start.29
  648.4 5.6 collective-permute-start.30
  650.8 36.6 %collective-permute-start.27 = (bf16[384,2048]{1,0:T(8,128)(2,1)S(1)}, bf16[384,2048]{1,0:T(8,128)(2,1)S(1)}, u32[]{:S(2)}, u32[]{:S(2)}) collective-permute-start(bf16[384,2048]{1,0:T(8,128)(2,1)S(1)} %slice.514), channel_id=1, source_target_pairs={{0,2},{1,3},{2,0},{3,1},{4,6},{5,7},{6,4},{7,5},{8,10},{9,11},{10,... | collective-permute-start | bytes 4718600 | tf_op jit(solution)/shard_map/ppermute | solution.py:29
  723.2 44.2 %slice-start.8 = ((s8[6291456]{0:T(1024)(128)(4,1)}), s8[4194304]{0:T(1024)(128)(4,1)S(1)}, s32[]{:S(2)}) async-start(s8[6291456]{0:T(1024)(128)(4,1)} %bitcast.168), calls=%async_computation.15 | async-start | bytes 8388608
  723.2 44.2 %slice-start.9 = ((s8[6291456]{0:T(1024)(128)(4,1)}), s8[2097152]{0:T(1024)(128)(4,1)S(1)}, s32[]{:S(2)}) async-start(s8[6291456]{0:T(1024)(128)(4,1)} %bitcast.168), calls=%async_computation.16 | async-start | bytes 4194304
  723.2 36.1 %collective-permute-start.31 = (bf16[384,2048]{1,0:T(8,128)(2,1)}, bf16[384,2048]{1,0:T(8,128)(2,1)}, u32[]{:S(2)}, u32[]{:S(2)}) collective-permute-start(bf16[384,2048]{1,0:T(8,128)(2,1)} %get-tuple-element.174.refs_0_), channel_id=1, source_target_pairs={{0,2},{1,3},{2,0},{3,1},{4,6},{5,7},{6,4},{7,5},{8,10},{9,11},{10,... | collective-permute-start | bytes 4718600 | tf_op jit(solution)/shard_map/ppermute | solution.py:29
  767.3 40.3 %collective-permute-start.33 = (bf16[768,2048]{1,0:T(8,128)(2,1)S(1)}, bf16[768,2048]{1,0:T(8,128)(2,1)S(1)}, u32[]{:S(2)}, u32[]{:S(2)}) collective-permute-start(bf16[768,2048]{1,0:T(8,128)(2,1)S(1)} %convolution_convert_fusion), channel_id=1, source_target_pairs={{0,1},{1,0},{2,3},{3,2},{4,5},{5,4},{6,7},{7,6},{8,9},{9,8},{10,11... | collective-permute-start | bytes 9437192 | tf_op jit(solution)/shard_map/ppermute | solution.py:29
  767.4 40.2 %slice-start.6 = ((s8[5767168]{0:T(1024)(128)(4,1)}), s8[4194304]{0:T(1024)(128)(4,1)S(1)}, s32[]{:S(2)}) async-start(s8[5767168]{0:T(1024)(128)(4,1)} %bitcast.162), calls=%async_computation.13 | async-start | bytes 8388608
  767.7 36.8 %collective-permute-start.32 = (bf16[384,2048]{1,0:T(8,128)(2,1)S(1)}, bf16[384,2048]{1,0:T(8,128)(2,1)S(1)}, u32[]{:S(2)}, u32[]{:S(2)}) collective-permute-start(bf16[384,2048]{1,0:T(8,128)(2,1)S(1)} %slice.513), channel_id=1, source_target_pairs={{0,2},{1,3},{2,0},{3,1},{4,6},{5,7},{6,4},{7,5},{8,10},{9,11},{10,... | collective-permute-start | bytes 4718600 | tf_op jit(solution)/shard_map/ppermute | solution.py:29
  887.3 9.6 collective-permute-start.35
  887.3 16.7 %collective-permute-start.37 = (bf16[384,2048]{1,0:T(8,128)(2,1)}, bf16[384,2048]{1,0:T(8,128)(2,1)}, u32[]{:S(2)}, u32[]{:S(2)}) collective-permute-start(bf16[384,2048]{1,0:T(8,128)(2,1)} %get-tuple-element.174.refs_0_), channel_id=1, source_target_pairs={{0,1},{1,0},{2,3},{3,2},{4,5},{5,4},{6,7},{7,6},{8,9},{9,8},{10,11... | collective-permute-start | bytes 4718600 | tf_op jit(solution)/shard_map/ppermute | solution.py:29
  887.8 16.2 %collective-permute-start.38 = (bf16[384,2048]{1,0:T(8,128)(2,1)}, bf16[384,2048]{1,0:T(8,128)(2,1)}, u32[]{:S(2)}, u32[]{:S(2)}) collective-permute-start(bf16[384,2048]{1,0:T(8,128)(2,1)} %collective-permute-done.31.refs_1_), channel_id=1, source_target_pairs={{0,1},{1,0},{2,3},{3,2},{4,5},{5,4},{6,7},{7,6},{8,9},{9,8},{10,11... | collective-permute-start | bytes 4718600 | tf_op jit(solution)/shard_map/ppermute | solution.py:29
  891.5 37.6 %collective-permute-start.34 = (bf16[384,2048]{1,0:T(8,128)(2,1)}, bf16[384,2048]{1,0:T(8,128)(2,1)}, u32[]{:S(2)}, u32[]{:S(2)}) collective-permute-start(bf16[384,2048]{1,0:T(8,128)(2,1)} %slice.512), channel_id=1, source_target_pairs={{0,2},{1,3},{2,0},{3,1},{4,6},{5,7},{6,4},{7,5},{8,10},{9,11},{10,... | collective-permute-start | bytes 4718600 | tf_op jit(solution)/shard_map/ppermute | solution.py:29
  902.4 66.9 %collective-permute-start.36 = (bf16[384,2048]{1,0:T(8,128)(2,1)}, bf16[384,2048]{1,0:T(8,128)(2,1)}, u32[]{:S(2)}, u32[]{:S(2)}) collective-permute-start(bf16[384,2048]{1,0:T(8,128)(2,1)} %slice.511), channel_id=1, source_target_pairs={{0,2},{1,3},{2,0},{3,1},{4,6},{5,7},{6,4},{7,5},{8,10},{9,11},{10,... | collective-permute-start | bytes 4718600 | tf_op jit(solution)/shard_map/ppermute | solution.py:29
  921.5 52.4 %collective-permute-start.39 = (bf16[4,64,2048]{2,1,0:T(8,128)(2,1)S(1)}, bf16[4,64,2048]{2,1,0:T(8,128)(2,1)}, u32[]{:S(2)}, u32[]{:S(2)}) collective-permute-start(bf16[4,64,2048]{2,1,0:T(8,128)(2,1)S(1)} %dynamic-slice_bitcast_fusion.1), channel_id=1, source_target_pairs={{0,4},{4,0},{8,12},{12,8},{16,20},{20,16},{24,28},{28,24},{1,5},{5... | collective-permute-start | bytes 3145736 | tf_op jit(solution)/shard_map/ppermute | solution.py:29
  929.0 40.2 %copy-start.36 = (f32[768,2048]{1,0:T(8,128)S(1)}, f32[768,2048]{1,0:T(8,128)}, u32[]{:S(2)}) copy-start(f32[768,2048]{1,0:T(8,128)} %copy-done.35) | copy-start | bytes 18874372
  992.1 6.1 collective-permute-start.40
  995.2 31.1 %collective-permute-start.42 = (bf16[4,640,256]{2,1,0:T(8,128)(2,1)S(1)}, bf16[4,640,256]{2,1,0:T(8,128)(2,1)S(1)}, u32[]{:S(2)}, u32[]{:S(2)}) collective-permute-start(bf16[4,640,256]{2,1,0:T(8,128)(2,1)S(1)} %dynamic-slice_bitcast_fusion), channel_id=1, source_target_pairs={{0,4},{4,0},{8,12},{12,8},{16,20},{20,16},{24,28},{28,24},{1,5},{5... | collective-permute-start | bytes 3932168 | tf_op jit(solution)/shard_map/ppermute | solution.py:29
  1002.8 36.6 %collective-permute-start.41 = (bf16[384,2048]{1,0:T(8,128)(2,1)S(1)}, bf16[384,2048]{1,0:T(8,128)(2,1)}, u32[]{:S(2)}, u32[]{:S(2)}) collective-permute-start(bf16[384,2048]{1,0:T(8,128)(2,1)S(1)} %slice.510), channel_id=1, source_target_pairs={{0,2},{1,3},{2,0},{3,1},{4,6},{5,7},{6,4},{7,5},{8,10},{9,11},{10,... | collective-permute-start | bytes 4718600 | tf_op jit(solution)/shard_map/ppermute | solution.py:29
  1006.3 26.1 %collective-permute-start.45 = (bf16[2,64,2048]{2,1,0:T(8,128)(2,1)S(1)}, bf16[2,64,2048]{2,1,0:T(8,128)(2,1)S(1)}, u32[]{:S(2)}, u32[]{:S(2)}) collective-permute-start(bf16[2,64,2048]{2,1,0:T(8,128)(2,1)S(1)} %dynamic-slice_bitcast_fusion.3), channel_id=1, source_target_pairs={{0,8},{4,12},{8,0},{12,4},{16,24},{20,28},{24,16},{28,20},{1,9},{5... | collective-permute-start | bytes 1572872 | tf_op jit(solution)/shard_map/ppermute | solution.py:29
  1033.3 22.2 %collective-permute-start.43 = (bf16[2,640,256]{2,1,0:T(8,128)(2,1)}, bf16[2,640,256]{2,1,0:T(8,128)(2,1)}, u32[]{:S(2)}, u32[]{:S(2)}) collective-permute-start(bf16[2,640,256]{2,1,0:T(8,128)(2,1)} %dynamic-slice_bitcast_fusion.2), channel_id=1, source_target_pairs={{0,8},{4,12},{8,0},{12,4},{16,24},{20,28},{24,16},{28,20},{1,9},{5... | collective-permute-start | bytes 1966088 | tf_op jit(solution)/shard_map/ppermute | solution.py:29
  1043.6 7.7 collective-permute-start.50
  1051.3 3.6 collective-permute-start.51
  1057.0 21.4 %collective-permute-start.46 = (bf16[1,64,2048]{2,1,0:T(8,128)(2,1)S(1)}, bf16[1,64,2048]{2,1,0:T(8,128)(2,1)}, u32[]{:S(2)}, u32[]{:S(2)}) collective-permute-start(bf16[1,64,2048]{2,1,0:T(8,128)(2,1)S(1)} %constant_dynamic-slice_fusion.4), channel_id=1, source_target_pairs={{0,16},{4,20},{8,24},{12,28},{16,0},{20,4},{24,8},{28,12},{1,17},{... | collective-permute-start | bytes 786440 | tf_op jit(solution)/shard_map/ppermute | solution.py:29
  1062.1 1.4 collective-permute-start.48
  1062.2 23.1 %collective-permute-start.44 = (bf16[1,640,256]{2,1,0:T(8,128)(2,1)S(1)}, bf16[1,640,256]{2,1,0:T(8,128)(2,1)S(1)}, u32[]{:S(2)}, u32[]{:S(2)}) collective-permute-start(bf16[1,640,256]{2,1,0:T(8,128)(2,1)S(1)} %constant_dynamic-slice_fusion.5), channel_id=1, source_target_pairs={{0,16},{4,20},{8,24},{12,28},{16,0},{20,4},{24,8},{28,12},{1,17},{... | collective-permute-start | bytes 983048 | tf_op jit(solution)/shard_map/ppermute | solution.py:29
  1063.5 29.4 %collective-permute-start.49 = (f32[1,64]{1,0:T(1,128)S(1)}, f32[1,64]{1,0:T(1,128)S(1)}, u32[]{:S(2)}, u32[]{:S(2)}) collective-permute-start(f32[1,64]{1,0:T(1,128)S(1)} %constant_dynamic-slice_fusion), channel_id=1, source_target_pairs={{0,2},{1,3},{2,0},{3,1},{4,6},{5,7},{6,4},{7,5},{8,10},{9,11},{10,... | collective-permute-start | bytes 776 | tf_op jit(solution)/shard_map/ppermute | solution.py:29
  1080.1 13.3 %collective-permute-start.47 = (bf16[64,2048]{1,0:T(8,128)(2,1)}, bf16[64,2048]{1,0:T(8,128)(2,1)S(1)}, u32[]{:S(2)}, u32[]{:S(2)}) collective-permute-start(bf16[64,2048]{1,0:T(8,128)(2,1)} %fusion.49), channel_id=1, source_target_pairs={{0,0},{4,1},{8,2},{12,3},{16,4},{20,5},{24,6},{28,7},{1,8},{5,9},{... | collective-permute-start | bytes 786440 | tf_op jit(solution)/shard_map/ppermute | solution.py:985
  1086.3 10.3 all-to-all-start.1
  (86 other events, 721.7 us)
Sparse Core Ops, SparseCore 0:
  25.7 103.8 all-gather.3
  132.3 90.8 all-gather.5
  226.0 161.8 all-gather.7
  723.3 309.2 reduce-scatter.1

commit v3 on v2

--- a/solution.py
+++ b/solution.py
@@ -865,13 +865,14 @@
             flat = after(flat, *cot_far[0], down_t)
         else:
             take_branch(s - 1, att)
-            flat = after(flat, *n2_far[-1])
         begins.append(reduce_pair(*merge_heads(flat, at, out_w, sp), sp))
         saved.append((q, k, k_t, v, att, lse))
     for s in range(1, seqs):
         cot_far.append(spread(after(cot_local[s], begins[-1]), sp, "sp", 2))
-    hidden_grads, cot_all = zip(*[hidden_grad(spread(far, sp), down_t) for far in cot_far])
-    gu_w = after(gu_w, *hidden_grads)
+    cot_parts = [spread(far, sp) for far in cot_far]
+    first = [after(part, begins[-1], *n2_far[0]) for part in cot_parts[0]]
+    hidden_grads, cot_all = [[member] for member in hidden_grad(first, down_t)]
+    gu_w = after(gu_w, hidden_grads[0])
     take_branch(seqs - 1, gu_w)
     begun = begins[-1]
     normed_two = [spread(n2_far[0], sp)]
@@ -883,13 +884,16 @@
     hiddens, gu_grads, n2_grads, middle_grads, grad_rows = [], [], [], [], []
     down_wgrad = 0.0
     for s in range(seqs):
-        n2 = [after(part, begun, *hidden_grads) for part in normed_two[s]]
+        n2 = [after(part, begun, hidden_grads[s]) for part in normed_two[s]]
         hid, gu_grad, joined = feed(n2, gu_w, hidden_grads[s])
         normed_two[s] = joined
         hiddens.append(hid)
         gu_grads.append(gu_grad)
         if s < seqs - 1:
             low, high = [n2_far[s + 1][0]], n2_far[s + 1]
+            parts = [after(part, gu_grad, *low) for part in cot_parts[s + 1]]
+            for array, made in zip((hidden_grads, cot_all), hidden_grad(parts, down_t)):
+                array.append(made)
             hid = after(hid, *low)
             down_wgrad = row_major(dot(cot_all[s], hid, 0, 0))
             begun_mixed.append(mlp_near(hid))

time: 1110 us -> 1120 us (level)
  waiting for transfers between devices: 346 us -> 383 us
  starting transfers between devices: 56.9 us -> 37.4 us
    ppermute x50, waiting for transfers between devices: 272 us -> 292 us  [swap(): return lax.ppermute(values, axis, [(i, i ^ bit) for i in range(count)])]
    ppermute x50, starting transfers between devices: 46.7 us -> 27.2 us  [swap(): return lax.ppermute(values, axis, [(i, i ^ bit) for i in range(count)])]
    all_gather x1, waiting for transfers between devices: 65.7 us -> 82.2 us  [body(): lax.all_gather(row_major(attn_mine), 'dp', axis=0, tiled=True)]
    unnamed x205 -> x201, local copies, waits for them, and re-layouts: 51.3 us -> 52.4 us
  transfers between devices with their start and end apart: 58 -> 58, of which waited for: 23 -> 24; matrix products, arithmetic and copies ran while one was open for 25% -> 25% of each run, Pallas kernels for 29% -> 28%
where the time goes in v3:
time: 1120 us
  waiting for transfers between devices  383 us (34%)
  Pallas kernels  317 us (28%)
  matrix products  175 us (16%)
  other arithmetic  97.5 us (9%)
  local copies, waits for them, and re-layouts  92.9 us (8%)
  starting transfers between devices  37.4 us (3%)
  between operations  16.2 us (1%)
    ppermute x50, waiting for transfers between devices, swap(): return lax.ppermute(values, axis, [(i, i ^ bit) for i in range(count)])  292 us
    dot_general x12, matrix products, dot(): lax.dot_general(left, right, (((left_dim,), (right_dim,)), ((), ())), pre...  175 us
    all_gather x1, waiting for transfers between devices, body(): lax.all_gather(row_major(attn_mine), 'dp', axis=0, tiled=True)  82.2 us
    pallas_call x2, Pallas kernels, attend_backward(): pl.pallas_call(functools.partial(backward_kernel, block), grid=(heads,),...  69.2 us
    pallas_call x2, Pallas kernels, feed(): pl.pallas_call(functools.partial(feed_kernel, pieces[-1][1] - pieces[-1][...  54.8 us
    unnamed x201, local copies, waits for them, and re-layouts  52.4 us
    pallas_call x2, Pallas kernels, attend_forward(): pl.pallas_call(functools.partial(forward_kernel, block), grid=(heads,), i...  51.3 us
    pallas_call x2, Pallas kernels, return_rows(): pl.pallas_call(functools.partial(return_kernel, blocks, last), in_specs=[...  35.3 us
  transfers between devices with their start and end apart: 58, of which 24 were waited for; matrix products, arithmetic and copies ran while one was open for 25% of the time, Pallas kernels for 28%

profile of v3, /device:TPU:0, one launch (start us, length us, event | category | flops | bytes accessed | tf_op | source)
XLA Modules:
  0.0 1119.0 jit_solution(5236724971756574138)
XLA Ops:
  11.9 4.2 all-to-all-start
  17.0 6.6 all-to-all-done
  45.6 82.2 %all-gather.4.cloned.1.call-done = bf16[2048,1280]{1,0:T(8,128)(2,1)} async-done(((bf16[256,1280]{1,0:T(8,128)(2,1)}), bf16[2048,1280]{1,0:T(8,128)(2,1)}) %all-gather.4.cloned.1.call-update) | async-done | bytes 5242896 | tf_op jit(solution)/shard_map/all_gather | solution.py:805
  132.8 34.1 %collective-permute-done.refs_1_ = bf16[384,2048]{1,0:T(8,128)(2,1)} collective-permute-done((bf16[384,2048]{1,0:T(8,128)(2,1)}, bf16[384,2048]{1,0:T(8,128)(2,1)}, u32[]{:S(2)}, u32[]{:S(2)}) %collective-permute-start) | collective-permute-done | bytes 1572896 | tf_op jit(solution)/shard_map/ppermute | solution.py:29
  173.7 27.9 %collective-permute-done.1.refs_1_ = bf16[384,2048]{1,0:T(8,128)(2,1)} collective-permute-done((bf16[384,2048]{1,0:T(8,128)(2,1)}, bf16[384,2048]{1,0:T(8,128)(2,1)}, u32[]{:S(2)}, u32[]{:S(2)}) %collective-permute-start.1) | collective-permute-done | bytes 1572896 | tf_op jit(solution)/shard_map/ppermute | solution.py:29
  205.8 3.0 slice.362
  208.8 4.8 reshape.260.w_ref.refs_4_
  213.7 3.5 slice.360
  217.1 4.5 copy.71
  224.2 12.9 %shard_map.211 = (bf16[1536,2048]{1,0:T(8,128)(2,1)}, bf16[8,64,1536]{2,1,0:T(8,128)(2,1)}, bf16[64,1536]{1,0:T(8,128)(2,1)}, bf16[64,1536]{1,0:T(8,128)(2,1)}, ...) custom-call(s32[4]{0:T(128)} %pad_add_fusion.at_ref, bf16[384,2048]{1,0:T(8,128)(2,1)} %get-tuple-element.113.refs_0_, ...), custom_call_target="tpu_custom_call" | custom-call | flops 1000000 | bytes 1000000 | tf_op jit(solution)/shard_map/pallas_call | solution.py:549
  240.5 25.5 %shard_map.212 = (bf16[8,64,1536]{2,1,0:T(8,128)(2,1)S(1)}, f32[8,1,1536]{2,1,0:T(1,128)S(1)}) custom-call(s32[1]{0:T(128)} %get-tuple-element.317.len_ref, bf16[8,64,1536]{2,1,0:T(8,128)(2,1)S(1)} %copy-done.2, bf16[1536,64]{1,0:T(8,128)(2,1)S(1)} %copy-done.10, bf16[64,1536]{1,0:T(8,128)(2,1)S(1)} %copy-done.21), custom_call_target="tpu_custom_call" | custom-call | flops 786432 | bytes 3145728 | tf_op jit(solution)/shard_map/pallas_call | solution.py:161
  267.3 7.3 shard_map.213
  275.0 5.4 collective-permute-done.6
  280.4 3.1 convert_add_fusion.7
  288.1 13.3 %shard_map.214 = (bf16[1536,2048]{1,0:T(8,128)(2,1)}, bf16[8,64,1536]{2,1,0:T(8,128)(2,1)}, bf16[64,1536]{1,0:T(8,128)(2,1)}, bf16[64,1536]{1,0:T(8,128)(2,1)}, ...) custom-call(s32[4]{0:T(128)} %pad_add_fusion.at_ref, bf16[384,2048]{1,0:T(8,128)(2,1)} %get-tuple-element.122.refs_0_, ...), custom_call_target="tpu_custom_call" | custom-call | flops 1000000 | bytes 1000000 | tf_op jit(solution)/shard_map/pallas_call | solution.py:549
  304.7 25.8 %shard_map.215 = (bf16[8,64,1536]{2,1,0:T(8,128)(2,1)S(1)}, f32[8,1,1536]{2,1,0:T(1,128)S(1)}) custom-call(s32[1]{0:T(128)} %get-tuple-element.318.len_ref, bf16[8,64,1536]{2,1,0:T(8,128)(2,1)S(1)} %copy-done, bf16[1536,64]{1,0:T(8,128)(2,1)S(1)} %copy-done.8, bf16[64,1536]{1,0:T(8,128)(2,1)S(1)} %copy-done.20), custom_call_target="tpu_custom_call" | custom-call | flops 786432 | bytes 3145728 | tf_op jit(solution)/shard_map/pallas_call | solution.py:161
  331.7 7.2 shard_map.216
  351.7 29.0 %collective-permute-done.11.refs_1_ = bf16[384,2048]{1,0:T(8,128)(2,1)} collective-permute-done((bf16[384,2048]{1,0:T(8,128)(2,1)S(1)}, bf16[384,2048]{1,0:T(8,128)(2,1)}, u32[]{:S(2)}, u32[]{:S(2)}) %collective-permute-start.11) | collective-permute-done | bytes 1572896 | tf_op jit(solution)/shard_map/ppermute | solution.py:29
  381.2 16.7 %shard_map.217 = (bf16[1536,1408]{1,0:T(8,128)(2,1)}, bf16[1536,2048]{1,0:T(8,128)(2,1)}) custom-call(bf16[384,2048]{1,0:T(8,128)(2,1)} %get-tuple-element.130.refs_0_, bf16[384,2048]{1,0:T(8,128)(2,1)} %collective-permute-done.5.refs_1_, bf16[384,2048]{1,0:T(8,128)(2,1)} %collective-permute-done.12.refs_2_, bf16[384,2048]{1,0:T(8,128)(2,1)} %copy-done.60, ...), custom_call_target="tpu_custom_call" | custom-call | flops 1000000 | bytes 1000000 | tf_op jit(solution)/shard_map/pallas_call | solution.py:402
  398.0 16.4 %collective-permute-done.20.refs_1_ = bf16[384,2048]{1,0:T(8,128)(2,1)} collective-permute-done((bf16[384,2048]{1,0:T(8,128)(2,1)}, bf16[384,2048]{1,0:T(8,128)(2,1)}, u32[]{:S(2)}, u32[]{:S(2)}) %collective-permute-start.20) | collective-permute-done | bytes 1572896 | tf_op jit(solution)/shard_map/ppermute | solution.py:29
  414.4 32.7 %collective-permute-done.16 = bf16[384,2048]{1,0:T(8,128)(2,1)S(1)} collective-permute-done((bf16[384,2048]{1,0:T(8,128)(2,1)S(1)}, bf16[384,2048]{1,0:T(8,128)(2,1)S(1)}, u32[]{:S(2)}, u32[]{:S(2)}) %collective-permute-start.16) | collective-permute-done | bytes 1572896 | tf_op jit(solution)/shard_map/ppermute | solution.py:29
  447.1 4.2 slice_add_fusion.4
  457.8 27.5 %shard_map.218 = (bf16[1536,1408]{1,0:T(8,128)(2,1)}, bf16[1536,2816]{1,0:T(8,128)(2,1)}, bf16[1536,2048]{1,0:T(8,128)(2,1)}) custom-call(bf16[384,2048]{1,0:T(8,128)(2,1)} %copy-done.44, bf16[384,2048]{1,0:T(8,128)(2,1)} %collective-permute-done.11.refs_1_, bf16[384,2048]{1,0:T(8,128)(2,1)} %collective-permute-done.14.refs_2_, ...), custom_call_target="tpu_custom_call" | custom-call | flops 4429185024 | bytes 12582912 | tf_op jit(solution)/shard_map/pallas_call | solution.py:433
  485.3 9.1 convolution_convert_fusion.1
  494.4 13.1 %fusion.12 = bf16[768,2048]{1,0:T(8,128)(2,1)} fusion(bf16[2048,2816]{1,0:T(8,128)(2,1)} %all-gather.8.cloned.1.call-done.refs_4_, bf16[1536,2816]{1,0:T(8,128)(2,1)S(1)} %copy-done.77), kind=kOutput, calls=%fused_computation.31 | convolution fusion | flops 8859942912 | bytes 19005440 | tf_op jit(solution)/shard_map/dot_general | solution.py:23
  508.0 16.8 %fusion.59 = f32[2048,1408]{1,0:T(8,128)} fusion(bf16[1536,2048]{1,0:T(8,128)(2,1)} %get-tuple-element.145, bf16[1536,1408]{1,0:T(8,128)(2,1)} %get-tuple-element.143), kind=kOutput, calls=%fused_computation.193 | convolution fusion | flops 8858370048 | bytes 22151168 | tf_op jit(solution)/shard_map/dot_general | solution.py:23
  525.3 10.4 convert_add_fusion.5
  535.8 13.1 %convert_add_fusion.4 = f32[768,2048]{1,0:T(8,128)} fusion(bf16[768,2048]{1,0:T(8,128)(2,1)} %collective-permute-done.19, bf16[2048,2816]{1,0:T(8,128)(2,1)S(1)} %bitcast.159, bf16[1536,2816]{1,0:T(8,128)(2,1)} %get-tuple-element.146), kind=kOutput, calls=%fused_computation.7 | convolution fusion | flops 8861515776 | bytes 25296896 | tf_op jit(solution)/shard_map/dot_general | solution.py:23
  551.5 17.1 %shard_map.219 = (bf16[1536,1408]{1,0:T(8,128)(2,1)}, bf16[1536,2048]{1,0:T(8,128)(2,1)}) custom-call(bf16[384,2048]{1,0:T(8,128)(2,1)} %get-tuple-element.149.refs_0_, bf16[384,2048]{1,0:T(8,128)(2,1)} %collective-permute-done.20.refs_1_, bf16[384,2048]{1,0:T(8,128)(2,1)} %collective-permute-done.21.refs_2_, ...), custom_call_target="tpu_custom_call" | custom-call | flops 1000000 | bytes 1000000 | tf_op jit(solution)/shard_map/pallas_call | solution.py:402
  568.6 27.3 %shard_map.220 = (bf16[1536,1408]{1,0:T(8,128)(2,1)}, bf16[1536,2816]{1,0:T(8,128)(2,1)}, bf16[1536,2048]{1,0:T(8,128)(2,1)}) custom-call(bf16[384,2048]{1,0:T(8,128)(2,1)} %multiply_convert_fusion.2.refs_0_, bf16[384,2048]{1,0:T(8,128)(2,1)} %collective-permute-done.18.refs_1_, bf16[384,2048]{1,0:T(8,128)(2,1)} %collective-permute-done.23.refs_2_, ...), custom_call_target="tpu_custom_call" | custom-call | flops 4429185024 | bytes 12582912 | tf_op jit(solution)/shard_map/pallas_call | solution.py:433
  598.9 15.8 %fusion.15 = bf16[768,2048]{1,0:T(8,128)(2,1)} fusion(bf16[2048,2816]{1,0:T(8,128)(2,1)} %all-gather.8.cloned.1.call-done.refs_4_, bf16[1536,2816]{1,0:T(8,128)(2,1)} %get-tuple-element.159), kind=kOutput, calls=%fused_computation.32 | convolution fusion | flops 8859942912 | bytes 19005440 | tf_op jit(solution)/shard_map/dot_general | solution.py:23
  616.9 4.7 fusion.54
  623.3 13.2 %convert_add_fusion.3 = f32[768,2048]{1,0:T(8,128)} fusion(bf16[768,2048]{1,0:T(8,128)(2,1)} %collective-permute-done.26, bf16[2048,2816]{1,0:T(8,128)(2,1)S(1)} %bitcast.161, bf16[1536,2816]{1,0:T(8,128)(2,1)} %get-tuple-element.159), kind=kOutput, calls=%fused_computation.6 | convolution fusion | flops 8861515776 | bytes 25296896 | tf_op jit(solution)/shard_map/dot_general | solution.py:23
  636.5 25.4 %fusion.60 = f32[2048,2816]{1,0:T(8,128)} fusion(bf16[1536,2048]{1,0:T(8,128)(2,1)} %get-tuple-element.162, bf16[1536,2816]{1,0:T(8,128)(2,1)} %get-tuple-element.146), kind=kOutput, calls=%fused_computation.194 | convolution fusion | flops 17716740096 | bytes 38010880 | tf_op jit(solution)/shard_map/dot_general | solution.py:23
  669.0 24.5 %add_convert_fusion = bf16[2048,2816]{1,0:T(8,128)(2,1)S(1)} fusion(f32[2048,2816]{1,0:T(8,128)} %fusion.60, bf16[1536,2048]{1,0:T(8,128)(2,1)} %get-tuple-element.166, bf16[1536,2816]{1,0:T(8,128)(2,1)} %get-tuple-element.159), kind=kOutput, calls=%fused_computation | convolution fusion | flops 17728274432 | bytes 49545216 | tf_op jit(solution)/shard_map/dot_general | solution.py:23
  693.6 7.7 collective-permute-done.27
  703.7 3.8 fusion.23
  710.5 17.1 %add_convert_fusion.1 = bf16[2048,1408]{1,0:T(8,128)(2,1)} fusion(f32[2048,1408]{1,0:T(8,128)} %fusion.59, bf16[1536,2048]{1,0:T(8,128)(2,1)} %get-tuple-element.171, bf16[1536,1408]{1,0:T(8,128)(2,1)} %get-tuple-element.172), kind=kOutput, calls=%fused_computation.2 | convolution fusion | flops 8864137216 | bytes 27918336 | tf_op jit(solution)/shard_map/dot_general | solution.py:23
  727.6 9.7 pad_maximum_fusion
  737.8 35.6 %collective-permute-done.31.refs_1_ = bf16[384,2048]{1,0:T(8,128)(2,1)} collective-permute-done((bf16[384,2048]{1,0:T(8,128)(2,1)}, bf16[384,2048]{1,0:T(8,128)(2,1)}, u32[]{:S(2)}, u32[]{:S(2)}) %collective-permute-start.31) | collective-permute-done | bytes 1572896 | tf_op jit(solution)/shard_map/ppermute | solution.py:29
  773.4 7.9 convolution_convert_fusion
  782.0 36.5 %collective-permute-done.32 = bf16[384,2048]{1,0:T(8,128)(2,1)S(1)} collective-permute-done((bf16[384,2048]{1,0:T(8,128)(2,1)S(1)}, bf16[384,2048]{1,0:T(8,128)(2,1)S(1)}, u32[]{:S(2)}, u32[]{:S(2)}) %collective-permute-start.32) | collective-permute-done | bytes 1572896 | tf_op jit(solution)/shard_map/ppermute | solution.py:29
  818.5 3.0 select_reduce_fusion.1
  821.5 8.9 convert_add_fusion.2
  830.5 15.1 %shard_map.221 = (bf16[8,64,1536]{2,1,0:T(8,128)(2,1)}, f32[8,1,1536]{2,1,0:T(1,128)}, f32[512,2048]{1,0:T(8,128)}) custom-call(s32[4]{0:T(128)} %pad_add_fusion.at_ref, bf16[384,2048]{1,0:T(8,128)(2,1)} %get-tuple-element.173.refs_0_, bf16[384,2048]{1,0:T(8,128)(2,1)} %collective-permute-done.28.refs_1_, bf16[384,2048]{1,0:T(8,128)(2,1)} %copy-done.58, ...), custom_call_target="tpu_custom_call" | custom-call | flops 1000000 | bytes 1000000 | tf_op jit(solution)/shard_map/pallas_call | solution.py:642
  846.4 34.6 %shard_map.222 = (bf16[8,64,1536]{2,1,0:T(8,128)(2,1)S(1)}, f32[1536,64]{1,0:T(8,128)S(1)}, f32[1536,64]{1,0:T(8,128)S(1)}) custom-call(s32[1]{0:T(128)} %get-tuple-element.317.len_ref, bf16[8,64,1536]{2,1,0:T(8,128)(2,1)S(1)} %copy-done.3, bf16[8,64,1536]{2,1,0:T(8,128)(2,1)} %get-tuple-element.174.grad_ref, bf16[1536,64]{1,0:T(8,128)(2,1)S(1)} %copy-done.11, ...), custom_call_target="tpu_custom_call" | custom-call | flops 786432 | bytes 4718592 | tf_op jit(solution)/shard_map/pallas_call | solution.py:232
  884.0 17.2 %shard_map.223 = (bf16[768,2048]{1,0:T(8,128)(2,1)}, bf16[768,2048]{1,0:T(8,128)(2,1)}, f32[640,2048]{1,0:T(8,128)}) custom-call(s32[4]{0:T(128)} %pad_add_fusion.at_ref, bf16[8,64,1536]{2,1,0:T(8,128)(2,1)} %copy-done.7, f32[1536,64]{1,0:T(8,128)} %copy-done.14, f32[1536,64]{1,0:T(8,128)} %copy-done.15, f32[32,1536]{1,0:T(8,128)} %get-tuple-element.306.refs_6_.refs_3_, ...), custom_call_target="tpu_custom_call" | custom-call | flops 1000000 | bytes 1000000 | tf_op jit(solution)/shard_map/pallas_call | solution.py:728
  901.9 3.7 slice.512
  906.1 4.8 collective-permute-done.35
  916.6 16.4 %shard_map.224 = (bf16[8,64,1536]{2,1,0:T(8,128)(2,1)}, f32[8,1,1536]{2,1,0:T(1,128)}, bf16[512,2048]{1,0:T(8,128)(2,1)}) custom-call(s32[4]{0:T(128)} %pad_add_fusion.at_ref, bf16[384,2048]{1,0:T(8,128)(2,1)} %get-tuple-element.188.refs_0_, bf16[384,2048]{1,0:T(8,128)(2,1)} %collective-permute-done.31.refs_1_, ...), custom_call_target="tpu_custom_call" | custom-call | flops 1000000 | bytes 1000000 | tf_op jit(solution)/shard_map/pallas_call | solution.py:642
  935.6 7.5 collective-permute-done.34
  943.1 5.6 select_reduce_fusion
  948.7 34.6 %shard_map.225 = (bf16[8,64,1536]{2,1,0:T(8,128)(2,1)S(1)}, f32[1536,64]{1,0:T(8,128)S(1)}, f32[1536,64]{1,0:T(8,128)S(1)}) custom-call(s32[1]{0:T(128)} %get-tuple-element.318.len_ref, bf16[8,64,1536]{2,1,0:T(8,128)(2,1)S(1)} %copy-done.1, bf16[8,64,1536]{2,1,0:T(8,128)(2,1)} %get-tuple-element.190.grad_ref, bf16[1536,64]{1,0:T(8,128)(2,1)S(1)} %copy-done.9, ...), custom_call_target="tpu_custom_call" | custom-call | flops 786432 | bytes 4718592 | tf_op jit(solution)/shard_map/pallas_call | solution.py:232
  983.3 4.7 slice_add_fusion.1
  988.1 18.0 %shard_map.226 = (bf16[768,2048]{1,0:T(8,128)(2,1)}, bf16[768,2048]{1,0:T(8,128)(2,1)}, bf16[8,640,256]{2,1,0:T(8,128)(2,1)}) custom-call(s32[4]{0:T(128)} %pad_add_fusion.at_ref, bf16[8,64,1536]{2,1,0:T(8,128)(2,1)} %copy-done.6, f32[1536,64]{1,0:T(8,128)} %copy-done.12, f32[1536,64]{1,0:T(8,128)} %copy-done.13, ...), custom_call_target="tpu_custom_call" | custom-call | flops 1000000 | bytes 1000000 | tf_op jit(solution)/shard_map/pallas_call | solution.py:728
  1012.2 4.3 convert_add_fusion
  1022.5 17.9 %collective-permute-done.42 = bf16[4,640,256]{2,1,0:T(8,128)(2,1)S(1)} collective-permute-done((bf16[4,640,256]{2,1,0:T(8,128)(2,1)S(1)}, bf16[4,640,256]{2,1,0:T(8,128)(2,1)S(1)}, u32[]{:S(2)}, u32[]{:S(2)}) %collective-permute-start.42) | collective-permute-done | bytes 1310752 | tf_op jit(solution)/shard_map/ppermute | solution.py:29
  1040.7 4.9 collective-permute-done.45
  1047.7 5.7 collective-permute-done.41
  1053.4 4.3 fusion.28
  1057.7 3.8 fusion.46
  1065.9 3.1 collective-permute-done.51
  1078.7 14.5 %collective-permute-done.46 = bf16[1,64,2048]{2,1,0:T(8,128)(2,1)} collective-permute-done((bf16[1,64,2048]{2,1,0:T(8,128)(2,1)S(1)}, bf16[1,64,2048]{2,1,0:T(8,128)(2,1)}, u32[]{:S(2)}, u32[]{:S(2)}) %collective-permute-start.46) | collective-permute-done | bytes 262176 | tf_op jit(solution)/shard_map/ppermute | solution.py:29
  1100.3 3.6 all-to-all-start.1
  (406 shorter events, 159.8 us)
Async XLA Ops:
  11.9 11.7 %all-to-all-start = ((bf16[4,64,768]{2,1,0:T(8,128)(2,1)}), bf16[4,64,768]{2,1,0:T(8,128)(2,1)S(1)}, u32[]{:S(2)}, u32[]{:S(2)}) async-start(bf16[4,64,768]{2,1,0:T(8,128)(2,1)} %pad_maximum_fusion.4), calls=%async_computation | async-start | bytes 786432 | tf_op jit(solution)/shard_map/all_to_all | solution.py:798
  16.1 111.7 %all-gather.4.cloned.1.call-start = ((), (), s32[]{:S(2)}) async-start(), calls=%async_computation.3 | async-start | bytes 5898240 | tf_op jit(solution)/shard_map/all_gather | solution.py:805
  16.1 0.7 collective-permute-start.4
  24.4 104.6 %copy-start.24 = (bf16[2,384,2048]{2,1,0:T(8,128)(2,1)S(1)}, bf16[2,384,2048]{2,1,0:T(8,128)(2,1)}, u32[]{:S(2)}) copy-start(bf16[2,384,2048]{2,1,0:T(8,128)(2,1)} %param.12) | copy-start | bytes 9437188
  24.4 242.8 %all-gather.6.cloned.1.call-start = ((), (), s32[]{:S(2)}) async-start(), calls=%async_computation.4 | async-start | bytes 6488064 | tf_op jit(solution)/shard_map/all_gather | solution.py:813
  26.9 424.4 %all-gather.8.cloned.1.call-start = ((), (), s32[]{:S(2)}) async-start(), calls=%async_computation.5 | async-start | bytes 12976128 | tf_op jit(solution)/shard_map/all_gather | solution.py:815
  127.8 941.8 %reduce-scatter.2.cloned.1.call-start = ((), (), s32[]{:S(2)}) async-start(), calls=%async_computation.6 | async-start | bytes 19464192 | tf_op jit(solution)/shard_map/reduce_scatter | solution.py:932
  131.4 35.6 %collective-permute-start = (bf16[384,2048]{1,0:T(8,128)(2,1)}, bf16[384,2048]{1,0:T(8,128)(2,1)}, u32[]{:S(2)}, u32[]{:S(2)}) collective-permute-start(bf16[384,2048]{1,0:T(8,128)(2,1)} %get-tuple-element.113.refs_0_), channel_id=1, source_target_pairs={{0,2},{1,3},{2,0},{3,1},{4,6},{5,7},{6,4},{7,5},{8,10},{9,11},{10,... | collective-permute-start | bytes 4718600 | tf_op jit(solution)/shard_map/ppermute | solution.py:29
  167.0 34.7 %collective-permute-start.1 = (bf16[384,2048]{1,0:T(8,128)(2,1)}, bf16[384,2048]{1,0:T(8,128)(2,1)}, u32[]{:S(2)}, u32[]{:S(2)}) collective-permute-start(bf16[384,2048]{1,0:T(8,128)(2,1)} %get-tuple-element.122.refs_0_), channel_id=1, source_target_pairs={{0,2},{1,3},{2,0},{3,1},{4,6},{5,7},{6,4},{7,5},{8,10},{9,11},{10,... | collective-permute-start | bytes 4718600 | tf_op jit(solution)/shard_map/ppermute | solution.py:29
  173.2 51.0 %collective-permute-start.2 = (bf16[384,2048]{1,0:T(8,128)(2,1)}, bf16[384,2048]{1,0:T(8,128)(2,1)}, u32[]{:S(2)}, u32[]{:S(2)}) collective-permute-start(bf16[384,2048]{1,0:T(8,128)(2,1)} %get-tuple-element.113.refs_0_), channel_id=1, source_target_pairs={{0,1},{1,0},{2,3},{3,2},{4,5},{5,4},{6,7},{7,6},{8,9},{9,8},{10,11... | collective-permute-start | bytes 4718600 | tf_op jit(solution)/shard_map/ppermute | solution.py:29
  173.2 51.0 %collective-permute-start.3 = (bf16[384,2048]{1,0:T(8,128)(2,1)}, bf16[384,2048]{1,0:T(8,128)(2,1)}, u32[]{:S(2)}, u32[]{:S(2)}) collective-permute-start(bf16[384,2048]{1,0:T(8,128)(2,1)} %collective-permute-done.refs_1_), channel_id=1, source_target_pairs={{0,1},{1,0},{2,3},{3,2},{4,5},{5,4},{6,7},{7,6},{8,9},{9,8},{10,11... | collective-permute-start | bytes 4718600 | tf_op jit(solution)/shard_map/ppermute | solution.py:29
  201.6 65.6 %collective-permute-start.5 = (bf16[384,2048]{1,0:T(8,128)(2,1)}, bf16[384,2048]{1,0:T(8,128)(2,1)}, u32[]{:S(2)}, u32[]{:S(2)}) collective-permute-start(bf16[384,2048]{1,0:T(8,128)(2,1)} %get-tuple-element.130.refs_0_), channel_id=1, source_target_pairs={{0,2},{1,3},{2,0},{3,1},{4,6},{5,7},{6,4},{7,5},{8,10},{9,11},{10,... | collective-permute-start | bytes 4718600 | tf_op jit(solution)/shard_map/ppermute | solution.py:29
  274.5 5.9 collective-permute-start.6
  274.5 12.4 %collective-permute-start.8 = (bf16[384,2048]{1,0:T(8,128)(2,1)}, bf16[384,2048]{1,0:T(8,128)(2,1)S(1)}, u32[]{:S(2)}, u32[]{:S(2)}) collective-permute-start(bf16[384,2048]{1,0:T(8,128)(2,1)} %get-tuple-element.122.refs_0_), channel_id=1, source_target_pairs={{0,1},{1,0},{2,3},{3,2},{4,5},{5,4},{6,7},{7,6},{8,9},{9,8},{10,11... | collective-permute-start | bytes 4718600 | tf_op jit(solution)/shard_map/ppermute | solution.py:29
  275.0 11.9 %collective-permute-start.9 = (bf16[384,2048]{1,0:T(8,128)(2,1)}, bf16[384,2048]{1,0:T(8,128)(2,1)}, u32[]{:S(2)}, u32[]{:S(2)}) collective-permute-start(bf16[384,2048]{1,0:T(8,128)(2,1)} %collective-permute-done.1.refs_1_), channel_id=1, source_target_pairs={{0,1},{1,0},{2,3},{3,2},{4,5},{5,4},{6,7},{7,6},{8,9},{9,8},{10,11... | collective-permute-start | bytes 4718600 | tf_op jit(solution)/shard_map/ppermute | solution.py:29
  286.3 53.1 %collective-permute-start.7 = (bf16[384,2048]{1,0:T(8,128)(2,1)S(1)}, bf16[384,2048]{1,0:T(8,128)(2,1)S(1)}, u32[]{:S(2)}, u32[]{:S(2)}) collective-permute-start(bf16[384,2048]{1,0:T(8,128)(2,1)S(1)} %slice.517), channel_id=1, source_target_pairs={{0,2},{1,3},{2,0},{3,1},{4,6},{5,7},{6,4},{7,5},{8,10},{9,11},{10,... | collective-permute-start | bytes 4718600 | tf_op jit(solution)/shard_map/ppermute | solution.py:29
  338.9 6.7 collective-permute-start.10
  339.0 12.1 %collective-permute-start.13 = (bf16[384,2048]{1,0:T(8,128)(2,1)}, bf16[384,2048]{1,0:T(8,128)(2,1)S(1)}, u32[]{:S(2)}, u32[]{:S(2)}) collective-permute-start(bf16[384,2048]{1,0:T(8,128)(2,1)} %collective-permute-done.5.refs_1_), channel_id=1, source_target_pairs={{0,1},{1,0},{2,3},{3,2},{4,5},{5,4},{6,7},{7,6},{8,9},{9,8},{10,11... | collective-permute-start | bytes 4718600 | tf_op jit(solution)/shard_map/ppermute | solution.py:29
  343.3 37.4 %collective-permute-start.11 = (bf16[384,2048]{1,0:T(8,128)(2,1)S(1)}, bf16[384,2048]{1,0:T(8,128)(2,1)}, u32[]{:S(2)}, u32[]{:S(2)}) collective-permute-start(bf16[384,2048]{1,0:T(8,128)(2,1)S(1)} %multiply_convert_fusion.3.refs_0_), channel_id=1, source_target_pairs={{0,2},{1,3},{2,0},{3,1},{4,6},{5,7},{6,4},{7,5},{8,10},{9,11},{10,... | collective-permute-start | bytes 4718600 | tf_op jit(solution)/shard_map/ppermute | solution.py:29
  345.0 35.7 %collective-permute-start.12 = (bf16[384,2048]{1,0:T(8,128)(2,1)}, bf16[384,2048]{1,0:T(8,128)(2,1)}, u32[]{:S(2)}, u32[]{:S(2)}) collective-permute-start(bf16[384,2048]{1,0:T(8,128)(2,1)} %get-tuple-element.130.refs_0_), channel_id=1, source_target_pairs={{0,1},{1,0},{2,3},{3,2},{4,5},{5,4},{6,7},{7,6},{8,9},{9,8},{10,11... | collective-permute-start | bytes 4718600 | tf_op jit(solution)/shard_map/ppermute | solution.py:29
  345.0 53.0 %collective-permute-start.14 = (bf16[384,2048]{1,0:T(8,128)(2,1)S(1)}, bf16[384,2048]{1,0:T(8,128)(2,1)}, u32[]{:S(2)}, u32[]{:S(2)}) collective-permute-start(bf16[384,2048]{1,0:T(8,128)(2,1)S(1)} %multiply_convert_fusion.3.refs_0_), channel_id=1, source_target_pairs={{0,1},{1,0},{2,3},{3,2},{4,5},{5,4},{6,7},{7,6},{8,9},{9,8},{10,11... | collective-permute-start | bytes 4718600 | tf_op jit(solution)/shard_map/ppermute | solution.py:29
  349.6 64.8 %collective-permute-start.20 = (bf16[384,2048]{1,0:T(8,128)(2,1)}, bf16[384,2048]{1,0:T(8,128)(2,1)}, u32[]{:S(2)}, u32[]{:S(2)}) collective-permute-start(bf16[384,2048]{1,0:T(8,128)(2,1)} %get-tuple-element.149.refs_0_), channel_id=1, source_target_pairs={{0,2},{1,3},{2,0},{3,1},{4,6},{5,7},{6,4},{7,5},{8,10},{9,11},{10,... | collective-permute-start | bytes 4718600 | tf_op jit(solution)/shard_map/ppermute | solution.py:29
  351.0 96.1 %collective-permute-start.16 = (bf16[384,2048]{1,0:T(8,128)(2,1)S(1)}, bf16[384,2048]{1,0:T(8,128)(2,1)S(1)}, u32[]{:S(2)}, u32[]{:S(2)}) collective-permute-start(bf16[384,2048]{1,0:T(8,128)(2,1)S(1)} %slice.516), channel_id=1, source_target_pairs={{0,2},{1,3},{2,0},{3,1},{4,6},{5,7},{6,4},{7,5},{8,10},{9,11},{10,... | collective-permute-start | bytes 4718600 | tf_op jit(solution)/shard_map/ppermute | solution.py:29
  380.7 70.7 %collective-permute-start.15 = (bf16[384,2048]{1,0:T(8,128)(2,1)}, bf16[384,2048]{1,0:T(8,128)(2,1)}, u32[]{:S(2)}, u32[]{:S(2)}) collective-permute-start(bf16[384,2048]{1,0:T(8,128)(2,1)} %collective-permute-done.11.refs_1_), channel_id=1, source_target_pairs={{0,1},{1,0},{2,3},{3,2},{4,5},{5,4},{6,7},{7,6},{8,9},{9,8},{10,11... | collective-permute-start | bytes 4718600 | tf_op jit(solution)/shard_map/ppermute | solution.py:29
  380.7 170.8 %collective-permute-start.21 = (bf16[384,2048]{1,0:T(8,128)(2,1)}, bf16[384,2048]{1,0:T(8,128)(2,1)}, u32[]{:S(2)}, u32[]{:S(2)}) collective-permute-start(bf16[384,2048]{1,0:T(8,128)(2,1)} %get-tuple-element.149.refs_0_), channel_id=1, source_target_pairs={{0,1},{1,0},{2,3},{3,2},{4,5},{5,4},{6,7},{7,6},{8,9},{9,8},{10,11... | collective-permute-start | bytes 4718600 | tf_op jit(solution)/shard_map/ppermute | solution.py:29
  414.4 137.1 %collective-permute-start.22 = (bf16[384,2048]{1,0:T(8,128)(2,1)}, bf16[384,2048]{1,0:T(8,128)(2,1)}, u32[]{:S(2)}, u32[]{:S(2)}) collective-permute-start(bf16[384,2048]{1,0:T(8,128)(2,1)} %collective-permute-done.20.refs_1_), channel_id=1, source_target_pairs={{0,1},{1,0},{2,3},{3,2},{4,5},{5,4},{6,7},{7,6},{8,9},{9,8},{10,11... | collective-permute-start | bytes 4718600 | tf_op jit(solution)/shard_map/ppermute | solution.py:29
  456.2 68.6 %collective-permute-start.18 = (bf16[384,2048]{1,0:T(8,128)(2,1)}, bf16[384,2048]{1,0:T(8,128)(2,1)}, u32[]{:S(2)}, u32[]{:S(2)}) collective-permute-start(bf16[384,2048]{1,0:T(8,128)(2,1)} %multiply_convert_fusion.2.refs_0_), channel_id=1, source_target_pairs={{0,2},{1,3},{2,0},{3,1},{4,6},{5,7},{6,4},{7,5},{8,10},{9,11},{10,... | collective-permute-start | bytes 4718600 | tf_op jit(solution)/shard_map/ppermute | solution.py:29
  494.4 30.4 %collective-permute-start.17 = (bf16[768,2048]{1,0:T(8,128)(2,1)}, bf16[768,2048]{1,0:T(8,128)(2,1)}, u32[]{:S(2)}, u32[]{:S(2)}) collective-permute-start(bf16[768,2048]{1,0:T(8,128)(2,1)} %convolution_convert_fusion.1), channel_id=1, source_target_pairs={{0,1},{1,0},{2,3},{3,2},{4,5},{5,4},{6,7},{7,6},{8,9},{9,8},{10,11... | collective-permute-start | bytes 9437192 | tf_op jit(solution)/shard_map/ppermute | solution.py:29
  507.5 28.2 %collective-permute-start.19 = (bf16[768,2048]{1,0:T(8,128)(2,1)}, bf16[768,2048]{1,0:T(8,128)(2,1)}, u32[]{:S(2)}, u32[]{:S(2)}) collective-permute-start(bf16[768,2048]{1,0:T(8,128)(2,1)} %fusion.12), channel_id=1, source_target_pairs={{0,1},{1,0},{2,3},{3,2},{4,5},{5,4},{6,7},{7,6},{8,9},{9,8},{10,11... | collective-permute-start | bytes 9437192 | tf_op jit(solution)/shard_map/ppermute | solution.py:29
  524.8 43.8 %collective-permute-start.23 = (bf16[384,2048]{1,0:T(8,128)(2,1)}, bf16[384,2048]{1,0:T(8,128)(2,1)}, u32[]{:S(2)}, u32[]{:S(2)}) collective-permute-start(bf16[384,2048]{1,0:T(8,128)(2,1)} %multiply_convert_fusion.2.refs_0_), channel_id=1, source_target_pairs={{0,1},{1,0},{2,3},{3,2},{4,5},{5,4},{6,7},{7,6},{8,9},{9,8},{10,11... | collective-permute-start | bytes 4718600 | tf_op jit(solution)/shard_map/ppermute | solution.py:29
  524.8 43.8 %collective-permute-start.24 = (bf16[384,2048]{1,0:T(8,128)(2,1)}, bf16[384,2048]{1,0:T(8,128)(2,1)}, u32[]{:S(2)}, u32[]{:S(2)}) collective-permute-start(bf16[384,2048]{1,0:T(8,128)(2,1)} %collective-permute-done.18.refs_1_), channel_id=1, source_target_pairs={{0,1},{1,0},{2,3},{3,2},{4,5},{5,4},{6,7},{7,6},{8,9},{9,8},{10,11... | collective-permute-start | bytes 4718600 | tf_op jit(solution)/shard_map/ppermute | solution.py:29
  551.0 45.0 %collective-permute-start.25 = (bf16[384,2048]{1,0:T(8,128)(2,1)S(1)}, bf16[384,2048]{1,0:T(8,128)(2,1)}, u32[]{:S(2)}, u32[]{:S(2)}) collective-permute-start(bf16[384,2048]{1,0:T(8,128)(2,1)S(1)} %slice.515), channel_id=1, source_target_pairs={{0,2},{1,3},{2,0},{3,1},{4,6},{5,7},{6,4},{7,5},{8,10},{9,11},{10,... | collective-permute-start | bytes 4718600 | tf_op jit(solution)/shard_map/ppermute | solution.py:29
  614.7 8.5 collective-permute-start.26
  621.7 40.3 %collective-permute-start.28 = (bf16[384,2048]{1,0:T(8,128)(2,1)}, bf16[384,2048]{1,0:T(8,128)(2,1)}, u32[]{:S(2)}, u32[]{:S(2)}) collective-permute-start(bf16[384,2048]{1,0:T(8,128)(2,1)} %get-tuple-element.173.refs_0_), channel_id=1, source_target_pairs={{0,2},{1,3},{2,0},{3,1},{4,6},{5,7},{6,4},{7,5},{8,10},{9,11},{10,... | collective-permute-start | bytes 4718600 | tf_op jit(solution)/shard_map/ppermute | solution.py:29
  662.0 3.7 collective-permute-start.29
  662.3 5.6 collective-permute-start.30
  664.7 36.6 %collective-permute-start.27 = (bf16[384,2048]{1,0:T(8,128)(2,1)S(1)}, bf16[384,2048]{1,0:T(8,128)(2,1)S(1)}, u32[]{:S(2)}, u32[]{:S(2)}) collective-permute-start(bf16[384,2048]{1,0:T(8,128)(2,1)S(1)} %slice.514), channel_id=1, source_target_pairs={{0,2},{1,3},{2,0},{3,1},{4,6},{5,7},{6,4},{7,5},{8,10},{9,11},{10,... | collective-permute-start | bytes 4718600 | tf_op jit(solution)/shard_map/ppermute | solution.py:29
  737.3 44.1 %slice-start.8 = ((s8[6291456]{0:T(1024)(128)(4,1)}), s8[4194304]{0:T(1024)(128)(4,1)S(1)}, s32[]{:S(2)}) async-start(s8[6291456]{0:T(1024)(128)(4,1)} %bitcast.168), calls=%async_computation.15 | async-start | bytes 8388608
  737.3 44.1 %slice-start.9 = ((s8[6291456]{0:T(1024)(128)(4,1)}), s8[2097152]{0:T(1024)(128)(4,1)S(1)}, s32[]{:S(2)}) async-start(s8[6291456]{0:T(1024)(128)(4,1)} %bitcast.168), calls=%async_computation.16 | async-start | bytes 4194304
  737.3 36.1 %collective-permute-start.31 = (bf16[384,2048]{1,0:T(8,128)(2,1)}, bf16[384,2048]{1,0:T(8,128)(2,1)}, u32[]{:S(2)}, u32[]{:S(2)}) collective-permute-start(bf16[384,2048]{1,0:T(8,128)(2,1)} %get-tuple-element.188.refs_0_), channel_id=1, source_target_pairs={{0,2},{1,3},{2,0},{3,1},{4,6},{5,7},{6,4},{7,5},{8,10},{9,11},{10,... | collective-permute-start | bytes 4718600 | tf_op jit(solution)/shard_map/ppermute | solution.py:29
  781.3 40.2 %collective-permute-start.33 = (bf16[768,2048]{1,0:T(8,128)(2,1)S(1)}, bf16[768,2048]{1,0:T(8,128)(2,1)S(1)}, u32[]{:S(2)}, u32[]{:S(2)}) collective-permute-start(bf16[768,2048]{1,0:T(8,128)(2,1)S(1)} %convolution_convert_fusion), channel_id=1, source_target_pairs={{0,1},{1,0},{2,3},{3,2},{4,5},{5,4},{6,7},{7,6},{8,9},{9,8},{10,11... | collective-permute-start | bytes 9437192 | tf_op jit(solution)/shard_map/ppermute | solution.py:29
  781.4 40.1 %slice-start.6 = ((s8[5767168]{0:T(1024)(128)(4,1)}), s8[4194304]{0:T(1024)(128)(4,1)S(1)}, s32[]{:S(2)}) async-start(s8[5767168]{0:T(1024)(128)(4,1)} %bitcast.162), calls=%async_computation.13 | async-start | bytes 8388608
  781.7 39.8 %slice-start.7 = ((s8[5767168]{0:T(1024)(128)(4,1)}), s8[1572864]{0:T(1024)(128)(4,1)S(1)}, s32[]{:S(2)}) async-start(s8[5767168]{0:T(1024)(128)(4,1)} %bitcast.162), calls=%async_computation.14 | async-start | bytes 3145728
  781.7 36.8 %collective-permute-start.32 = (bf16[384,2048]{1,0:T(8,128)(2,1)S(1)}, bf16[384,2048]{1,0:T(8,128)(2,1)S(1)}, u32[]{:S(2)}, u32[]{:S(2)}) collective-permute-start(bf16[384,2048]{1,0:T(8,128)(2,1)S(1)} %slice.513), channel_id=1, source_target_pairs={{0,2},{1,3},{2,0},{3,1},{4,6},{5,7},{6,4},{7,5},{8,10},{9,11},{10,... | collective-permute-start | bytes 4718600 | tf_op jit(solution)/shard_map/ppermute | solution.py:29
  901.2 9.6 collective-permute-start.35
  901.3 15.3 %collective-permute-start.37 = (bf16[384,2048]{1,0:T(8,128)(2,1)}, bf16[384,2048]{1,0:T(8,128)(2,1)}, u32[]{:S(2)}, u32[]{:S(2)}) collective-permute-start(bf16[384,2048]{1,0:T(8,128)(2,1)} %get-tuple-element.188.refs_0_), channel_id=1, source_target_pairs={{0,1},{1,0},{2,3},{3,2},{4,5},{5,4},{6,7},{7,6},{8,9},{9,8},{10,11... | collective-permute-start | bytes 4718600 | tf_op jit(solution)/shard_map/ppermute | solution.py:29
  901.8 14.8 %collective-permute-start.38 = (bf16[384,2048]{1,0:T(8,128)(2,1)}, bf16[384,2048]{1,0:T(8,128)(2,1)}, u32[]{:S(2)}, u32[]{:S(2)}) collective-permute-start(bf16[384,2048]{1,0:T(8,128)(2,1)} %collective-permute-done.31.refs_1_), channel_id=1, source_target_pairs={{0,1},{1,0},{2,3},{3,2},{4,5},{5,4},{6,7},{7,6},{8,9},{9,8},{10,11... | collective-permute-start | bytes 4718600 | tf_op jit(solution)/shard_map/ppermute | solution.py:29
  905.5 37.6 %collective-permute-start.34 = (bf16[384,2048]{1,0:T(8,128)(2,1)}, bf16[384,2048]{1,0:T(8,128)(2,1)}, u32[]{:S(2)}, u32[]{:S(2)}) collective-permute-start(bf16[384,2048]{1,0:T(8,128)(2,1)} %slice.512), channel_id=1, source_target_pairs={{0,2},{1,3},{2,0},{3,1},{4,6},{5,7},{6,4},{7,5},{8,10},{9,11},{10,... | collective-permute-start | bytes 4718600 | tf_op jit(solution)/shard_map/ppermute | solution.py:29
  916.2 67.1 %collective-permute-start.36 = (bf16[384,2048]{1,0:T(8,128)(2,1)}, bf16[384,2048]{1,0:T(8,128)(2,1)}, u32[]{:S(2)}, u32[]{:S(2)}) collective-permute-start(bf16[384,2048]{1,0:T(8,128)(2,1)} %slice.511), channel_id=1, source_target_pairs={{0,2},{1,3},{2,0},{3,1},{4,6},{5,7},{6,4},{7,5},{8,10},{9,11},{10,... | collective-permute-start | bytes 4718600 | tf_op jit(solution)/shard_map/ppermute | solution.py:29
  934.5 53.6 %collective-permute-start.39 = (bf16[4,64,2048]{2,1,0:T(8,128)(2,1)S(1)}, bf16[4,64,2048]{2,1,0:T(8,128)(2,1)}, u32[]{:S(2)}, u32[]{:S(2)}) collective-permute-start(bf16[4,64,2048]{2,1,0:T(8,128)(2,1)S(1)} %dynamic-slice_bitcast_fusion.1), channel_id=1, source_target_pairs={{0,4},{4,0},{8,12},{12,8},{16,20},{20,16},{24,28},{28,24},{1,5},{5... | collective-permute-start | bytes 3145736 | tf_op jit(solution)/shard_map/ppermute | solution.py:29
  943.1 40.2 %copy-start.36 = (f32[768,2048]{1,0:T(8,128)S(1)}, f32[768,2048]{1,0:T(8,128)}, u32[]{:S(2)}) copy-start(f32[768,2048]{1,0:T(8,128)} %copy-done.35) | copy-start | bytes 18874372
  1006.1 6.1 collective-permute-start.40
  1009.2 31.2 %collective-permute-start.42 = (bf16[4,640,256]{2,1,0:T(8,128)(2,1)S(1)}, bf16[4,640,256]{2,1,0:T(8,128)(2,1)S(1)}, u32[]{:S(2)}, u32[]{:S(2)}) collective-permute-start(bf16[4,640,256]{2,1,0:T(8,128)(2,1)S(1)} %dynamic-slice_bitcast_fusion), channel_id=1, source_target_pairs={{0,4},{4,0},{8,12},{12,8},{16,20},{20,16},{24,28},{28,24},{1,5},{5... | collective-permute-start | bytes 3932168 | tf_op jit(solution)/shard_map/ppermute | solution.py:29
  1016.7 36.7 %collective-permute-start.41 = (bf16[384,2048]{1,0:T(8,128)(2,1)S(1)}, bf16[384,2048]{1,0:T(8,128)(2,1)}, u32[]{:S(2)}, u32[]{:S(2)}) collective-permute-start(bf16[384,2048]{1,0:T(8,128)(2,1)S(1)} %slice.510), channel_id=1, source_target_pairs={{0,2},{1,3},{2,0},{3,1},{4,6},{5,7},{6,4},{7,5},{8,10},{9,11},{10,... | collective-permute-start | bytes 4718600 | tf_op jit(solution)/shard_map/ppermute | solution.py:29
  1019.2 26.4 %collective-permute-start.45 = (bf16[2,64,2048]{2,1,0:T(8,128)(2,1)S(1)}, bf16[2,64,2048]{2,1,0:T(8,128)(2,1)S(1)}, u32[]{:S(2)}, u32[]{:S(2)}) collective-permute-start(bf16[2,64,2048]{2,1,0:T(8,128)(2,1)S(1)} %dynamic-slice_bitcast_fusion.3), channel_id=1, source_target_pairs={{0,8},{4,12},{8,0},{12,4},{16,24},{20,28},{24,16},{28,20},{1,9},{5... | collective-permute-start | bytes 1572872 | tf_op jit(solution)/shard_map/ppermute | solution.py:29
  1046.5 23.1 %collective-permute-start.43 = (bf16[2,640,256]{2,1,0:T(8,128)(2,1)}, bf16[2,640,256]{2,1,0:T(8,128)(2,1)}, u32[]{:S(2)}, u32[]{:S(2)}) collective-permute-start(bf16[2,640,256]{2,1,0:T(8,128)(2,1)} %dynamic-slice_bitcast_fusion.2), channel_id=1, source_target_pairs={{0,8},{4,12},{8,0},{12,4},{16,24},{20,28},{24,16},{28,20},{1,9},{5... | collective-permute-start | bytes 1966088 | tf_op jit(solution)/shard_map/ppermute | solution.py:29
  1057.7 7.7 collective-permute-start.50
  1065.4 3.6 collective-permute-start.51
  1071.1 22.2 %collective-permute-start.46 = (bf16[1,64,2048]{2,1,0:T(8,128)(2,1)S(1)}, bf16[1,64,2048]{2,1,0:T(8,128)(2,1)}, u32[]{:S(2)}, u32[]{:S(2)}) collective-permute-start(bf16[1,64,2048]{2,1,0:T(8,128)(2,1)S(1)} %constant_dynamic-slice_fusion.4), channel_id=1, source_target_pairs={{0,16},{4,20},{8,24},{12,28},{16,0},{20,4},{24,8},{28,12},{1,17},{... | collective-permute-start | bytes 786440 | tf_op jit(solution)/shard_map/ppermute | solution.py:29
  1077.0 1.2 collective-permute-start.48
  1077.0 22.2 %collective-permute-start.44 = (bf16[1,640,256]{2,1,0:T(8,128)(2,1)S(1)}, bf16[1,640,256]{2,1,0:T(8,128)(2,1)S(1)}, u32[]{:S(2)}, u32[]{:S(2)}) collective-permute-start(bf16[1,640,256]{2,1,0:T(8,128)(2,1)S(1)} %constant_dynamic-slice_fusion.5), channel_id=1, source_target_pairs={{0,16},{4,20},{8,24},{12,28},{16,0},{20,4},{24,8},{28,12},{1,17},{... | collective-permute-start | bytes 983048 | tf_op jit(solution)/shard_map/ppermute | solution.py:29
  1078.1 28.7 %collective-permute-start.49 = (f32[1,64]{1,0:T(1,128)S(1)}, f32[1,64]{1,0:T(1,128)S(1)}, u32[]{:S(2)}, u32[]{:S(2)}) collective-permute-start(f32[1,64]{1,0:T(1,128)S(1)} %constant_dynamic-slice_fusion), channel_id=1, source_target_pairs={{0,2},{1,3},{2,0},{3,1},{4,6},{5,7},{6,4},{7,5},{8,10},{9,11},{10,... | collective-permute-start | bytes 776 | tf_op jit(solution)/shard_map/ppermute | solution.py:29
  1095.0 12.4 %collective-permute-start.47 = (bf16[64,2048]{1,0:T(8,128)(2,1)}, bf16[64,2048]{1,0:T(8,128)(2,1)S(1)}, u32[]{:S(2)}, u32[]{:S(2)}) collective-permute-start(bf16[64,2048]{1,0:T(8,128)(2,1)} %fusion.49), channel_id=1, source_target_pairs={{0,0},{4,1},{8,2},{12,3},{16,4},{20,5},{24,6},{28,7},{1,8},{5,9},{... | collective-permute-start | bytes 786440 | tf_op jit(solution)/shard_map/ppermute | solution.py:989
  1100.3 10.3 all-to-all-start.1
  (84 other events, 768.6 us)
Sparse Core Ops, SparseCore 0:
  24.6 103.1 all-gather.3
  130.5 90.8 all-gather.5
  224.2 161.8 all-gather.7
  737.4 308.3 reduce-scatter.1
